TPU v7x, 32 devices: a whole 2x2x4 slice. The times are simulated.
32 devices in a mesh: tm: 8 (over z, y), row: 4 (over x, core).
Axes of the slice: x: 2, y: 2, z: 4, core: 2. Of those that a mesh axis runs over, the one named last changes fastest.
Arguments:
- latents: bfloat16 [16, 24, 80, 256], P('tm', 'row'), may hold values from -6 to 6
- conv_weight: bfloat16 [3, 3, 768, 256], replicated, may hold values from -0.078125 to 0.078125
- norm_gain: float32 [256], replicated, may hold values from 0.1 to 1.9
- depth_target: bfloat16 [16, 24, 80, 128], P('tm', 'row'), may hold values from -6 to 6
Outputs:
- features: bfloat16 [16, 24, 80, 256], P('tm', 'row')
- gram: float32 [256, 256], replicated
- cross: float32 [256, 128], replicated
All inputs are finite; a program needn't handle non-finite values.
Results may differ from a plain program's by a relative error of at most 0.003.
Values may be sent and summed in bfloat16 or wider, within the bound.
No kernel may reach another device: no remote copies, remote signals or barrier semaphores. Data moves between devices by JAX's collectives and lax.ppermute only.
A program may use at most 64 MiB of HBM per device.

v0:
```python
import jax
import jax.numpy as jnp
from jax import lax
from jax.sharding import PartitionSpec as P


def from_behind(value, axis, steps):
    count = lax.axis_size(axis)
    first, last = (max(0, -steps), min(count, count - steps))
    return lax.ppermute(value, axis, [(source, source + steps) for source in range(first, last)])


def extended(cells, sides, width):
    for axis, dim in sides:
        count = lax.axis_size(axis)
        ends = count - 1
        head = lax.slice_in_dim(cells, 0, width, axis=dim)
        tail = lax.slice_in_dim(cells, cells.shape[dim] - width, cells.shape[dim], axis=dim)
        cells = jnp.concatenate(
            [
                lax.ppermute(tail, axis, [(i, (i + 1) % count) for i in range(ends)]),
                cells,
                lax.ppermute(head, axis, [((i + 1) % count, i) for i in range(ends)]),
            ],
            axis=dim,
        )
    return cells


def convolve(padded, conv_weight):
    frames = padded.shape[0] - 2
    rows = padded.shape[1] - 2
    cols = padded.shape[2]
    chans = conv_weight.shape[3]
    wide = jnp.pad(padded, ((0, 0), (0, 0), (1, 1), (0, 0)))
    stacked = jnp.concatenate(
        [wide[:, :, 0:cols], wide[:, :, 1 : cols + 1], wide[:, :, 2 : cols + 2]], axis=3
    )
    total = jnp.zeros((frames * rows * cols, chans), jnp.float32)
    for dtime in range(3):
        for drow in range(3):
            piece = stacked[dtime : dtime + frames, drow : drow + rows].reshape(
                frames * rows * cols, -1
            )
            total = total + jnp.dot(
                piece, conv_weight[dtime, drow], preferred_element_type=jnp.float32
            )
    return total


def on_device(latents, conv_weight, norm_gain, depth_target):
    cached = from_behind(latents, "tm", 1)
    joined = jnp.concatenate([cached, latents], axis=0)
    padded = extended(joined, (("row", 1),), 1)
    conv = convolve(padded, conv_weight)
    flat_in = latents.reshape(conv.shape[0], conv.shape[1]).astype(jnp.float32)
    normed = conv * jax.lax.rsqrt(jnp.mean(conv * conv, axis=1, keepdims=True) + 1e-06) * norm_gain
    flat = (flat_in + jax.nn.silu(normed)).astype(jnp.bfloat16)
    targets = depth_target.reshape(flat.shape[0], -1)
    gram_part = jnp.dot(flat.T, flat, preferred_element_type=jnp.float32)
    cross_part = jnp.dot(flat.T, targets, preferred_element_type=jnp.float32)
    count = flat.shape[0] * lax.axis_size("tm") * lax.axis_size("row")
    gram_sum, cross_sum = lax.psum((gram_part, cross_part), ("tm", "row"))
    return (flat.reshape(latents.shape), gram_sum / count, cross_sum / count)


def solution(mesh):
    in_specs = (P("tm", "row", None, None), P(), P(), P("tm", "row", None, None))
    out_specs = (P("tm", "row", None, None), P(), P())
    return jax.shard_map(
        on_device, mesh=mesh, in_specs=in_specs, out_specs=out_specs, check_vma=False
    )
```

profile of v0, /device:TPU:0, one launch (start us, length us, event | category | flops | bytes accessed | tf_op | source)
XLA Modules:
  0.0 185.2 jit_solution(1242855013756441076)
XLA Ops:
  7.2 0.0 copy-start
  7.2 0.0 all-reduce.4.cloned.1.call-start
  7.2 5.0 %collective-permute-start = (bf16[2,6,80,256]{3,2,1,0:T(8,128)(2,1)}, bf16[2,6,80,256]{3,2,1,0:T(8,128)(2,1)S(1)}, u32[]{:S(2)}, u32[]{:S(2)}) collective-permute-start(bf16[2,6,80,256]{3,2,1,0:T(8,128)(2,1)} %param.4), channel_id=1, source_target_pairs={{0,4},{4,8},{8,12},{12,16},{16,20},{20,24},{24,28},{1,5},{5,9},{9,... | collective-permute-start | bytes 1474568 | tf_op jit(solution)/shard_map/ppermute | solution.py:10
  12.3 10.7 %collective-permute-done = bf16[2,6,80,256]{3,2,1,0:T(8,128)(2,1)S(1)} collective-permute-done((bf16[2,6,80,256]{3,2,1,0:T(8,128)(2,1)}, bf16[2,6,80,256]{3,2,1,0:T(8,128)(2,1)S(1)}, u32[]{:S(2)}, u32[]{:S(2)}) %collective-permute-start) | collective-permute-done | bytes 491552 | tf_op jit(solution)/shard_map/ppermute | solution.py:10
  23.1 1.1 constant_dynamic-update-slice_fusion
  24.2 1.3 collective-permute-start.1
  25.5 1.3 collective-permute-start.2
  26.8 0.0 collective-permute-done.1
  26.8 3.7 %collective-permute-done.2 = bf16[4,1,80,256]{3,2,1,0:T(8,128)(2,1)S(1)} collective-permute-done((bf16[4,1,80,256]{3,2,1,0:T(8,128)(2,1)S(1)}, bf16[4,1,80,256]{3,2,1,0:T(8,128)(2,1)S(1)}, u32[]{:S(2)}, u32[]{:S(2)}) %collective-permute-start.2) | collective-permute-done | bytes 163872 | tf_op jit(solution)/shard_map/ppermute | solution.py:23
  30.5 0.8 fusion.5
  31.2 0.9 fusion.41
  32.1 0.3 pad_maximum_fusion
  32.5 0.0 copy-start.1
  32.5 1.2 fusion.40
  33.7 0.7 copy-done.1
  34.5 0.5 fusion.14
  35.0 0.5 fusion.16
  35.6 0.5 fusion.18
  36.1 0.5 fusion.20
  36.7 0.6 fusion.22
  37.2 0.5 fusion.24
  37.8 0.5 fusion.26
  38.4 0.5 fusion.28
  38.9 0.0 copy-start.2
  38.9 0.0 copy-start.4
  38.9 0.9 multiply_reduce_fusion
  39.9 0.1 copy-done.2
  40.0 0.0 copy-done.4
  40.0 0.4 fusion.13
  40.4 0.0 copy-start.3
  40.4 1.0 fusion.43
  41.4 0.0 copy-done
  41.4 1.0 fusion.44
  42.4 0.0 all-reduce.4.cloned.1.call-update
  42.4 132.7 %all-reduce.4.cloned.1.call-done = (f32[256,256]{1,0:T(8,128)}, f32[256,128]{1,0:T(8,128)}) async-done(((f32[256,256]{1,0:T(8,128)}, f32[256,128]{1,0:T(8,128)}), (f32[256,256]{1,0:T(8,128)}, f32[256,128]{1,0:T(8,128)})) %all-reduce.4.cloned.1.call-update) | async-done | bytes 393232 | tf_op jit(solution)/shard_map/psum | solution.py:63
  175.2 1.7 broadcast_multiply_fusion
  176.8 0.0 copy-done.3
  176.8 1.6 broadcast_multiply_fusion.1
  (3 shorter events, 0.1 us)
Async XLA Ops:
  7.2 34.3 %copy-start = (bf16[2,6,80,128]{3,2,1,0:T(8,128)(2,1)S(1)}, bf16[2,6,80,128]{3,2,1,0:T(8,128)(2,1)}, u32[]{:S(2)}) copy-start(bf16[2,6,80,128]{3,2,1,0:T(8,128)(2,1)} %param.7) | copy-start | bytes 737284
  7.2 168.0 %all-reduce.4.cloned.1.call-start = ((), (), s32[]{:S(2)}) async-start(), calls=%async_computation | async-start | bytes 786432 | tf_op jit(solution)/shard_map/psum | solution.py:63
  7.2 15.8 %collective-permute-start = (bf16[2,6,80,256]{3,2,1,0:T(8,128)(2,1)}, bf16[2,6,80,256]{3,2,1,0:T(8,128)(2,1)S(1)}, u32[]{:S(2)}, u32[]{:S(2)}) collective-permute-start(bf16[2,6,80,256]{3,2,1,0:T(8,128)(2,1)} %param.4), channel_id=1, source_target_pairs={{0,4},{4,8},{8,12},{12,16},{16,20},{20,24},{24,28},{1,5},{5,9},{9,... | collective-permute-start | bytes 1474568 | tf_op jit(solution)/shard_map/ppermute | solution.py:10
  24.2 2.6 %collective-permute-start.1 = (bf16[4,1,80,256]{3,2,1,0:T(8,128)(2,1)S(1)}, bf16[4,1,80,256]{3,2,1,0:T(8,128)(2,1)S(1)}, u32[]{:S(2)}, u32[]{:S(2)}) collective-permute-start(bf16[4,1,80,256]{3,2,1,0:T(8,128)(2,1)S(1)} %get-tuple-element.16), channel_id=1, source_target_pairs={{0,1},{1,2},{2,3},{4,5},{5,6},{6,7},{8,9},{9,10},{10,11},{12,13},{... | collective-permute-start | bytes 491528 | tf_op jit(solution)/shard_map/ppermute | solution.py:21
  25.5 5.0 %collective-permute-start.2 = (bf16[4,1,80,256]{3,2,1,0:T(8,128)(2,1)S(1)}, bf16[4,1,80,256]{3,2,1,0:T(8,128)(2,1)S(1)}, u32[]{:S(2)}, u32[]{:S(2)}) collective-permute-start(bf16[4,1,80,256]{3,2,1,0:T(8,128)(2,1)S(1)} %get-tuple-element.17), channel_id=1, source_target_pairs={{1,0},{2,1},{3,2},{5,4},{6,5},{7,6},{9,8},{10,9},{11,10},{13,12},{... | collective-permute-start | bytes 491528 | tf_op jit(solution)/shard_map/ppermute | solution.py:23
  32.5 2.0 %copy-start.1 = (bf16[3,3,768,256]{3,2,1,0:T(8,128)(2,1)S(1)}, bf16[3,3,768,256]{3,2,1,0:T(8,128)(2,1)}, u32[]{:S(2)}) copy-start(bf16[3,3,768,256]{3,2,1,0:T(8,128)(2,1)} %param.5) | copy-start | bytes 10616836
  38.9 1.0 copy-start.2
  38.9 1.0 copy-start.4
  40.4 136.5 %copy-start.3 = (bf16[960,256]{1,0:T(8,128)(2,1)}, bf16[960,256]{1,0:T(8,128)(2,1)S(1)}, u32[]{:S(2)}) copy-start(bf16[960,256]{1,0:T(8,128)(2,1)S(1)} %fusion.13) | copy-start | bytes 1474564
Sparse Core Ops, SparseCore 0:
  42.6 132.5 all-reduce.3
where the time goes:
time: 186 us; the launch traced here: 185 us
  waiting for transfers between devices  147 us (79%)
  between operations  14.2 us (8%)
  starting transfers between devices  7.66 us (4%)
  matrix products  7.34 us (4%)
  other arithmetic  4.74 us (3%)
  local copies, waits for them, and re-layouts  4.12 us (2%)
    psum x1, waiting for transfers between devices, on_device(): gram_sum, cross_sum = lax.psum((gram_part, cross_part), ('tm', 'row'))  133 us
    ppermute x1, waiting for transfers between devices, from_behind(): lax.ppermute(value, axis, [(source, source + steps) for source in range(f...  10.7 us
    dot_general x9, matrix products, convolve(): jnp.dot(piece, conv_weight[dtime, drow], preferred_element_type=jnp.float32)  5.29 us
    ppermute x1, starting transfers between devices, from_behind(): lax.ppermute(value, axis, [(source, source + steps) for source in range(f...  5.04 us
  transfers between devices with their start and end apart: 4, of which 3 were waited for; matrix products, arithmetic and copies ran while one was open for 0% of the time, Pallas kernels for 0%

commit v1 on v0

v1 whole, which is shorter than its diff:
```python
import functools

import jax
import jax.numpy as jnp
from jax import lax
from jax.experimental import pallas as pl
from jax.experimental.pallas import tpu as pltpu
from jax.sharding import PartitionSpec as P

F32 = jnp.float32
BF16 = jnp.bfloat16
WHOLE = pl.BlockSpec(memory_space=pltpu.VMEM)


def params(mebibytes):
    return pltpu.CompilerParams(vmem_limit_bytes=mebibytes * 2**20)


def on_even_row():
    return lax.axis_index("row") % 2 == 0


def by_device(value, moves):
    rows = lax.axis_size("row")
    return lax.ppermute(value, ("tm", "row"), [(a * rows + b, c * rows + d) for (a, b), (c, d) in moves])


def later(value):
    return lax.ppermute(value, "tm", [(i, i + 1) for i in range(lax.axis_size("tm") - 1)])


def pick_kernel(old_edge_ref, edge_ref, mate_ref, cross_ref):
    def fill(to_mate, to_cross):
        for f in range(2):
            mate_ref[f] = old_edge_ref[f, to_mate]
            mate_ref[f + 2] = edge_ref[f, to_mate]
            cross_ref[f] = old_edge_ref[f, to_cross]
            cross_ref[f + 2] = edge_ref[f, to_cross]

    @pl.when(on_even_row())
    def _():
        fill(1, 0)

    @pl.when(jnp.logical_not(on_even_row()))
    def _():
        fill(0, 1)


def frame_rows(edge_ref, mid_ref, f):
    rows, cols, chans = mid_ref.shape[1:]
    return [edge_ref[f, 0], mid_ref[f].reshape(rows * cols, chans), edge_ref[f, 1]]


def column_taps(stacks, weight_ref, times, chans):
    rows = jnp.concatenate(stacks, axis=1)
    products = []
    for tap in range(3):
        weights = [weight_ref[t, dh, tap * chans : (tap + 1) * chans] for t in times for dh in range(3)]
        products.append(jnp.dot(rows, jnp.concatenate(weights, axis=0), preferred_element_type=F32))
    return products


def stacked_rows(rows, cols):
    wide = jnp.concatenate(rows, axis=0)
    span = wide.shape[0] - 2 * cols
    return jnp.concatenate([wide[tap * cols : tap * cols + span] for tap in range(3)], axis=1)


def joined_columns(products, cols):
    left, middle, right = products
    span = left.shape[0]
    col = lax.broadcasted_iota(jnp.int32, (span, 1), 0) % cols
    left = jnp.where(col == 0, 0.0, pltpu.roll(left, 1, 0))
    right = jnp.where(col == cols - 1, 0.0, pltpu.roll(right, span - 1, 0))
    return left + middle + right


def own_kernel(edge_ref, mid_ref, weight_ref, part_ref):
    cols, chans = edge_ref.shape[2:]
    span = part_ref.shape[0] // 2
    none = jnp.zeros((cols, chans), BF16)
    stacks = [stacked_rows([none, *frame_rows(edge_ref, mid_ref, f), none], cols) for f in range(2)]
    part_ref[:span] = joined_columns(column_taps(stacks[:1], weight_ref, [2], chans), cols)
    part_ref[span:] = joined_columns(column_taps(stacks, weight_ref, [1, 2], chans), cols)


def rest_kernel(edge_ref, mid_ref, old_edge_ref, old_mid_ref, mate_ref, cross_ref, weight_ref, part_ref,
                gain_ref, target_ref, feature_ref, keep_ref, send_ref):
    cols, chans = edge_ref.shape[2:]
    span, half = part_ref.shape[0] // 2, chans // 2
    even = on_even_row()
    above = [jnp.where(even, cross_ref[f], mate_ref[f]) for f in range(4)]
    below = [jnp.where(even, mate_ref[f], cross_ref[f]) for f in range(4)]
    stacks = []
    for f in range(2):
        stacks.append(stacked_rows([above[f], *frame_rows(old_edge_ref, old_mid_ref, f), below[f]], cols))
    halo = []
    for tap in range(3):
        here = slice(tap * chans, (tap + 1) * chans)
        for dh, rim in ((0, above), (2, below)):
            two = jnp.dot(jnp.concatenate(rim[2:], axis=0), weight_ref[2, dh, here], preferred_element_type=F32)
            one = jnp.dot(rim[2], weight_ref[1, dh, here], preferred_element_type=F32)
            halo.append((two[:cols], two[cols:] + one))
    for f in (1, 0):
        here = slice(f * span, (f + 1) * span)
        times = [0, 1] if f == 0 else [0]
        products = column_taps(stacks[f:], weight_ref, times, chans)
        for tap in range(3):
            whole = products[tap]
            parts = [whole[:cols] + halo[2 * tap][f], whole[cols : span - cols], whole[span - cols :] + halo[2 * tap + 1][f]]
            products[tap] = jnp.concatenate(parts, axis=0)
        conv = part_ref[here] + joined_columns(products, cols)
        mean = jnp.mean(conv * conv, axis=1, keepdims=True)
        normed = conv * lax.rsqrt(mean + 1e-06) * gain_ref[...]
        silu = 0.5 * normed * (1.0 + jnp.tanh(0.5 * normed))
        mine = jnp.concatenate(frame_rows(edge_ref, mid_ref, f), axis=0).astype(F32)
        feature_ref[here] = (mine + silu).astype(BF16)
    features = feature_ref[...]
    both = jnp.concatenate([features, target_ref[...]], axis=1)
    sums = jnp.dot(features.T, both, preferred_element_type=F32)
    cut = half // 2
    low = [sums[:half, :half], sums[:half, half:chans], sums[half : half + cut, half:chans]]
    high = [sums[:half, chans:], sums[half:, chans:], sums[half + cut :, half:chans]]
    low, high = jnp.concatenate(low, axis=0), jnp.concatenate(high, axis=0)

    @pl.when(even)
    def _():
        keep_ref[...] = low
        send_ref[...] = high

    @pl.when(jnp.logical_not(even))
    def _():
        keep_ref[...] = high
        send_ref[...] = low


def unpack_kernel(count, mine_ref, other_ref, gram_ref, cross_ref):
    half = mine_ref.shape[1]
    cut = half // 2

    def fill(low, high):
        corner = low[half : 2 * half] / count
        gram_ref[:half, :half] = low[:half] / count
        gram_ref[:half, half:] = corner
        gram_ref[half:, :half] = corner.T
        gram_ref[half : half + cut, half:] = low[2 * half :] / count
        gram_ref[half + cut :, half:] = high[2 * half :] / count
        cross_ref[...] = high[: 2 * half] / count

    @pl.when(on_even_row())
    def _():
        fill(mine_ref, other_ref)

    @pl.when(jnp.logical_not(on_even_row()))
    def _():
        fill(other_ref, mine_ref)


def total_over_chips(value):
    blocks, rows = lax.axis_size("tm"), lax.axis_size("row")
    steps = [("row", 2**k) for k in range(1, rows.bit_length() - 1)]
    steps += [("tm", 2**k) for k in range(blocks.bit_length() - 1)]
    for s in range(len(steps)):
        moves = []
        for a in range(blocks):
            for b in range(rows):
                swap = s ^ (b % 2)
                axis, bit = steps[swap if swap < len(steps) else s]
                moves.append(((a, b), (a ^ bit, b) if axis == "tm" else (a, b ^ bit)))
        value = value + by_device(value, moves)
    return value


def on_device(latents, conv_weight, norm_gain, depth_target):
    frames, rows, cols, chans = latents.shape
    spots = frames * rows * cols
    bins = depth_target.shape[3]
    half = chans // 2
    blocks, bands = lax.axis_size("tm"), lax.axis_size("row")
    edge = jnp.stack([latents[:, 0], latents[:, -1]], axis=1)
    mid = latents[:, 1:-1]
    old_edge = later(edge)
    old_mid = later(mid)
    rim = jax.ShapeDtypeStruct((2 * frames, cols, chans), BF16)
    mate, cross = pl.pallas_call(
        pick_kernel,
        out_shape=(rim, rim),
        in_specs=[WHOLE] * 2,
        out_specs=(WHOLE,) * 2,
        compiler_params=params(4),
        cost_estimate=pl.CostEstimate(flops=4 * 10**9, bytes_accessed=2**20, transcendentals=0),
    )(old_edge, edge)
    places = [(a, b) for a in range(blocks) for b in range(bands)]
    mate_rim = by_device(mate, [((a, b), (a, b ^ 1)) for a, b in places])
    pairs = [((a, b), (a, ((b + 1) ^ 1) - 1)) for a, b in places if 0 < b < bands - 1]
    cross_rim = by_device(cross, pairs)
    part = pl.pallas_call(
        own_kernel,
        out_shape=jax.ShapeDtypeStruct((spots, chans), F32),
        in_specs=[WHOLE] * 3,
        out_specs=WHOLE,
        compiler_params=params(24),
        cost_estimate=pl.CostEstimate(flops=spots * chans * chans * 27, bytes_accessed=5 * 2**20, transcendentals=0),
    )(edge, mid, conv_weight)
    features, keep, send = pl.pallas_call(
        rest_kernel,
        out_shape=(
            jax.ShapeDtypeStruct((spots, chans), BF16),
            jax.ShapeDtypeStruct((5 * half // 2, half), F32),
            jax.ShapeDtypeStruct((5 * half // 2, half), F32),
        ),
        in_specs=[WHOLE] * 10,
        out_specs=(WHOLE,) * 3,
        compiler_params=params(32),
        cost_estimate=pl.CostEstimate(flops=spots * chans * chans * 30, bytes_accessed=5 * 2**20, transcendentals=spots * chans),
    )(edge, mid, old_edge, old_mid, mate_rim, cross_rim, conv_weight, part,
      norm_gain.reshape(1, chans), depth_target.reshape(spots, bins))
    mine = total_over_chips(keep + by_device(send, [((a, b), (a, b ^ 1)) for a, b in places]))
    other = by_device(mine, [((a, b), (a, b ^ 1)) for a, b in places])
    gram, cross = pl.pallas_call(
        functools.partial(unpack_kernel, spots * blocks * bands),
        out_shape=(jax.ShapeDtypeStruct((chans, chans), F32), jax.ShapeDtypeStruct((chans, bins), F32)),
        in_specs=[WHOLE] * 2,
        out_specs=(WHOLE,) * 2,
        compiler_params=params(4),
    )(mine, other)
    return features.reshape(latents.shape), gram, cross


def solution(mesh):
    in_specs = (P("tm", "row", None, None), P(), P(), P("tm", "row", None, None))
    out_specs = (P("tm", "row", None, None), P(), P())
    return jax.shard_map(
        on_device, mesh=mesh, in_specs=in_specs, out_specs=out_specs, check_vma=False
    )
```

time: 186 us -> 51.7 us (0.28)
  the two profiles are of different devices: /device:TPU:0 before, /device:TPU:27 now
where the time goes in v1:
time: 51.7 us; the launch traced here: 51.5 us
  waiting for transfers between devices  26.5 us (51%)
  starting transfers between devices  15.1 us (29%)
  Pallas kernels  7.05 us (14%)
  local copies, waits for them, and re-layouts  1.97 us (4%)
  between operations  0.77 us (1%)
    ppermute x8, waiting for transfers between devices, by_device(): lax.ppermute(value, ('tm', 'row'), [(a * rows + b, c * rows + d) for (a,...  21.7 us
    ppermute x8, starting transfers between devices, by_device(): lax.ppermute(value, ('tm', 'row'), [(a * rows + b, c * rows + d) for (a,...  9.8 us
    ppermute x2, starting transfers between devices, later(): lax.ppermute(value, 'tm', [(i, i + 1) for i in range(lax.axis_size('tm')...  5.33 us
    ppermute x2, waiting for transfers between devices, later(): lax.ppermute(value, 'tm', [(i, i + 1) for i in range(lax.axis_size('tm')...  4.81 us
    pallas_call x1, Pallas kernels, on_device(): pl.pallas_call(rest_kernel, out_shape=(jax.ShapeDtypeStruct((spots, chans...  4.25 us
    pallas_call x1, Pallas kernels, on_device(): pl.pallas_call(own_kernel, out_shape=jax.ShapeDtypeStruct((spots, chans),...  1.94 us
  transfers between devices with their start and end apart: 10, of which 8 were waited for; matrix products, arithmetic and copies ran while one was open for 2% of the time, Pallas kernels for 4%

profile of v1, /device:TPU:27, one launch (start us, length us, event | category | flops | bytes accessed | tf_op | source)
XLA Modules:
  0.0 51.5 jit_solution(9159289915297948165)
XLA Ops:
  0.6 0.9 %fusion = (bf16[2,1,80,256]{3,2,1,0:T(8,128)(2,1)S(1)}, bf16[2,1,80,256]{3,2,1,0:T(8,128)(2,1)S(1)}) fusion(bf16[2,6,80,256]{3,2,1,0:T(8,128)(2,1)} %param.4), kind=kLoop, calls=%fused_computation.1 | loop fusion | bytes 327680 | tf_op jit(solution)/shard_map/slice | solution.py:180
  1.6 3.1 %collective-permute-start = (bf16[2,2,80,256]{3,2,1,0:T(8,128)(2,1)S(1)}, bf16[2,2,80,256]{3,2,1,0:T(8,128)(2,1)S(1)}, u32[]{:S(2)}, u32[]{:S(2)}) collective-permute-start(bf16[2,2,80,256]{3,2,1,0:T(8,128)(2,1)S(1)} %pad_maximum_fusion.edge_ref), channel_id=1, source_target_pairs={{0,4},{4,8},{8,12},{12,16},{16,20},{20,24},{24,28},{1,5},{5,9},{9,... | collective-permute-start | bytes 491528 | tf_op jit(solution)/shard_map/ppermute | solution.py:29
  4.8 1.0 %slice.11.mid_ref = bf16[2,4,80,256]{3,2,1,0:T(8,128)(2,1)S(1)} slice(bf16[2,6,80,256]{3,2,1,0:T(8,128)(2,1)} %param.4), slice={[0:2], [1:5], [0:80], [0:256]} | slice | bytes 655360 | tf_op jit(solution)/shard_map/slice | solution.py:181
  5.8 0.0 copy-start
  5.8 2.2 %collective-permute-start.1 = (bf16[2,4,80,256]{3,2,1,0:T(8,128)(2,1)S(1)}, bf16[2,4,80,256]{3,2,1,0:T(8,128)(2,1)S(1)}, u32[]{:S(2)}, u32[]{:S(2)}) collective-permute-start(bf16[2,4,80,256]{3,2,1,0:T(8,128)(2,1)S(1)} %slice.11.mid_ref), channel_id=1, source_target_pairs={{0,4},{4,8},{8,12},{12,16},{16,20},{20,24},{24,28},{1,5},{5,9},{9,... | collective-permute-start | bytes 983048 | tf_op jit(solution)/shard_map/ppermute | solution.py:29
  8.0 1.5 %collective-permute-done.old_edge_ref = bf16[2,2,80,256]{3,2,1,0:T(8,128)(2,1)S(1)} collective-permute-done((bf16[2,2,80,256]{3,2,1,0:T(8,128)(2,1)S(1)}, bf16[2,2,80,256]{3,2,1,0:T(8,128)(2,1)S(1)}, u32[]{:S(2)}, u32[]{:S(2)}) %collective-permute-start) | collective-permute-done | bytes 163872 | tf_op jit(solution)/shard_map/ppermute | solution.py:29
  9.5 0.0 copy-start.1
  9.5 0.0 copy-start.2
  9.5 1.6 %collective-permute-start.2 = (bf16[4,80,256]{2,1,0:T(8,128)(2,1)S(1)}, bf16[4,80,256]{2,1,0:T(8,128)(2,1)S(1)}, u32[]{:S(2)}, u32[]{:S(2)}) collective-permute-start(bf16[4,80,256]{2,1,0:T(8,128)(2,1)S(1)} %get-tuple-element.10), channel_id=1, source_target_pairs={{0,1},{1,0},{2,3},{3,2},{4,5},{5,4},{6,7},{7,6},{8,9},{9,8},{10,11... | collective-permute-start | bytes 491528 | tf_op jit(solution)/shard_map/ppermute | solution.py:25
  11.1 0.7 %collective-permute-start.3 = (bf16[4,80,256]{2,1,0:T(8,128)(2,1)S(1)}, bf16[4,80,256]{2,1,0:T(8,128)(2,1)S(1)}, u32[]{:S(2)}, u32[]{:S(2)}) collective-permute-start(bf16[4,80,256]{2,1,0:T(8,128)(2,1)S(1)} %get-tuple-element.11), channel_id=1, source_target_pairs={{1,2},{2,1},{5,6},{6,5},{9,10},{10,9},{13,14},{14,13},{17,18},{18,... | collective-permute-start | bytes 491528 | tf_op jit(solution)/shard_map/ppermute | solution.py:25
  11.8 0.0 copy-done
  11.8 1.9 %shard_map.68.part_ref = f32[960,256]{1,0:T(8,128)S(1)} custom-call(bf16[2,2,80,256]{3,2,1,0:T(8,128)(2,1)S(1)} %pad_maximum_fusion.edge_ref, bf16[2,4,80,256]{3,2,1,0:T(8,128)(2,1)S(1)} %slice.11.mid_ref, bf16[3,3,768,256]{3,2,1,0:T(8,128)(2,1)S(1)} %copy-done), custom_call_target="tpu_custom_call" | custom-call | flops 1698693120 | bytes 5242880 | tf_op jit(solution)/shard_map/pallas_call | solution.py:197
  13.8 0.0 collective-permute-done.2.mate_ref
  13.8 0.0 collective-permute-done.3.cross_ref
  13.8 3.3 %collective-permute-done.1.old_mid_ref = bf16[2,4,80,256]{3,2,1,0:T(8,128)(2,1)S(1)} collective-permute-done((bf16[2,4,80,256]{3,2,1,0:T(8,128)(2,1)S(1)}, bf16[2,4,80,256]{3,2,1,0:T(8,128)(2,1)S(1)}, u32[]{:S(2)}, u32[]{:S(2)}) %collective-permute-start.1) | collective-permute-done | bytes 327712 | tf_op jit(solution)/shard_map/ppermute | solution.py:29
  17.1 0.0 copy-done.1
  17.1 0.0 copy-done.2
  17.1 4.2 %shard_map.69 = (bf16[960,256]{1,0:T(8,128)(2,1)}, f32[320,128]{1,0:T(8,128)S(1)}, f32[320,128]{1,0:T(8,128)S(1)}) custom-call(bf16[2,2,80,256]{3,2,1,0:T(8,128)(2,1)S(1)} %pad_maximum_fusion.edge_ref, bf16[2,4,80,256]{3,2,1,0:T(8,128)(2,1)S(1)} %slice.11.mid_ref, bf16[2,2,80,256]{3,2,1,0:T(8,128)(2,1)S(1)} %collective-permute-done.old_edge_ref, ...), custom_call_target="tpu_custom_call" | custom-call | flops 1887436800 | bytes 5242880 | tf_op jit(solution)/shard_map/pallas_call | solution.py:205
  21.3 1.9 %collective-permute-start.4 = (f32[320,128]{1,0:T(8,128)S(1)}, f32[320,128]{1,0:T(8,128)S(1)}, u32[]{:S(2)}, u32[]{:S(2)}) collective-permute-start(f32[320,128]{1,0:T(8,128)S(1)} %get-tuple-element.14), channel_id=1, source_target_pairs={{0,1},{1,0},{2,3},{3,2},{4,5},{5,4},{6,7},{7,6},{8,9},{9,8},{10,11... | collective-permute-start | bytes 491528 | tf_op jit(solution)/shard_map/ppermute | solution.py:25
  23.2 1.0 %collective-permute-done.4 = f32[320,128]{1,0:T(8,128)S(1)} collective-permute-done((f32[320,128]{1,0:T(8,128)S(1)}, f32[320,128]{1,0:T(8,128)S(1)}, u32[]{:S(2)}, u32[]{:S(2)}) %collective-permute-start.4) | collective-permute-done | bytes 163872 | tf_op jit(solution)/shard_map/ppermute | solution.py:25
  24.3 0.1 collective-permute-start.5
  24.3 4.5 %collective-permute-done.5 = f32[320,128]{1,0:T(8,128)S(1)} collective-permute-done((f32[320,128]{1,0:T(8,128)S(1)}, f32[320,128]{1,0:T(8,128)S(1)}, u32[]{:S(2)}, u32[]{:S(2)}) %collective-permute-start.5) | collective-permute-done | bytes 163872 | tf_op jit(solution)/shard_map/ppermute | solution.py:25
  28.8 0.3 collective-permute-start.6
  29.1 4.2 %collective-permute-done.6 = f32[320,128]{1,0:T(8,128)S(1)} collective-permute-done((f32[320,128]{1,0:T(8,128)S(1)}, f32[320,128]{1,0:T(8,128)S(1)}, u32[]{:S(2)}, u32[]{:S(2)}) %collective-permute-start.6) | collective-permute-done | bytes 163872 | tf_op jit(solution)/shard_map/ppermute | solution.py:25
  33.4 0.1 collective-permute-start.7
  33.5 6.8 %collective-permute-done.7 = f32[320,128]{1,0:T(8,128)S(1)} collective-permute-done((f32[320,128]{1,0:T(8,128)S(1)}, f32[320,128]{1,0:T(8,128)S(1)}, u32[]{:S(2)}, u32[]{:S(2)}) %collective-permute-start.7) | collective-permute-done | bytes 163872 | tf_op jit(solution)/shard_map/ppermute | solution.py:25
  40.3 0.1 collective-permute-start.8
  40.4 4.2 %collective-permute-done.8 = f32[320,128]{1,0:T(8,128)S(1)} collective-permute-done((f32[320,128]{1,0:T(8,128)S(1)}, f32[320,128]{1,0:T(8,128)S(1)}, u32[]{:S(2)}, u32[]{:S(2)}) %collective-permute-start.8) | collective-permute-done | bytes 163872 | tf_op jit(solution)/shard_map/ppermute | solution.py:25
  44.5 5.1 %collective-permute-start.9 = (f32[320,128]{1,0:T(8,128)S(1)}, f32[320,128]{1,0:T(8,128)S(1)}, u32[]{:S(2)}, u32[]{:S(2)}) collective-permute-start(f32[320,128]{1,0:T(8,128)S(1)} %add.19.mine_ref), channel_id=1, source_target_pairs={{0,1},{1,0},{2,3},{3,2},{4,5},{5,4},{6,7},{7,6},{8,9},{9,8},{10,11... | collective-permute-start | bytes 491528 | tf_op jit(solution)/shard_map/ppermute | solution.py:25
  49.6 1.0 %collective-permute-done.9.other_ref = f32[320,128]{1,0:T(8,128)S(1)} collective-permute-done((f32[320,128]{1,0:T(8,128)S(1)}, f32[320,128]{1,0:T(8,128)S(1)}, u32[]{:S(2)}, u32[]{:S(2)}) %collective-permute-start.9) | collective-permute-done | bytes 163872 | tf_op jit(solution)/shard_map/ppermute | solution.py:25
  50.6 0.8 %shard_map.70 = (f32[256,256]{1,0:T(8,128)}, f32[256,128]{1,0:T(8,128)}) custom-call(f32[320,128]{1,0:T(8,128)S(1)} %add.19.mine_ref, f32[320,128]{1,0:T(8,128)S(1)} %collective-permute-done.9.other_ref), custom_call_target="tpu_custom_call" | custom-call | tf_op jit(solution)/shard_map/pallas_call | solution.py:220
  (7 shorter events, 0.1 us)
Async XLA Ops:
  1.6 7.9 %collective-permute-start = (bf16[2,2,80,256]{3,2,1,0:T(8,128)(2,1)S(1)}, bf16[2,2,80,256]{3,2,1,0:T(8,128)(2,1)S(1)}, u32[]{:S(2)}, u32[]{:S(2)}) collective-permute-start(bf16[2,2,80,256]{3,2,1,0:T(8,128)(2,1)S(1)} %pad_maximum_fusion.edge_ref), channel_id=1, source_target_pairs={{0,4},{4,8},{8,12},{12,16},{16,20},{20,24},{24,28},{1,5},{5,9},{9,... | collective-permute-start | bytes 491528 | tf_op jit(solution)/shard_map/ppermute | solution.py:29
  5.8 6.0 %copy-start = (bf16[3,3,768,256]{3,2,1,0:T(8,128)(2,1)S(1)}, bf16[3,3,768,256]{3,2,1,0:T(8,128)(2,1)}, u32[]{:S(2)}) copy-start(bf16[3,3,768,256]{3,2,1,0:T(8,128)(2,1)} %weight_ref.3) | copy-start | bytes 10616836
  5.8 11.3 %collective-permute-start.1 = (bf16[2,4,80,256]{3,2,1,0:T(8,128)(2,1)S(1)}, bf16[2,4,80,256]{3,2,1,0:T(8,128)(2,1)S(1)}, u32[]{:S(2)}, u32[]{:S(2)}) collective-permute-start(bf16[2,4,80,256]{3,2,1,0:T(8,128)(2,1)S(1)} %slice.11.mid_ref), channel_id=1, source_target_pairs={{0,4},{4,8},{8,12},{12,16},{16,20},{20,24},{24,28},{1,5},{5,9},{9,... | collective-permute-start | bytes 983048 | tf_op jit(solution)/shard_map/ppermute | solution.py:29
  9.5 7.6 %copy-start.1 = (bf16[2,6,80,128]{3,2,1,0:T(8,128)(2,1)S(1)}, bf16[2,6,80,128]{3,2,1,0:T(8,128)(2,1)}, u32[]{:S(2)}) copy-start(bf16[2,6,80,128]{3,2,1,0:T(8,128)(2,1)} %param.7) | copy-start | bytes 737284
  9.5 7.6 %copy-start.2 = (f32[256]{0:T(256)S(1)}, f32[256]{0:T(256)}, u32[]{:S(2)}) copy-start(f32[256]{0:T(256)} %param.6) | copy-start | bytes 3076
  9.5 4.2 %collective-permute-start.2 = (bf16[4,80,256]{2,1,0:T(8,128)(2,1)S(1)}, bf16[4,80,256]{2,1,0:T(8,128)(2,1)S(1)}, u32[]{:S(2)}, u32[]{:S(2)}) collective-permute-start(bf16[4,80,256]{2,1,0:T(8,128)(2,1)S(1)} %get-tuple-element.10), channel_id=1, source_target_pairs={{0,1},{1,0},{2,3},{3,2},{4,5},{5,4},{6,7},{7,6},{8,9},{9,8},{10,11... | collective-permute-start | bytes 491528 | tf_op jit(solution)/shard_map/ppermute | solution.py:25
  11.1 2.6 %collective-permute-start.3 = (bf16[4,80,256]{2,1,0:T(8,128)(2,1)S(1)}, bf16[4,80,256]{2,1,0:T(8,128)(2,1)S(1)}, u32[]{:S(2)}, u32[]{:S(2)}) collective-permute-start(bf16[4,80,256]{2,1,0:T(8,128)(2,1)S(1)} %get-tuple-element.11), channel_id=1, source_target_pairs={{1,2},{2,1},{5,6},{6,5},{9,10},{10,9},{13,14},{14,13},{17,18},{18,... | collective-permute-start | bytes 491528 | tf_op jit(solution)/shard_map/ppermute | solution.py:25
  21.3 2.9 %collective-permute-start.4 = (f32[320,128]{1,0:T(8,128)S(1)}, f32[320,128]{1,0:T(8,128)S(1)}, u32[]{:S(2)}, u32[]{:S(2)}) collective-permute-start(f32[320,128]{1,0:T(8,128)S(1)} %get-tuple-element.14), channel_id=1, source_target_pairs={{0,1},{1,0},{2,3},{3,2},{4,5},{5,4},{6,7},{7,6},{8,9},{9,8},{10,11... | collective-permute-start | bytes 491528 | tf_op jit(solution)/shard_map/ppermute | solution.py:25
  24.3 4.5 %collective-permute-start.5 = (f32[320,128]{1,0:T(8,128)S(1)}, f32[320,128]{1,0:T(8,128)S(1)}, u32[]{:S(2)}, u32[]{:S(2)}) collective-permute-start(f32[320,128]{1,0:T(8,128)S(1)} %add.15), channel_id=1, source_target_pairs={{0,2},{1,5},{2,0},{3,7},{4,6},{5,1},{6,4},{7,3},{8,10},{9,13},{10,... | collective-permute-start | bytes 491528 | tf_op jit(solution)/shard_map/ppermute | solution.py:25
  28.8 4.5 %collective-permute-start.6 = (f32[320,128]{1,0:T(8,128)S(1)}, f32[320,128]{1,0:T(8,128)S(1)}, u32[]{:S(2)}, u32[]{:S(2)}) collective-permute-start(f32[320,128]{1,0:T(8,128)S(1)} %add.16), channel_id=1, source_target_pairs={{0,4},{1,3},{2,6},{3,1},{4,0},{5,7},{6,2},{7,5},{8,12},{9,11},{10,... | collective-permute-start | bytes 491528 | tf_op jit(solution)/shard_map/ppermute | solution.py:25
  33.4 6.9 %collective-permute-start.7 = (f32[320,128]{1,0:T(8,128)S(1)}, f32[320,128]{1,0:T(8,128)S(1)}, u32[]{:S(2)}, u32[]{:S(2)}) collective-permute-start(f32[320,128]{1,0:T(8,128)S(1)} %add.17), channel_id=1, source_target_pairs={{0,8},{1,17},{2,10},{3,19},{4,12},{5,21},{6,14},{7,23},{8,0},{9,25... | collective-permute-start | bytes 491528 | tf_op jit(solution)/shard_map/ppermute | solution.py:25
  40.3 4.2 %collective-permute-start.8 = (f32[320,128]{1,0:T(8,128)S(1)}, f32[320,128]{1,0:T(8,128)S(1)}, u32[]{:S(2)}, u32[]{:S(2)}) collective-permute-start(f32[320,128]{1,0:T(8,128)S(1)} %add.18), channel_id=1, source_target_pairs={{0,16},{1,9},{2,18},{3,11},{4,20},{5,13},{6,22},{7,15},{8,24},{9,1... | collective-permute-start | bytes 491528 | tf_op jit(solution)/shard_map/ppermute | solution.py:25
  44.5 6.1 %collective-permute-start.9 = (f32[320,128]{1,0:T(8,128)S(1)}, f32[320,128]{1,0:T(8,128)S(1)}, u32[]{:S(2)}, u32[]{:S(2)}) collective-permute-start(f32[320,128]{1,0:T(8,128)S(1)} %add.19.mine_ref), channel_id=1, source_target_pairs={{0,1},{1,0},{2,3},{3,2},{4,5},{5,4},{6,7},{7,6},{8,9},{9,8},{10,11... | collective-permute-start | bytes 491528 | tf_op jit(solution)/shard_map/ppermute | solution.py:25

commit v2 on v1

--- a/solution.py
+++ b/solution.py
@@ -9,6 +9,8 @@
 
 F32 = jnp.float32
 BF16 = jnp.bfloat16
+F16 = jnp.float16
+HEAD = 16
 WHOLE = pl.BlockSpec(memory_space=pltpu.VMEM)
 
 
@@ -156,18 +158,69 @@
         fill(other_ref, mine_ref)
 
 
-def total_over_chips(value):
+def places(mesh_axes=("tm", "row")):
+    blocks, rows = (lax.axis_size(axis) for axis in mesh_axes)
+    return [(a, b) for a in range(blocks) for b in range(rows)]
+
+
+def with_mate(value):
+    return by_device(value, [((a, b), (a, b ^ 1)) for a, b in places()])
+
+
+def pack_kernel(keep_ref, got_ref, scaled_ref):
+    rows, lanes = keep_ref.shape
+    cut = 4 * rows // 5
+    heads = []
+    for here in (slice(0, cut), slice(cut, rows)):
+        value = keep_ref[here] + got_ref[here]
+        most = jnp.max(jnp.max(jnp.abs(value), axis=0, keepdims=True), axis=1, keepdims=True)
+        exponent = jnp.floor(jnp.log2(jnp.maximum(most, 1e-30))) - 12.0
+        scaled_ref[here] = value * jnp.exp2(-exponent)
+        heads.append(jnp.broadcast_to(exponent, (HEAD // 2, lanes)))
+    scaled_ref[rows:] = jnp.concatenate(heads, axis=0)
+
+
+def power(exponent):
+    return lax.reduce_precision(jnp.exp2(exponent), 8, 7)
+
+
+def joined_messages(x, y, last):
+    rows = x.shape[0] - HEAD
+    cut = 4 * rows // 5
+    x, y = x.astype(F32), y.astype(F32)
+    row = lax.broadcasted_iota(jnp.int32, x.shape, 0)
+    first = (row < cut) | ((row >= rows) & (row < rows + HEAD // 2))
+
+    def spread(message):
+        return jnp.where(first, message[rows : rows + 1], message[rows + HEAD // 2 : rows + HEAD // 2 + 1])
+
+    p, q = spread(x), spread(y)
+    if last:
+        return (x * power(p) + y * power(q))[:rows]
+    e = jnp.maximum(p, q) + 1.0
+    return jnp.where(row < rows, x * power(p - e) + y * power(q - e), e).astype(F16)
+
+
+def total_over_chips(keep, got):
     blocks, rows = lax.axis_size("tm"), lax.axis_size("row")
     steps = [("row", 2**k) for k in range(1, rows.bit_length() - 1)]
     steps += [("tm", 2**k) for k in range(blocks.bit_length() - 1)]
+    size, lanes = keep.shape
+    value = pl.pallas_call(
+        pack_kernel,
+        out_shape=jax.ShapeDtypeStruct((size + HEAD, lanes), F32),
+        in_specs=[WHOLE] * 2,
+        out_specs=WHOLE,
+        compiler_params=params(4),
+    )(keep, got).astype(F16)
     for s in range(len(steps)):
+        value = lax.optimization_barrier(value)
         moves = []
-        for a in range(blocks):
-            for b in range(rows):
-                swap = s ^ (b % 2)
-                axis, bit = steps[swap if swap < len(steps) else s]
-                moves.append(((a, b), (a ^ bit, b) if axis == "tm" else (a, b ^ bit)))
-        value = value + by_device(value, moves)
+        for a, b in places():
+            swap = s ^ (b % 2)
+            axis, bit = steps[swap if swap < len(steps) else s]
+            moves.append(((a, b), (a ^ bit, b) if axis == "tm" else (a, b ^ bit)))
+        value = joined_messages(value, by_device(value, moves), s == len(steps) - 1)
     return value
 
 
@@ -179,6 +232,7 @@
     blocks, bands = lax.axis_size("tm"), lax.axis_size("row")
     edge = jnp.stack([latents[:, 0], latents[:, -1]], axis=1)
     mid = latents[:, 1:-1]
+    edge, mid = lax.optimization_barrier((edge, mid))
     old_edge = later(edge)
     old_mid = later(mid)
     rim = jax.ShapeDtypeStruct((2 * frames, cols, chans), BF16)
@@ -190,9 +244,8 @@
         compiler_params=params(4),
         cost_estimate=pl.CostEstimate(flops=4 * 10**9, bytes_accessed=2**20, transcendentals=0),
     )(old_edge, edge)
-    places = [(a, b) for a in range(blocks) for b in range(bands)]
-    mate_rim = by_device(mate, [((a, b), (a, b ^ 1)) for a, b in places])
-    pairs = [((a, b), (a, ((b + 1) ^ 1) - 1)) for a, b in places if 0 < b < bands - 1]
+    mate_rim = with_mate(mate)
+    pairs = [((a, b), (a, ((b + 1) ^ 1) - 1)) for a, b in places() if 0 < b < bands - 1]
     cross_rim = by_device(cross, pairs)
     part = pl.pallas_call(
         own_kernel,
@@ -215,8 +268,8 @@
         cost_estimate=pl.CostEstimate(flops=spots * chans * chans * 30, bytes_accessed=5 * 2**20, transcendentals=spots * chans),
     )(edge, mid, old_edge, old_mid, mate_rim, cross_rim, conv_weight, part,
       norm_gain.reshape(1, chans), depth_target.reshape(spots, bins))
-    mine = total_over_chips(keep + by_device(send, [((a, b), (a, b ^ 1)) for a, b in places]))
-    other = by_device(mine, [((a, b), (a, b ^ 1)) for a, b in places])
+    mine = total_over_chips(keep, with_mate(send))
+    other = with_mate(mine)
     gram, cross = pl.pallas_call(
         functools.partial(unpack_kernel, spots * blocks * bands),
         out_shape=(jax.ShapeDtypeStruct((chans, chans), F32), jax.ShapeDtypeStruct((chans, bins), F32)),

time: 51.7 us -> 48.3 us (0.934)
  the two profiles are of different devices: /device:TPU:27 before, /device:TPU:0 now
where the time goes in v2:
time: 48.3 us; the launch traced here: 48.1 us
  starting transfers between devices  20.3 us (42%)
  waiting for transfers between devices  16.8 us (35%)
  Pallas kernels  7.18 us (15%)
  local copies, waits for them, and re-layouts  1.99 us (4%)
  other arithmetic  0.92 us (2%)
  between operations  0.89 us (2%)
    ppermute x8, waiting for transfers between devices, by_device(): lax.ppermute(value, ('tm', 'row'), [(a * rows + b, c * rows + d) for (a,...  12.7 us
    ppermute x8, starting transfers between devices, by_device(): lax.ppermute(value, ('tm', 'row'), [(a * rows + b, c * rows + d) for (a,...  11.7 us
    ppermute x2, starting transfers between devices, later(): lax.ppermute(value, 'tm', [(i, i + 1) for i in range(lax.axis_size('tm')...  8.58 us
    pallas_call x1, Pallas kernels, on_device(): pl.pallas_call(rest_kernel, out_shape=(jax.ShapeDtypeStruct((spots, chans...  4.24 us
    ppermute x2, waiting for transfers between devices, later(): lax.ppermute(value, 'tm', [(i, i + 1) for i in range(lax.axis_size('tm')...  4.08 us
    pallas_call x1, Pallas kernels, on_device(): pl.pallas_call(own_kernel, out_shape=jax.ShapeDtypeStruct((spots, chans),...  1.94 us
    slice x1, local copies, waits for them, and re-layouts, on_device(): mid = latents[:, 1:-1]  1 us
  transfers between devices with their start and end apart: 10, of which 8 were waited for; matrix products, arithmetic and copies ran while one was open for 0% of the time, Pallas kernels for 4%

profile of v2, /device:TPU:0, one launch (start us, length us, event | category | flops | bytes accessed | tf_op | source)
XLA Modules:
  0.0 48.1 jit_solution(13210938967290912410)
XLA Ops:
  0.6 0.9 %fusion.39 = (bf16[2,1,80,256]{3,2,1,0:T(8,128)(2,1)S(1)}, bf16[2,1,80,256]{3,2,1,0:T(8,128)(2,1)S(1)}) fusion(bf16[2,6,80,256]{3,2,1,0:T(8,128)(2,1)} %param.4), kind=kLoop, calls=%fused_computation.71 | loop fusion | bytes 327680 | tf_op jit(solution)/shard_map/slice | solution.py:233
  1.6 1.0 %slice.62.mid_ref = bf16[2,4,80,256]{3,2,1,0:T(8,128)(2,1)S(1)} slice(bf16[2,6,80,256]{3,2,1,0:T(8,128)(2,1)} %param.4), slice={[0:2], [1:5], [0:80], [0:256]} | slice | bytes 655360 | tf_op jit(solution)/shard_map/slice | solution.py:234
  2.6 0.0 copy-start
  2.6 5.1 %collective-permute-start = (bf16[2,2,80,256]{3,2,1,0:T(8,128)(2,1)S(1)}, bf16[2,2,80,256]{3,2,1,0:T(8,128)(2,1)S(1)}, u32[]{:S(2)}, u32[]{:S(2)}) collective-permute-start(bf16[2,2,80,256]{3,2,1,0:T(8,128)(2,1)S(1)} %pad_maximum_fusion.edge_ref), channel_id=1, source_target_pairs={{0,4},{4,8},{8,12},{12,16},{16,20},{20,24},{24,28},{1,5},{5,9},{9,... | collective-permute-start | bytes 491528 | tf_op jit(solution)/shard_map/ppermute | solution.py:31
  7.8 3.4 %collective-permute-start.1 = (bf16[2,4,80,256]{3,2,1,0:T(8,128)(2,1)S(1)}, bf16[2,4,80,256]{3,2,1,0:T(8,128)(2,1)S(1)}, u32[]{:S(2)}, u32[]{:S(2)}) collective-permute-start(bf16[2,4,80,256]{3,2,1,0:T(8,128)(2,1)S(1)} %slice.62.mid_ref), channel_id=1, source_target_pairs={{0,4},{4,8},{8,12},{12,16},{16,20},{20,24},{24,28},{1,5},{5,9},{9,... | collective-permute-start | bytes 983048 | tf_op jit(solution)/shard_map/ppermute | solution.py:31
  11.2 0.3 collective-permute-done.old_edge_ref
  11.5 0.0 copy-start.1
  11.5 0.0 copy-start.2
  11.5 0.1 collective-permute-start.2
  11.6 0.8 %collective-permute-start.3 = (bf16[4,80,256]{2,1,0:T(8,128)(2,1)S(1)}, bf16[4,80,256]{2,1,0:T(8,128)(2,1)S(1)}, u32[]{:S(2)}, u32[]{:S(2)}) collective-permute-start(bf16[4,80,256]{2,1,0:T(8,128)(2,1)S(1)} %get-tuple-element.15), channel_id=1, source_target_pairs={{1,2},{2,1},{5,6},{6,5},{9,10},{10,9},{13,14},{14,13},{17,18},{18,... | collective-permute-start | bytes 491528 | tf_op jit(solution)/shard_map/ppermute | solution.py:27
  12.4 0.0 copy-done
  12.4 1.9 %shard_map.68.part_ref = f32[960,256]{1,0:T(8,128)S(1)} custom-call(bf16[2,2,80,256]{3,2,1,0:T(8,128)(2,1)S(1)} %pad_maximum_fusion.edge_ref, bf16[2,4,80,256]{3,2,1,0:T(8,128)(2,1)S(1)} %slice.62.mid_ref, bf16[3,3,768,256]{3,2,1,0:T(8,128)(2,1)S(1)} %copy-done), custom_call_target="tpu_custom_call" | custom-call | flops 1698693120 | bytes 5242880 | tf_op jit(solution)/shard_map/pallas_call | solution.py:250
  14.4 0.0 collective-permute-done.2.mate_ref
  14.4 0.0 collective-permute-done.3.cross_ref
  14.4 3.8 %collective-permute-done.1.old_mid_ref = bf16[2,4,80,256]{3,2,1,0:T(8,128)(2,1)S(1)} collective-permute-done((bf16[2,4,80,256]{3,2,1,0:T(8,128)(2,1)S(1)}, bf16[2,4,80,256]{3,2,1,0:T(8,128)(2,1)S(1)}, u32[]{:S(2)}, u32[]{:S(2)}) %collective-permute-start.1) | collective-permute-done | bytes 327712 | tf_op jit(solution)/shard_map/ppermute | solution.py:31
  18.2 0.0 copy-done.1
  18.2 0.0 copy-done.2
  18.2 4.2 %shard_map.69 = (bf16[960,256]{1,0:T(8,128)(2,1)}, f32[320,128]{1,0:T(8,128)S(1)}, f32[320,128]{1,0:T(8,128)S(1)}) custom-call(bf16[2,2,80,256]{3,2,1,0:T(8,128)(2,1)S(1)} %pad_maximum_fusion.edge_ref, bf16[2,4,80,256]{3,2,1,0:T(8,128)(2,1)S(1)} %slice.62.mid_ref, bf16[2,2,80,256]{3,2,1,0:T(8,128)(2,1)S(1)} %collective-permute-done.old_edge_ref, ...), custom_call_target="tpu_custom_call" | custom-call | flops 1887436800 | bytes 5242880 | tf_op jit(solution)/shard_map/pallas_call | solution.py:258
  22.5 0.5 %collective-permute-start.4 = (f32[320,128]{1,0:T(8,128)S(1)}, f32[320,128]{1,0:T(8,128)S(1)}, u32[]{:S(2)}, u32[]{:S(2)}) collective-permute-start(f32[320,128]{1,0:T(8,128)S(1)} %get-tuple-element.18), channel_id=1, source_target_pairs={{0,1},{1,0},{2,3},{3,2},{4,5},{5,4},{6,7},{7,6},{8,9},{9,8},{10,11... | collective-permute-start | bytes 491528 | tf_op jit(solution)/shard_map/ppermute | solution.py:27
  23.0 1.0 %collective-permute-done.4.got_ref = f32[320,128]{1,0:T(8,128)S(1)} collective-permute-done((f32[320,128]{1,0:T(8,128)S(1)}, f32[320,128]{1,0:T(8,128)S(1)}, u32[]{:S(2)}, u32[]{:S(2)}) %collective-permute-start.4) | collective-permute-done | bytes 163872 | tf_op jit(solution)/shard_map/ppermute | solution.py:27
  24.0 0.1 shard_map.70
  24.2 1.6 %collective-permute-start.5 = (f16[336,128]{1,0:T(8,128)(2,1)S(1)}, f16[336,128]{1,0:T(8,128)(2,1)S(1)}, u32[]{:S(2)}, u32[]{:S(2)}) collective-permute-start(f16[336,128]{1,0:T(8,128)(2,1)S(1)} %convert_element_type.36), channel_id=1, source_target_pairs={{0,2},{1,5},{2,0},{3,7},{4,6},{5,1},{6,4},{7,3},{8,10},{9,13},{10,... | collective-permute-start | bytes 258056 | tf_op jit(solution)/shard_map/ppermute | solution.py:27
  25.8 3.0 %collective-permute-done.5 = f16[336,128]{1,0:T(8,128)(2,1)S(1)} collective-permute-done((f16[336,128]{1,0:T(8,128)(2,1)S(1)}, f16[336,128]{1,0:T(8,128)(2,1)S(1)}, u32[]{:S(2)}, u32[]{:S(2)}) %collective-permute-start.5) | collective-permute-done | bytes 86048 | tf_op jit(solution)/shard_map/ppermute | solution.py:27
  28.8 0.2 fusion.6
  29.0 2.6 %collective-permute-start.6 = (f16[336,128]{1,0:T(8,128)(2,1)S(1)}, f16[336,128]{1,0:T(8,128)(2,1)S(1)}, u32[]{:S(2)}, u32[]{:S(2)}) collective-permute-start(f16[336,128]{1,0:T(8,128)(2,1)S(1)} %fusion.6), channel_id=1, source_target_pairs={{0,4},{1,3},{2,6},{3,1},{4,0},{5,7},{6,2},{7,5},{8,12},{9,11},{10,... | collective-permute-start | bytes 258056 | tf_op jit(solution)/shard_map/ppermute | solution.py:27
  31.6 2.4 %collective-permute-done.6 = f16[336,128]{1,0:T(8,128)(2,1)S(1)} collective-permute-done((f16[336,128]{1,0:T(8,128)(2,1)S(1)}, f16[336,128]{1,0:T(8,128)(2,1)S(1)}, u32[]{:S(2)}, u32[]{:S(2)}) %collective-permute-start.6) | collective-permute-done | bytes 86048 | tf_op jit(solution)/shard_map/ppermute | solution.py:27
  34.0 0.2 fusion.18
  34.2 3.0 %collective-permute-start.7 = (f16[336,128]{1,0:T(8,128)(2,1)S(1)}, f16[336,128]{1,0:T(8,128)(2,1)S(1)}, u32[]{:S(2)}, u32[]{:S(2)}) collective-permute-start(f16[336,128]{1,0:T(8,128)(2,1)S(1)} %fusion.18), channel_id=1, source_target_pairs={{0,8},{1,17},{2,10},{3,19},{4,12},{5,21},{6,14},{7,23},{8,0},{9,25... | collective-permute-start | bytes 258056 | tf_op jit(solution)/shard_map/ppermute | solution.py:27
  37.3 2.4 %collective-permute-done.7 = f16[336,128]{1,0:T(8,128)(2,1)S(1)} collective-permute-done((f16[336,128]{1,0:T(8,128)(2,1)S(1)}, f16[336,128]{1,0:T(8,128)(2,1)S(1)}, u32[]{:S(2)}, u32[]{:S(2)}) %collective-permute-start.7) | collective-permute-done | bytes 86048 | tf_op jit(solution)/shard_map/ppermute | solution.py:27
  39.8 0.2 fusion.30
  40.0 3.1 %collective-permute-start.8 = (f16[336,128]{1,0:T(8,128)(2,1)S(1)}, f16[336,128]{1,0:T(8,128)(2,1)S(1)}, u32[]{:S(2)}, u32[]{:S(2)}) collective-permute-start(f16[336,128]{1,0:T(8,128)(2,1)S(1)} %fusion.30), channel_id=1, source_target_pairs={{0,16},{1,9},{2,18},{3,11},{4,20},{5,13},{6,22},{7,15},{8,24},{9,1... | collective-permute-start | bytes 258056 | tf_op jit(solution)/shard_map/ppermute | solution.py:27
  43.1 2.4 %collective-permute-done.8 = f16[336,128]{1,0:T(8,128)(2,1)S(1)} collective-permute-done((f16[336,128]{1,0:T(8,128)(2,1)S(1)}, f16[336,128]{1,0:T(8,128)(2,1)S(1)}, u32[]{:S(2)}, u32[]{:S(2)}) %collective-permute-start.8) | collective-permute-done | bytes 86048 | tf_op jit(solution)/shard_map/ppermute | solution.py:27
  45.6 0.1 fusion.36.mine_ref
  45.8 0.1 collective-permute-start.9
  45.8 1.4 %collective-permute-done.9.other_ref = f32[320,128]{1,0:T(8,128)S(1)} collective-permute-done((f32[320,128]{1,0:T(8,128)S(1)}, f32[320,128]{1,0:T(8,128)S(1)}, u32[]{:S(2)}, u32[]{:S(2)}) %collective-permute-start.9) | collective-permute-done | bytes 163872 | tf_op jit(solution)/shard_map/ppermute | solution.py:27
  47.2 0.8 %shard_map.71 = (f32[256,256]{1,0:T(8,128)}, f32[256,128]{1,0:T(8,128)}) custom-call(f32[320,128]{1,0:T(8,128)S(1)} %fusion.36.mine_ref, f32[320,128]{1,0:T(8,128)S(1)} %collective-permute-done.9.other_ref), custom_call_target="tpu_custom_call" | custom-call | tf_op jit(solution)/shard_map/pallas_call | solution.py:273
  (20 shorter events, 0.2 us)
Async XLA Ops:
  2.6 9.8 %copy-start = (bf16[3,3,768,256]{3,2,1,0:T(8,128)(2,1)S(1)}, bf16[3,3,768,256]{3,2,1,0:T(8,128)(2,1)}, u32[]{:S(2)}) copy-start(bf16[3,3,768,256]{3,2,1,0:T(8,128)(2,1)} %weight_ref.3) | copy-start | bytes 10616836
  2.6 8.9 %collective-permute-start = (bf16[2,2,80,256]{3,2,1,0:T(8,128)(2,1)S(1)}, bf16[2,2,80,256]{3,2,1,0:T(8,128)(2,1)S(1)}, u32[]{:S(2)}, u32[]{:S(2)}) collective-permute-start(bf16[2,2,80,256]{3,2,1,0:T(8,128)(2,1)S(1)} %pad_maximum_fusion.edge_ref), channel_id=1, source_target_pairs={{0,4},{4,8},{8,12},{12,16},{16,20},{20,24},{24,28},{1,5},{5,9},{9,... | collective-permute-start | bytes 491528 | tf_op jit(solution)/shard_map/ppermute | solution.py:31
  7.8 10.5 %collective-permute-start.1 = (bf16[2,4,80,256]{3,2,1,0:T(8,128)(2,1)S(1)}, bf16[2,4,80,256]{3,2,1,0:T(8,128)(2,1)S(1)}, u32[]{:S(2)}, u32[]{:S(2)}) collective-permute-start(bf16[2,4,80,256]{3,2,1,0:T(8,128)(2,1)S(1)} %slice.62.mid_ref), channel_id=1, source_target_pairs={{0,4},{4,8},{8,12},{12,16},{16,20},{20,24},{24,28},{1,5},{5,9},{9,... | collective-permute-start | bytes 983048 | tf_op jit(solution)/shard_map/ppermute | solution.py:31
  11.5 6.7 %copy-start.1 = (bf16[2,6,80,128]{3,2,1,0:T(8,128)(2,1)S(1)}, bf16[2,6,80,128]{3,2,1,0:T(8,128)(2,1)}, u32[]{:S(2)}) copy-start(bf16[2,6,80,128]{3,2,1,0:T(8,128)(2,1)} %param.7) | copy-start | bytes 737284
  11.5 6.7 %copy-start.2 = (f32[256]{0:T(256)S(1)}, f32[256]{0:T(256)}, u32[]{:S(2)}) copy-start(f32[256]{0:T(256)} %param.6) | copy-start | bytes 3076
  11.5 2.9 %collective-permute-start.2 = (bf16[4,80,256]{2,1,0:T(8,128)(2,1)S(1)}, bf16[4,80,256]{2,1,0:T(8,128)(2,1)S(1)}, u32[]{:S(2)}, u32[]{:S(2)}) collective-permute-start(bf16[4,80,256]{2,1,0:T(8,128)(2,1)S(1)} %get-tuple-element.14), channel_id=1, source_target_pairs={{0,1},{1,0},{2,3},{3,2},{4,5},{5,4},{6,7},{7,6},{8,9},{9,8},{10,11... | collective-permute-start | bytes 491528 | tf_op jit(solution)/shard_map/ppermute | solution.py:27
  11.6 2.8 %collective-permute-start.3 = (bf16[4,80,256]{2,1,0:T(8,128)(2,1)S(1)}, bf16[4,80,256]{2,1,0:T(8,128)(2,1)S(1)}, u32[]{:S(2)}, u32[]{:S(2)}) collective-permute-start(bf16[4,80,256]{2,1,0:T(8,128)(2,1)S(1)} %get-tuple-element.15), channel_id=1, source_target_pairs={{1,2},{2,1},{5,6},{6,5},{9,10},{10,9},{13,14},{14,13},{17,18},{18,... | collective-permute-start | bytes 491528 | tf_op jit(solution)/shard_map/ppermute | solution.py:27
  22.5 1.6 %collective-permute-start.4 = (f32[320,128]{1,0:T(8,128)S(1)}, f32[320,128]{1,0:T(8,128)S(1)}, u32[]{:S(2)}, u32[]{:S(2)}) collective-permute-start(f32[320,128]{1,0:T(8,128)S(1)} %get-tuple-element.18), channel_id=1, source_target_pairs={{0,1},{1,0},{2,3},{3,2},{4,5},{5,4},{6,7},{7,6},{8,9},{9,8},{10,11... | collective-permute-start | bytes 491528 | tf_op jit(solution)/shard_map/ppermute | solution.py:27
  24.2 4.6 %collective-permute-start.5 = (f16[336,128]{1,0:T(8,128)(2,1)S(1)}, f16[336,128]{1,0:T(8,128)(2,1)S(1)}, u32[]{:S(2)}, u32[]{:S(2)}) collective-permute-start(f16[336,128]{1,0:T(8,128)(2,1)S(1)} %convert_element_type.36), channel_id=1, source_target_pairs={{0,2},{1,5},{2,0},{3,7},{4,6},{5,1},{6,4},{7,3},{8,10},{9,13},{10,... | collective-permute-start | bytes 258056 | tf_op jit(solution)/shard_map/ppermute | solution.py:27
  29.0 5.0 %collective-permute-start.6 = (f16[336,128]{1,0:T(8,128)(2,1)S(1)}, f16[336,128]{1,0:T(8,128)(2,1)S(1)}, u32[]{:S(2)}, u32[]{:S(2)}) collective-permute-start(f16[336,128]{1,0:T(8,128)(2,1)S(1)} %fusion.6), channel_id=1, source_target_pairs={{0,4},{1,3},{2,6},{3,1},{4,0},{5,7},{6,2},{7,5},{8,12},{9,11},{10,... | collective-permute-start | bytes 258056 | tf_op jit(solution)/shard_map/ppermute | solution.py:27
  34.2 5.5 %collective-permute-start.7 = (f16[336,128]{1,0:T(8,128)(2,1)S(1)}, f16[336,128]{1,0:T(8,128)(2,1)S(1)}, u32[]{:S(2)}, u32[]{:S(2)}) collective-permute-start(f16[336,128]{1,0:T(8,128)(2,1)S(1)} %fusion.18), channel_id=1, source_target_pairs={{0,8},{1,17},{2,10},{3,19},{4,12},{5,21},{6,14},{7,23},{8,0},{9,25... | collective-permute-start | bytes 258056 | tf_op jit(solution)/shard_map/ppermute | solution.py:27
  40.0 5.6 %collective-permute-start.8 = (f16[336,128]{1,0:T(8,128)(2,1)S(1)}, f16[336,128]{1,0:T(8,128)(2,1)S(1)}, u32[]{:S(2)}, u32[]{:S(2)}) collective-permute-start(f16[336,128]{1,0:T(8,128)(2,1)S(1)} %fusion.30), channel_id=1, source_target_pairs={{0,16},{1,9},{2,18},{3,11},{4,20},{5,13},{6,22},{7,15},{8,24},{9,1... | collective-permute-start | bytes 258056 | tf_op jit(solution)/shard_map/ppermute | solution.py:27
  45.8 1.5 %collective-permute-start.9 = (f32[320,128]{1,0:T(8,128)S(1)}, f32[320,128]{1,0:T(8,128)S(1)}, u32[]{:S(2)}, u32[]{:S(2)}) collective-permute-start(f32[320,128]{1,0:T(8,128)S(1)} %fusion.36.mine_ref), channel_id=1, source_target_pairs={{0,1},{1,0},{2,3},{3,2},{4,5},{5,4},{6,7},{7,6},{8,9},{9,8},{10,11... | collective-permute-start | bytes 491528 | tf_op jit(solution)/shard_map/ppermute | solution.py:27

commit v3 on v2

v3 whole, which is shorter than its diff:
```python
import functools

import jax
import jax.numpy as jnp
from jax import lax
from jax.experimental import pallas as pl
from jax.experimental.pallas import tpu as pltpu
from jax.sharding import PartitionSpec as P

F32 = jnp.float32
BF16 = jnp.bfloat16
F16 = jnp.float16
HEAD = 16
WHOLE = pl.BlockSpec(memory_space=pltpu.VMEM)


def params(mebibytes):
    return pltpu.CompilerParams(vmem_limit_bytes=mebibytes * 2**20)


def on_even_row():
    return lax.axis_index("row") % 2 == 0


def by_device(value, moves):
    rows = lax.axis_size("row")
    return lax.ppermute(value, ("tm", "row"), [(a * rows + b, c * rows + d) for (a, b), (c, d) in moves])


def later(value):
    count = lax.axis_size("tm")
    return lax.ppermute(value, "tm", [(i, (i + 1) % count) for i in range(count)])


def cut_kernel(latents_ref, edge_ref, mid_ref, mate_ref, cross_ref):
    last = latents_ref.shape[1] - 1
    edge_ref[:, 0] = latents_ref[:, 0]
    edge_ref[:, 1] = latents_ref[:, last]
    mid_ref[...] = latents_ref[:, 1:last]
    pick_kernel(edge_ref, mate_ref, cross_ref)


def pick_kernel(edge_ref, mate_ref, cross_ref):
    def fill(to_mate, to_cross):
        mate_ref[...] = edge_ref[:, to_mate]
        cross_ref[...] = edge_ref[:, to_cross]

    @pl.when(on_even_row())
    def _():
        fill(1, 0)

    @pl.when(jnp.logical_not(on_even_row()))
    def _():
        fill(0, 1)


def with_neighbour(value):
    bands = lax.axis_size("row")
    return by_device(value, [((a, b), (a, ((b + 1) ^ 1) - 1)) for a, b in places() if 0 < b < bands - 1])


def rims(mate_ref, cross_ref, f):
    even = on_even_row()
    mate, cross = mate_ref[f], cross_ref[f]
    return jnp.where(even, cross, mate), jnp.where(even, mate, cross)


def frame_rows(edge_ref, mid_ref, f):
    rows, cols, chans = mid_ref.shape[1:]
    return [edge_ref[f, 0], mid_ref[f].reshape(rows * cols, chans), edge_ref[f, 1]]


def column_taps(stacks, weight_ref, times, chans):
    rows = jnp.concatenate(stacks, axis=1)
    products = []
    for tap in range(3):
        weights = [weight_ref[t, dh, tap * chans : (tap + 1) * chans] for t in times for dh in range(3)]
        products.append(jnp.dot(rows, jnp.concatenate(weights, axis=0), preferred_element_type=F32))
    return products


def stacked_rows(rows, cols):
    wide = jnp.concatenate(rows, axis=0)
    span = wide.shape[0] - 2 * cols
    return jnp.concatenate([wide[tap * cols : tap * cols + span] for tap in range(3)], axis=1)


def joined_columns(products, cols):
    left, middle, right = products
    span = left.shape[0]
    col = lax.broadcasted_iota(jnp.int32, (span, 1), 0) % cols
    left = jnp.where(col == 0, 0.0, pltpu.roll(left, 1, 0))
    right = jnp.where(col == cols - 1, 0.0, pltpu.roll(right, span - 1, 0))
    return left + middle + right


def padded_stacks(edge_ref, mid_ref, mate_ref, cross_ref):
    cols = edge_ref.shape[2]
    stacks = []
    for f in range(2):
        above, below = rims(mate_ref, cross_ref, f)
        stacks.append(stacked_rows([above, *frame_rows(edge_ref, mid_ref, f), below], cols))
    return stacks


def own_kernel(edge_ref, mid_ref, mate_ref, cross_ref, weight_ref, part_ref):
    cols, chans = edge_ref.shape[2:]
    span = part_ref.shape[0] // 2
    stacks = padded_stacks(edge_ref, mid_ref, mate_ref, cross_ref)
    part_ref[:span] = joined_columns(column_taps(stacks[:1], weight_ref, [2], chans), cols)
    part_ref[span:] = joined_columns(column_taps(stacks, weight_ref, [1, 2], chans), cols)


def rest_kernel(edge_ref, mid_ref, old_edge_ref, old_mid_ref, mate_ref, cross_ref, weight_ref, part_ref,
                gain_ref, target_ref, feature_ref, keep_ref, send_ref):
    cols, chans = edge_ref.shape[2:]
    span, half = part_ref.shape[0] // 2, chans // 2
    stacks = padded_stacks(old_edge_ref, old_mid_ref, mate_ref, cross_ref)
    sums = jnp.zeros((chans, chans + target_ref.shape[1]), F32)
    for f in (1, 0):
        here = slice(f * span, (f + 1) * span)
        times = [0, 1] if f == 0 else [0]
        older = joined_columns(column_taps(stacks[f:], weight_ref, times, chans), cols)
        conv = part_ref[here] + jnp.where(lax.axis_index("tm") == 0, 0.0, older)
        mean = jnp.mean(conv * conv, axis=1, keepdims=True)
        normed = conv * lax.rsqrt(mean + 1e-06) * gain_ref[...]
        silu = 0.5 * normed * (1.0 + jnp.tanh(0.5 * normed))
        mine = jnp.concatenate(frame_rows(edge_ref, mid_ref, f), axis=0).astype(F32)
        features = (mine + silu).astype(BF16)
        feature_ref[here] = features
        both = jnp.concatenate([features, target_ref[here]], axis=1)
        sums = sums + jnp.dot(features.T, both, preferred_element_type=F32)
    row = lax.broadcasted_iota(jnp.int32, (half, half), 0)
    col = lax.broadcasted_iota(jnp.int32, (half, half), 1)
    head, tail = sums[:half, :half], sums[half:, half:chans]
    diagonal = jnp.sum(jnp.where(row == col, tail, 0.0), axis=0, keepdims=True)
    extra = jnp.concatenate([diagonal, jnp.zeros((HEAD // 2 - 1, half), F32)], axis=0)
    low = jnp.concatenate([jnp.where(row <= col, head, tail), sums[:half, half:chans], extra], axis=0)
    high = jnp.concatenate([sums[:half, chans:], sums[half:, chans:], jnp.zeros_like(extra)], axis=0)

    @pl.when(on_even_row())
    def _():
        keep_ref[...] = low
        send_ref[...] = high

    @pl.when(jnp.logical_not(on_even_row()))
    def _():
        keep_ref[...] = high
        send_ref[...] = low


def unpack_kernel(count, mine_ref, other_ref, gram_ref, cross_ref):
    half = mine_ref.shape[1]
    row = lax.broadcasted_iota(jnp.int32, (half, half), 0)
    col = lax.broadcasted_iota(jnp.int32, (half, half), 1)

    def fill(low, high):
        mixed, corner = low[:half] / count, low[half : 2 * half] / count
        diagonal = low[2 * half : 2 * half + 1] / count
        flipped = mixed.T
        gram_ref[:half, :half] = jnp.where(row <= col, mixed, flipped)
        gram_ref[:half, half:] = corner
        gram_ref[half:, :half] = corner.T
        gram_ref[half:, half:] = jnp.where(row > col, mixed, jnp.where(row == col, diagonal, flipped))
        cross_ref[...] = high[: 2 * half] / count

    @pl.when(on_even_row())
    def _():
        fill(mine_ref, other_ref)

    @pl.when(jnp.logical_not(on_even_row()))
    def _():
        fill(other_ref, mine_ref)


def places(mesh_axes=("tm", "row")):
    blocks, rows = (lax.axis_size(axis) for axis in mesh_axes)
    return [(a, b) for a in range(blocks) for b in range(rows)]


def with_mate(value):
    return by_device(value, [((a, b), (a, b ^ 1)) for a, b in places()])


def pack_kernel(keep_ref, got_ref, scaled_ref):
    rows, lanes = keep_ref.shape
    value = keep_ref[...] + got_ref[...]
    most = jnp.max(jnp.max(jnp.abs(value), axis=0, keepdims=True), axis=1, keepdims=True)
    exponent = jnp.floor(jnp.log2(jnp.maximum(most, 1e-30))) - 12.0
    scaled_ref[:rows] = value * jnp.exp2(-exponent)
    scaled_ref[rows:] = jnp.broadcast_to(exponent, (HEAD // 2, lanes))


def power(exponent):
    return lax.reduce_precision(jnp.exp2(exponent), 8, 7)


def joined_messages(messages, last):
    rows = messages[0].shape[0] - HEAD // 2
    messages = [message.astype(F32) for message in messages]
    exponents = [message[rows : rows + 1] for message in messages]
    e = functools.reduce(jnp.maximum, exponents) + len(messages) // 2
    if last:
        terms = [message[:rows] * power(p) for message, p in zip(messages, exponents)]
    else:
        terms = [message * power(p - e) for message, p in zip(messages, exponents)]
    while len(terms) > 1:
        terms = [a + b for a, b in zip(terms[::2], terms[1::2])]
    if last:
        return terms[0]
    row = lax.broadcasted_iota(jnp.int32, terms[0].shape, 0)
    return jnp.where(row < rows, terms[0], e).astype(F16)


def total_over_chips(keep, got):
    blocks, rows = lax.axis_size("tm"), lax.axis_size("row")
    bits = [(0, 2**k) for k in range(1, rows.bit_length() - 1)]
    bits += [(2**k, 0) for k in range(blocks.bit_length() - 1)]
    rounds = []
    for i in range(0, len(bits), 2):
        flips = bits[i : i + 2]
        if len(flips) == 2:
            flips.append((flips[0][0] ^ flips[1][0], flips[0][1] ^ flips[1][1]))
        rounds.append(flips)
    size, lanes = keep.shape
    value = pl.pallas_call(
        pack_kernel,
        out_shape=jax.ShapeDtypeStruct((size + HEAD // 2, lanes), F32),
        in_specs=[WHOLE] * 2,
        out_specs=WHOLE,
        compiler_params=params(4),
    )(keep, got).astype(F16)
    for s, flips in enumerate(rounds):
        value = lax.optimization_barrier(value)
        other = rounds[s ^ 1] if s ^ 1 < len(rounds) and len(rounds[s ^ 1]) == len(flips) else flips
        messages = [value]
        for pair in zip(flips, other):
            moves = [((a, b), (a ^ pair[b % 2][0], b ^ pair[b % 2][1])) for a, b in places()]
            messages.append(by_device(value, moves))
        value = joined_messages(messages, s == len(rounds) - 1)
    return value


def on_device(latents, conv_weight, norm_gain, depth_target):
    frames, rows, cols, chans = latents.shape
    spots = frames * rows * cols
    bins = depth_target.shape[3]
    half = chans // 2
    blocks, bands = lax.axis_size("tm"), lax.axis_size("row")
    rim = jax.ShapeDtypeStruct((frames, cols, chans), BF16)
    edge, mid, to_mate, to_cross = pl.pallas_call(
        cut_kernel,
        out_shape=(
            jax.ShapeDtypeStruct((frames, 2, cols, chans), BF16),
            jax.ShapeDtypeStruct((frames, rows - 2, cols, chans), BF16),
            rim,
            rim,
        ),
        in_specs=[WHOLE],
        out_specs=(WHOLE,) * 4,
        compiler_params=params(4),
    )(latents)
    old_edge = later(edge)
    old_mid = later(mid)
    mate, cross = with_mate(to_mate), with_neighbour(to_cross)
    old_to_mate, old_to_cross = pl.pallas_call(
        pick_kernel,
        out_shape=(rim, rim),
        in_specs=[WHOLE],
        out_specs=(WHOLE,) * 2,
        compiler_params=params(4),
        cost_estimate=pl.CostEstimate(flops=4 * 10**9, bytes_accessed=2**20, transcendentals=0),
    )(old_edge)
    old_mate, old_cross = with_mate(old_to_mate), with_neighbour(old_to_cross)
    part = pl.pallas_call(
        own_kernel,
        out_shape=jax.ShapeDtypeStruct((spots, chans), F32),
        in_specs=[WHOLE] * 5,
        out_specs=WHOLE,
        compiler_params=params(24),
        cost_estimate=pl.CostEstimate(flops=spots * chans * chans * 27, bytes_accessed=5 * 2**20, transcendentals=0),
    )(edge, mid, mate, cross, conv_weight)
    features, keep, send = pl.pallas_call(
        rest_kernel,
        out_shape=(
            jax.ShapeDtypeStruct((spots, chans), BF16),
            jax.ShapeDtypeStruct((2 * half + HEAD // 2, half), F32),
            jax.ShapeDtypeStruct((2 * half + HEAD // 2, half), F32),
        ),
        in_specs=[WHOLE] * 10,
        out_specs=(WHOLE,) * 3,
        compiler_params=params(32),
        cost_estimate=pl.CostEstimate(flops=spots * chans * chans * 30, bytes_accessed=5 * 2**20, transcendentals=spots * chans),
    )(edge, mid, old_edge, old_mid, old_mate, old_cross, conv_weight, part,
      norm_gain.reshape(1, chans), depth_target.reshape(spots, bins))
    mine = total_over_chips(keep, with_mate(send))
    other = with_mate(mine)
    gram, cross = pl.pallas_call(
        functools.partial(unpack_kernel, spots * blocks * bands),
        out_shape=(jax.ShapeDtypeStruct((chans, chans), F32), jax.ShapeDtypeStruct((chans, bins), F32)),
        in_specs=[WHOLE] * 2,
        out_specs=(WHOLE,) * 2,
        compiler_params=params(4),
    )(mine, other)
    return features.reshape(latents.shape), gram, cross


def solution(mesh):
    in_specs = (P("tm", "row", None, None), P(), P(), P("tm", "row", None, None))
    out_specs = (P("tm", "row", None, None), P(), P())
    return jax.shard_map(
        on_device, mesh=mesh, in_specs=in_specs, out_specs=out_specs, check_vma=False
    )
```

time: 48.3 us -> 42.5 us (0.88)
  starting transfers between devices: 20.3 us -> 14.9 us
  waiting for transfers between devices: 16.8 us -> 18.5 us
  local copies, waits for them, and re-layouts: 1.99 us -> 1.04 us
  other arithmetic: 0.92 us -> 0.32 us
    ppermute x2, starting transfers between devices: 8.58 us -> 4.59 us  [later(): lax.ppermute(value, 'tm', [(i, (i + 1) % count) for i in range(count)])]
    ppermute x2, waiting for transfers between devices: 4.08 us -> 7.37 us  [later(): lax.ppermute(value, 'tm', [(i, (i + 1) % count) for i in range(count)])]
    slice x2 -> x0, local copies, waits for them, and re-layouts: 1.95 us -> none  [the longest x1 1 us: on_device(): mid = latents[:, 1:-1]]
    ppermute x8 -> x12, waiting for transfers between devices: 12.7 us -> 11.1 us  [by_device(): lax.ppermute(value, ('tm', 'row'), [(a * rows + b, c * rows + d) for (a,...]
    ppermute x8 -> x12, starting transfers between devices: 11.7 us -> 10.3 us  [by_device(): lax.ppermute(value, ('tm', 'row'), [(a * rows + b, c * rows + d) for (a,...]
    unnamed x6 -> x8, local copies, waits for them, and re-layouts: 0.02 us -> 1.04 us
    convert_element_type x11 -> x9, other arithmetic: 0.73 us -> 0.2 us  [the longest x1 0.11 us: joined_messages(): return jnp.where(row < rows, terms[0], e).astype(F16)]
  transfers between devices with their start and end apart: 10 -> 14, of which waited for: 8 -> 10; matrix products, arithmetic and copies ran while one was open for 0% -> 0% of each run, Pallas kernels for 4% -> 5%
where the time goes in v3:
time: 42.5 us; the launch traced here: 42.3 us
  waiting for transfers between devices  18.5 us (44%)
  starting transfers between devices  14.9 us (35%)
  Pallas kernels  6.73 us (16%)
  local copies, waits for them, and re-layouts  1.04 us (2%)
  between operations  0.86 us (2%)
    ppermute x12, waiting for transfers between devices, by_device(): lax.ppermute(value, ('tm', 'row'), [(a * rows + b, c * rows + d) for (a,...  11.1 us
    ppermute x12, starting transfers between devices, by_device(): lax.ppermute(value, ('tm', 'row'), [(a * rows + b, c * rows + d) for (a,...  10.3 us
    ppermute x2, waiting for transfers between devices, later(): lax.ppermute(value, 'tm', [(i, (i + 1) % count) for i in range(count)])  7.37 us
    ppermute x2, starting transfers between devices, later(): lax.ppermute(value, 'tm', [(i, (i + 1) % count) for i in range(count)])  4.59 us
    pallas_call x1, Pallas kernels, on_device(): pl.pallas_call(rest_kernel, out_shape=(jax.ShapeDtypeStruct((spots, chans...  3.76 us
    pallas_call x1, Pallas kernels, on_device(): pl.pallas_call(own_kernel, out_shape=jax.ShapeDtypeStruct((spots, chans),...  1.94 us
    unnamed x8, local copies, waits for them, and re-layouts  1.04 us
  transfers between devices with their start and end apart: 14, of which 10 were waited for; matrix products, arithmetic and copies ran while one was open for 0% of the time, Pallas kernels for 5%

profile of v3, /device:TPU:0, one launch (start us, length us, event | category | flops | bytes accessed | tf_op | source)
XLA Modules:
  0.0 42.3 jit_solution(17212571794261171706)
XLA Ops:
  0.6 0.0 copy-start
  0.6 1.0 %copy-done = bf16[2,6,80,256]{3,2,1,0:T(8,128)(2,1)S(1)} copy-done((bf16[2,6,80,256]{3,2,1,0:T(8,128)(2,1)S(1)}, bf16[2,6,80,256]{3,2,1,0:T(8,128)(2,1)}, u32[]{:S(2)}) %copy-start) | copy-done | bytes 491544
  1.7 3.0 %collective-permute-start = (bf16[2,2,80,256]{3,2,1,0:T(8,128)(2,1)S(1)}, bf16[2,2,80,256]{3,2,1,0:T(8,128)(2,1)S(1)}, u32[]{:S(2)}, u32[]{:S(2)}) collective-permute-start(bf16[2,2,80,256]{3,2,1,0:T(8,128)(2,1)S(1)} %get-tuple-element.14.edge_ref), channel_id=1, source_target_pairs={{0,4},{4,8},{8,12},{12,16},{16,20},{20,24},{24,28},{28,0},{1,5},{5... | collective-permute-start | bytes 491528 | tf_op jit(solution)/shard_map/ppermute | solution.py:32
  4.7 0.0 collective-permute-start.4
  4.7 0.7 %collective-permute-start.5 = (bf16[2,80,256]{2,1,0:T(8,128)(2,1)S(1)}, bf16[2,80,256]{2,1,0:T(8,128)(2,1)S(1)}, u32[]{:S(2)}, u32[]{:S(2)}) collective-permute-start(bf16[2,80,256]{2,1,0:T(8,128)(2,1)S(1)} %get-tuple-element.19), channel_id=1, source_target_pairs={{1,2},{2,1},{5,6},{6,5},{9,10},{10,9},{13,14},{14,13},{17,18},{18,... | collective-permute-start | bytes 245768 | tf_op jit(solution)/shard_map/ppermute | solution.py:27
  5.4 0.0 copy-start.1
  5.4 1.6 %collective-permute-start.1 = (bf16[2,4,80,256]{3,2,1,0:T(8,128)(2,1)S(1)}, bf16[2,4,80,256]{3,2,1,0:T(8,128)(2,1)S(1)}, u32[]{:S(2)}, u32[]{:S(2)}) collective-permute-start(bf16[2,4,80,256]{3,2,1,0:T(8,128)(2,1)S(1)} %get-tuple-element.15.mid_ref), channel_id=1, source_target_pairs={{0,4},{4,8},{8,12},{12,16},{16,20},{20,24},{24,28},{28,0},{1,5},{5... | collective-permute-start | bytes 983048 | tf_op jit(solution)/shard_map/ppermute | solution.py:32
  7.0 5.0 %collective-permute-done.edge_ref.old_edge_ref = bf16[2,2,80,256]{3,2,1,0:T(8,128)(2,1)S(1)} collective-permute-done((bf16[2,2,80,256]{3,2,1,0:T(8,128)(2,1)S(1)}, bf16[2,2,80,256]{3,2,1,0:T(8,128)(2,1)S(1)}, u32[]{:S(2)}, u32[]{:S(2)}) %collective-permute-start) | collective-permute-done | bytes 163872 | tf_op jit(solution)/shard_map/ppermute | solution.py:32
  12.0 0.0 copy-start.2
  12.0 0.0 copy-start.3
  12.0 0.1 collective-permute-start.2
  12.1 0.8 %collective-permute-start.3 = (bf16[2,80,256]{2,1,0:T(8,128)(2,1)S(1)}, bf16[2,80,256]{2,1,0:T(8,128)(2,1)S(1)}, u32[]{:S(2)}, u32[]{:S(2)}) collective-permute-start(bf16[2,80,256]{2,1,0:T(8,128)(2,1)S(1)} %get-tuple-element.17), channel_id=1, source_target_pairs={{1,2},{2,1},{5,6},{6,5},{9,10},{10,9},{13,14},{14,13},{17,18},{18,... | collective-permute-start | bytes 245768 | tf_op jit(solution)/shard_map/ppermute | solution.py:27
  12.9 0.0 collective-permute-done.4.mate_ref
  12.9 0.0 collective-permute-done.5.cross_ref
  12.9 0.0 copy-done.1
  12.9 1.9 %shard_map.69.part_ref = f32[960,256]{1,0:T(8,128)S(1)} custom-call(bf16[2,2,80,256]{3,2,1,0:T(8,128)(2,1)S(1)} %get-tuple-element.14.edge_ref, bf16[2,4,80,256]{3,2,1,0:T(8,128)(2,1)S(1)} %get-tuple-element.15.mid_ref, bf16[2,80,256]{2,1,0:T(8,128)(2,1)S(1)} %collective-permute-done.4.mate_ref, bf16[2,80,256]{2,1,0:T(8,128)(2,1)S(1)} %collective-permute-done.5.cross_ref, ...), custom_call_target="tpu_custom_call" | custom-call | flops 1698693120 | bytes 5242880 | tf_op jit(solution)/shard_map/pallas_call | solution.py:275
  14.9 0.0 collective-permute-done.2.mate_ref
  14.9 0.0 collective-permute-done.3.cross_ref
  14.9 2.4 %collective-permute-done.1.old_mid_ref = bf16[2,4,80,256]{3,2,1,0:T(8,128)(2,1)S(1)} collective-permute-done((bf16[2,4,80,256]{3,2,1,0:T(8,128)(2,1)S(1)}, bf16[2,4,80,256]{3,2,1,0:T(8,128)(2,1)S(1)}, u32[]{:S(2)}, u32[]{:S(2)}) %collective-permute-start.1) | collective-permute-done | bytes 327712 | tf_op jit(solution)/shard_map/ppermute | solution.py:32
  17.3 0.0 copy-done.2
  17.3 0.0 copy-done.3
  17.3 3.8 %shard_map.70 = (bf16[960,256]{1,0:T(8,128)(2,1)}, f32[264,128]{1,0:T(8,128)S(1)}, f32[264,128]{1,0:T(8,128)S(1)}) custom-call(bf16[2,2,80,256]{3,2,1,0:T(8,128)(2,1)S(1)} %get-tuple-element.14.edge_ref, bf16[2,4,80,256]{3,2,1,0:T(8,128)(2,1)S(1)} %get-tuple-element.15.mid_ref, bf16[2,2,80,256]{3,2,1,0:T(8,128)(2,1)S(1)} %collective-permute-done.edge_ref.old_edge_ref, ...), custom_call_target="tpu_custom_call" | custom-call | flops 1887436800 | bytes 5242880 | tf_op jit(solution)/shard_map/pallas_call | solution.py:283
  21.1 1.5 %collective-permute-start.6 = (f32[264,128]{1,0:T(8,128)S(1)}, f32[264,128]{1,0:T(8,128)S(1)}, u32[]{:S(2)}, u32[]{:S(2)}) collective-permute-start(f32[264,128]{1,0:T(8,128)S(1)} %get-tuple-element.22), channel_id=1, source_target_pairs={{0,1},{1,0},{2,3},{3,2},{4,5},{5,4},{6,7},{7,6},{8,9},{9,8},{10,11... | collective-permute-start | bytes 405512 | tf_op jit(solution)/shard_map/ppermute | solution.py:27
  22.6 1.0 %collective-permute-done.6.got_ref = f32[264,128]{1,0:T(8,128)S(1)} collective-permute-done((f32[264,128]{1,0:T(8,128)S(1)}, f32[264,128]{1,0:T(8,128)S(1)}, u32[]{:S(2)}, u32[]{:S(2)}) %collective-permute-start.6) | collective-permute-done | bytes 135200 | tf_op jit(solution)/shard_map/ppermute | solution.py:27
  23.6 0.1 shard_map.71
  23.7 2.1 %collective-permute-start.7 = (f16[272,128]{1,0:T(8,128)(2,1)S(1)}, f16[272,128]{1,0:T(8,128)(2,1)S(1)}, u32[]{:S(2)}, u32[]{:S(2)}) collective-permute-start(f16[272,128]{1,0:T(8,128)(2,1)S(1)} %convert_element_type.30), channel_id=1, source_target_pairs={{0,2},{1,9},{2,0},{3,11},{4,6},{5,13},{6,4},{7,15},{8,10},{9,1},{1... | collective-permute-start | bytes 208904 | tf_op jit(solution)/shard_map/ppermute | solution.py:27
  25.8 0.0 collective-permute-start.8
  25.8 1.5 %collective-permute-start.9 = (f16[272,128]{1,0:T(8,128)(2,1)S(1)}, f16[272,128]{1,0:T(8,128)(2,1)S(1)}, u32[]{:S(2)}, u32[]{:S(2)}) collective-permute-start(f16[272,128]{1,0:T(8,128)(2,1)S(1)} %convert_element_type.30), channel_id=1, source_target_pairs={{0,6},{1,25},{2,4},{3,27},{4,2},{5,29},{6,0},{7,31},{8,14},{9,17},... | collective-permute-start | bytes 208904 | tf_op jit(solution)/shard_map/ppermute | solution.py:27
  27.4 0.7 %collective-permute-done.7 = f16[272,128]{1,0:T(8,128)(2,1)S(1)} collective-permute-done((f16[272,128]{1,0:T(8,128)(2,1)S(1)}, f16[272,128]{1,0:T(8,128)(2,1)S(1)}, u32[]{:S(2)}, u32[]{:S(2)}) %collective-permute-start.7) | collective-permute-done | bytes 69664 | tf_op jit(solution)/shard_map/ppermute | solution.py:27
  28.1 2.0 %collective-permute-done.8 = f16[272,128]{1,0:T(8,128)(2,1)S(1)} collective-permute-done((f16[272,128]{1,0:T(8,128)(2,1)S(1)}, f16[272,128]{1,0:T(8,128)(2,1)S(1)}, u32[]{:S(2)}, u32[]{:S(2)}) %collective-permute-start.8) | collective-permute-done | bytes 69664 | tf_op jit(solution)/shard_map/ppermute | solution.py:27
  30.1 0.9 %collective-permute-done.9 = f16[272,128]{1,0:T(8,128)(2,1)S(1)} collective-permute-done((f16[272,128]{1,0:T(8,128)(2,1)S(1)}, f16[272,128]{1,0:T(8,128)(2,1)S(1)}, u32[]{:S(2)}, u32[]{:S(2)}) %collective-permute-start.9) | collective-permute-done | bytes 69664 | tf_op jit(solution)/shard_map/ppermute | solution.py:27
  31.1 0.1 select_convert_fusion
  31.2 0.3 collective-permute-start.10
  31.5 2.5 %collective-permute-start.12 = (f16[272,128]{1,0:T(8,128)(2,1)S(1)}, f16[272,128]{1,0:T(8,128)(2,1)S(1)}, u32[]{:S(2)}, u32[]{:S(2)}) collective-permute-start(f16[272,128]{1,0:T(8,128)(2,1)S(1)} %select_convert_fusion), channel_id=1, source_target_pairs={{0,24},{1,7},{2,26},{3,5},{4,28},{5,3},{6,30},{7,1},{8,16},{9,15},... | collective-permute-start | bytes 208904 | tf_op jit(solution)/shard_map/ppermute | solution.py:27
  34.0 0.7 %collective-permute-start.11 = (f16[272,128]{1,0:T(8,128)(2,1)S(1)}, f16[272,128]{1,0:T(8,128)(2,1)S(1)}, u32[]{:S(2)}, u32[]{:S(2)}) collective-permute-start(f16[272,128]{1,0:T(8,128)(2,1)S(1)} %select_convert_fusion), channel_id=1, source_target_pairs={{0,16},{1,5},{2,18},{3,7},{4,20},{5,1},{6,22},{7,3},{8,24},{9,13},... | collective-permute-start | bytes 208904 | tf_op jit(solution)/shard_map/ppermute | solution.py:27
  34.8 0.8 %collective-permute-done.10 = f16[272,128]{1,0:T(8,128)(2,1)S(1)} collective-permute-done((f16[272,128]{1,0:T(8,128)(2,1)S(1)}, f16[272,128]{1,0:T(8,128)(2,1)S(1)}, u32[]{:S(2)}, u32[]{:S(2)}) %collective-permute-start.10) | collective-permute-done | bytes 69664 | tf_op jit(solution)/shard_map/ppermute | solution.py:27
  35.6 2.2 %collective-permute-done.12 = f16[272,128]{1,0:T(8,128)(2,1)S(1)} collective-permute-done((f16[272,128]{1,0:T(8,128)(2,1)S(1)}, f16[272,128]{1,0:T(8,128)(2,1)S(1)}, u32[]{:S(2)}, u32[]{:S(2)}) %collective-permute-start.12) | collective-permute-done | bytes 69664 | tf_op jit(solution)/shard_map/ppermute | solution.py:27
  37.8 2.2 %collective-permute-done.11 = f16[272,128]{1,0:T(8,128)(2,1)S(1)} collective-permute-done((f16[272,128]{1,0:T(8,128)(2,1)S(1)}, f16[272,128]{1,0:T(8,128)(2,1)S(1)}, u32[]{:S(2)}, u32[]{:S(2)}) %collective-permute-start.11) | collective-permute-done | bytes 69664 | tf_op jit(solution)/shard_map/ppermute | solution.py:27
  40.0 0.1 collective-permute-start.13
  40.1 1.3 %collective-permute-done.13.other_ref = f32[264,128]{1,0:T(8,128)S(1)} collective-permute-done((f32[264,128]{1,0:T(8,128)S(1)}, f32[264,128]{1,0:T(8,128)S(1)}, u32[]{:S(2)}, u32[]{:S(2)}) %collective-permute-start.13) | collective-permute-done | bytes 135200 | tf_op jit(solution)/shard_map/ppermute | solution.py:27
  41.5 0.8 %shard_map.72 = (f32[256,256]{1,0:T(8,128)}, f32[256,128]{1,0:T(8,128)}) custom-call(f32[264,128]{1,0:T(8,128)S(1)} %fusion.1.mine_ref, f32[264,128]{1,0:T(8,128)S(1)} %collective-permute-done.13.other_ref), custom_call_target="tpu_custom_call" | custom-call | tf_op jit(solution)/shard_map/pallas_call | solution.py:298
  (19 shorter events, 0.3 us)
Async XLA Ops:
  0.6 1.0 %copy-start = (bf16[2,6,80,256]{3,2,1,0:T(8,128)(2,1)S(1)}, bf16[2,6,80,256]{3,2,1,0:T(8,128)(2,1)}, u32[]{:S(2)}) copy-start(bf16[2,6,80,256]{3,2,1,0:T(8,128)(2,1)} %latents_ref.1) | copy-start | bytes 1474564
  1.7 10.3 %collective-permute-start = (bf16[2,2,80,256]{3,2,1,0:T(8,128)(2,1)S(1)}, bf16[2,2,80,256]{3,2,1,0:T(8,128)(2,1)S(1)}, u32[]{:S(2)}, u32[]{:S(2)}) collective-permute-start(bf16[2,2,80,256]{3,2,1,0:T(8,128)(2,1)S(1)} %get-tuple-element.14.edge_ref), channel_id=1, source_target_pairs={{0,4},{4,8},{8,12},{12,16},{16,20},{20,24},{24,28},{28,0},{1,5},{5... | collective-permute-start | bytes 491528 | tf_op jit(solution)/shard_map/ppermute | solution.py:32
  4.7 8.2 %collective-permute-start.4 = (bf16[2,80,256]{2,1,0:T(8,128)(2,1)S(1)}, bf16[2,80,256]{2,1,0:T(8,128)(2,1)S(1)}, u32[]{:S(2)}, u32[]{:S(2)}) collective-permute-start(bf16[2,80,256]{2,1,0:T(8,128)(2,1)S(1)} %get-tuple-element.18), channel_id=1, source_target_pairs={{0,1},{1,0},{2,3},{3,2},{4,5},{5,4},{6,7},{7,6},{8,9},{9,8},{10,11... | collective-permute-start | bytes 245768 | tf_op jit(solution)/shard_map/ppermute | solution.py:27
  4.7 8.2 %collective-permute-start.5 = (bf16[2,80,256]{2,1,0:T(8,128)(2,1)S(1)}, bf16[2,80,256]{2,1,0:T(8,128)(2,1)S(1)}, u32[]{:S(2)}, u32[]{:S(2)}) collective-permute-start(bf16[2,80,256]{2,1,0:T(8,128)(2,1)S(1)} %get-tuple-element.19), channel_id=1, source_target_pairs={{1,2},{2,1},{5,6},{6,5},{9,10},{10,9},{13,14},{14,13},{17,18},{18,... | collective-permute-start | bytes 245768 | tf_op jit(solution)/shard_map/ppermute | solution.py:27
  5.4 7.5 %copy-start.1 = (bf16[3,3,768,256]{3,2,1,0:T(8,128)(2,1)S(1)}, bf16[3,3,768,256]{3,2,1,0:T(8,128)(2,1)}, u32[]{:S(2)}) copy-start(bf16[3,3,768,256]{3,2,1,0:T(8,128)(2,1)} %weight_ref.3) | copy-start | bytes 10616836
  5.4 11.9 %collective-permute-start.1 = (bf16[2,4,80,256]{3,2,1,0:T(8,128)(2,1)S(1)}, bf16[2,4,80,256]{3,2,1,0:T(8,128)(2,1)S(1)}, u32[]{:S(2)}, u32[]{:S(2)}) collective-permute-start(bf16[2,4,80,256]{3,2,1,0:T(8,128)(2,1)S(1)} %get-tuple-element.15.mid_ref), channel_id=1, source_target_pairs={{0,4},{4,8},{8,12},{12,16},{16,20},{20,24},{24,28},{28,0},{1,5},{5... | collective-permute-start | bytes 983048 | tf_op jit(solution)/shard_map/ppermute | solution.py:32
  12.0 5.3 %copy-start.2 = (bf16[2,6,80,128]{3,2,1,0:T(8,128)(2,1)S(1)}, bf16[2,6,80,128]{3,2,1,0:T(8,128)(2,1)}, u32[]{:S(2)}) copy-start(bf16[2,6,80,128]{3,2,1,0:T(8,128)(2,1)} %param.7) | copy-start | bytes 737284
  12.0 5.3 %copy-start.3 = (f32[256]{0:T(256)S(1)}, f32[256]{0:T(256)}, u32[]{:S(2)}) copy-start(f32[256]{0:T(256)} %param.6) | copy-start | bytes 3076
  12.0 2.9 %collective-permute-start.2 = (bf16[2,80,256]{2,1,0:T(8,128)(2,1)S(1)}, bf16[2,80,256]{2,1,0:T(8,128)(2,1)S(1)}, u32[]{:S(2)}, u32[]{:S(2)}) collective-permute-start(bf16[2,80,256]{2,1,0:T(8,128)(2,1)S(1)} %get-tuple-element.16), channel_id=1, source_target_pairs={{0,1},{1,0},{2,3},{3,2},{4,5},{5,4},{6,7},{7,6},{8,9},{9,8},{10,11... | collective-permute-start | bytes 245768 | tf_op jit(solution)/shard_map/ppermute | solution.py:27
  12.1 2.8 %collective-permute-start.3 = (bf16[2,80,256]{2,1,0:T(8,128)(2,1)S(1)}, bf16[2,80,256]{2,1,0:T(8,128)(2,1)S(1)}, u32[]{:S(2)}, u32[]{:S(2)}) collective-permute-start(bf16[2,80,256]{2,1,0:T(8,128)(2,1)S(1)} %get-tuple-element.17), channel_id=1, source_target_pairs={{1,2},{2,1},{5,6},{6,5},{9,10},{10,9},{13,14},{14,13},{17,18},{18,... | collective-permute-start | bytes 245768 | tf_op jit(solution)/shard_map/ppermute | solution.py:27
  21.1 2.5 %collective-permute-start.6 = (f32[264,128]{1,0:T(8,128)S(1)}, f32[264,128]{1,0:T(8,128)S(1)}, u32[]{:S(2)}, u32[]{:S(2)}) collective-permute-start(f32[264,128]{1,0:T(8,128)S(1)} %get-tuple-element.22), channel_id=1, source_target_pairs={{0,1},{1,0},{2,3},{3,2},{4,5},{5,4},{6,7},{7,6},{8,9},{9,8},{10,11... | collective-permute-start | bytes 405512 | tf_op jit(solution)/shard_map/ppermute | solution.py:27
  23.7 4.4 %collective-permute-start.7 = (f16[272,128]{1,0:T(8,128)(2,1)S(1)}, f16[272,128]{1,0:T(8,128)(2,1)S(1)}, u32[]{:S(2)}, u32[]{:S(2)}) collective-permute-start(f16[272,128]{1,0:T(8,128)(2,1)S(1)} %convert_element_type.30), channel_id=1, source_target_pairs={{0,2},{1,9},{2,0},{3,11},{4,6},{5,13},{6,4},{7,15},{8,10},{9,1},{1... | collective-permute-start | bytes 208904 | tf_op jit(solution)/shard_map/ppermute | solution.py:27
  25.8 4.3 %collective-permute-start.8 = (f16[272,128]{1,0:T(8,128)(2,1)S(1)}, f16[272,128]{1,0:T(8,128)(2,1)S(1)}, u32[]{:S(2)}, u32[]{:S(2)}) collective-permute-start(f16[272,128]{1,0:T(8,128)(2,1)S(1)} %convert_element_type.30), channel_id=1, source_target_pairs={{0,4},{1,17},{2,6},{3,19},{4,0},{5,21},{6,2},{7,23},{8,12},{9,25},... | collective-permute-start | bytes 208904 | tf_op jit(solution)/shard_map/ppermute | solution.py:27
  25.8 5.2 %collective-permute-start.9 = (f16[272,128]{1,0:T(8,128)(2,1)S(1)}, f16[272,128]{1,0:T(8,128)(2,1)S(1)}, u32[]{:S(2)}, u32[]{:S(2)}) collective-permute-start(f16[272,128]{1,0:T(8,128)(2,1)S(1)} %convert_element_type.30), channel_id=1, source_target_pairs={{0,6},{1,25},{2,4},{3,27},{4,2},{5,29},{6,0},{7,31},{8,14},{9,17},... | collective-permute-start | bytes 208904 | tf_op jit(solution)/shard_map/ppermute | solution.py:27
  31.2 4.4 %collective-permute-start.10 = (f16[272,128]{1,0:T(8,128)(2,1)S(1)}, f16[272,128]{1,0:T(8,128)(2,1)S(1)}, u32[]{:S(2)}, u32[]{:S(2)}) collective-permute-start(f16[272,128]{1,0:T(8,128)(2,1)S(1)} %select_convert_fusion), channel_id=1, source_target_pairs={{0,8},{1,3},{2,10},{3,1},{4,12},{5,7},{6,14},{7,5},{8,0},{9,11},{1... | collective-permute-start | bytes 208904 | tf_op jit(solution)/shard_map/ppermute | solution.py:27
  31.5 6.2 %collective-permute-start.12 = (f16[272,128]{1,0:T(8,128)(2,1)S(1)}, f16[272,128]{1,0:T(8,128)(2,1)S(1)}, u32[]{:S(2)}, u32[]{:S(2)}) collective-permute-start(f16[272,128]{1,0:T(8,128)(2,1)S(1)} %select_convert_fusion), channel_id=1, source_target_pairs={{0,24},{1,7},{2,26},{3,5},{4,28},{5,3},{6,30},{7,1},{8,16},{9,15},... | collective-permute-start | bytes 208904 | tf_op jit(solution)/shard_map/ppermute | solution.py:27
  34.0 6.0 %collective-permute-start.11 = (f16[272,128]{1,0:T(8,128)(2,1)S(1)}, f16[272,128]{1,0:T(8,128)(2,1)S(1)}, u32[]{:S(2)}, u32[]{:S(2)}) collective-permute-start(f16[272,128]{1,0:T(8,128)(2,1)S(1)} %select_convert_fusion), channel_id=1, source_target_pairs={{0,16},{1,5},{2,18},{3,7},{4,20},{5,1},{6,22},{7,3},{8,24},{9,13},... | collective-permute-start | bytes 208904 | tf_op jit(solution)/shard_map/ppermute | solution.py:27
  40.0 1.4 %collective-permute-start.13 = (f32[264,128]{1,0:T(8,128)S(1)}, f32[264,128]{1,0:T(8,128)S(1)}, u32[]{:S(2)}, u32[]{:S(2)}) collective-permute-start(f32[264,128]{1,0:T(8,128)S(1)} %fusion.1.mine_ref), channel_id=1, source_target_pairs={{0,1},{1,0},{2,3},{3,2},{4,5},{5,4},{6,7},{7,6},{8,9},{9,8},{10,11... | collective-permute-start | bytes 405512 | tf_op jit(solution)/shard_map/ppermute | solution.py:27

commit v4 on v3

--- a/solution.py
+++ b/solution.py
@@ -12,6 +12,7 @@
 F16 = jnp.float16
 HEAD = 16
 WHOLE = pl.BlockSpec(memory_space=pltpu.VMEM)
+ANY = pl.BlockSpec(memory_space=pl.ANY)
 
 
 def params(mebibytes):
@@ -20,6 +21,16 @@
 
 def on_even_row():
     return lax.axis_index("row") % 2 == 0
+
+
+def odd_bits(value):
+    for shift in (8, 4, 2, 1):
+        value = value ^ (value >> shift)
+    return value & 1
+
+
+def has_low():
+    return odd_bits(lax.axis_index("tm") ^ lax.axis_index("row")) == 0
 
 
 def by_device(value, moves):
@@ -32,11 +43,12 @@
     return lax.ppermute(value, "tm", [(i, (i + 1) % count) for i in range(count)])
 
 
-def cut_kernel(latents_ref, edge_ref, mid_ref, mate_ref, cross_ref):
+def cut_kernel(latents_ref, edge_ref, early_ref, late_ref, mate_ref, cross_ref):
     last = latents_ref.shape[1] - 1
     edge_ref[:, 0] = latents_ref[:, 0]
     edge_ref[:, 1] = latents_ref[:, last]
-    mid_ref[...] = latents_ref[:, 1:last]
+    early_ref[...] = latents_ref[0, 1:last]
+    late_ref[...] = latents_ref[1, 1:last]
     pick_kernel(edge_ref, mate_ref, cross_ref)
 
 
@@ -56,18 +68,21 @@
 
 def with_neighbour(value):
     bands = lax.axis_size("row")
-    return by_device(value, [((a, b), (a, ((b + 1) ^ 1) - 1)) for a, b in places() if 0 < b < bands - 1])
+    return by_device(value, [((a, b), (a, (((b + 1) ^ 1) - 1) % bands)) for a, b in places()])
 
 
 def rims(mate_ref, cross_ref, f):
     even = on_even_row()
+    band = lax.axis_index("row")
+    at_end = (band == 0) | (band == lax.axis_size("row") - 1)
     mate, cross = mate_ref[f], cross_ref[f]
+    cross = jnp.where(at_end, jnp.zeros_like(cross), cross)
     return jnp.where(even, cross, mate), jnp.where(even, mate, cross)
 
 
-def frame_rows(edge_ref, mid_ref, f):
-    rows, cols, chans = mid_ref.shape[1:]
-    return [edge_ref[f, 0], mid_ref[f].reshape(rows * cols, chans), edge_ref[f, 1]]
+def frame_rows(edge_ref, middle_ref, f):
+    rows, cols, chans = middle_ref.shape
+    return [edge_ref[f, 0], middle_ref[...].reshape(rows * cols, chans), edge_ref[f, 1]]
 
 
 def column_taps(stacks, weight_ref, times, chans):
@@ -94,42 +109,63 @@
     return left + middle + right
 
 
-def padded_stacks(edge_ref, mid_ref, mate_ref, cross_ref):
-    cols = edge_ref.shape[2]
-    stacks = []
-    for f in range(2):
-        above, below = rims(mate_ref, cross_ref, f)
-        stacks.append(stacked_rows([above, *frame_rows(edge_ref, mid_ref, f), below], cols))
-    return stacks
-
-
-def own_kernel(edge_ref, mid_ref, mate_ref, cross_ref, weight_ref, part_ref):
+def padded_stack(edge_ref, middle_ref, mate_ref, cross_ref, f):
+    above, below = rims(mate_ref, cross_ref, f)
+    return stacked_rows([above, *frame_rows(edge_ref, middle_ref, f), below], edge_ref.shape[2])
+
+
+def own_kernel(edge_ref, early_ref, late_ref, mate_ref, cross_ref, weight_ref, part_ref):
     cols, chans = edge_ref.shape[2:]
     span = part_ref.shape[0] // 2
-    stacks = padded_stacks(edge_ref, mid_ref, mate_ref, cross_ref)
-    part_ref[:span] = joined_columns(column_taps(stacks[:1], weight_ref, [2], chans), cols)
-    part_ref[span:] = joined_columns(column_taps(stacks, weight_ref, [1, 2], chans), cols)
-
-
-def rest_kernel(edge_ref, mid_ref, old_edge_ref, old_mid_ref, mate_ref, cross_ref, weight_ref, part_ref,
-                gain_ref, target_ref, feature_ref, keep_ref, send_ref):
+    early = padded_stack(edge_ref, early_ref, mate_ref, cross_ref, 0)
+    late = padded_stack(edge_ref, late_ref, mate_ref, cross_ref, 1)
+    part_ref[:span] = joined_columns(column_taps([early], weight_ref, [2], chans), cols)
+    part_ref[span:] = joined_columns(column_taps([early, late], weight_ref, [1, 2], chans), cols)
+
+
+def older_terms(stack, weight_ref, time, cols, chans):
+    terms = joined_columns(column_taps([stack], weight_ref, [time], chans), cols)
+    return jnp.where(lax.axis_index("tm") == 0, 0.0, terms)
+
+
+def features_of(conv, own_rows, gain_ref):
+    mean = jnp.mean(conv * conv, axis=1, keepdims=True)
+    normed = conv * lax.rsqrt(mean + 1e-06) * gain_ref[...]
+    silu = 0.5 * normed * (1.0 + jnp.tanh(0.5 * normed))
+    return (jnp.concatenate(own_rows, axis=0).astype(F32) + silu).astype(BF16)
+
+
+def moments(features, targets):
+    both = jnp.concatenate([features, targets], axis=1)
+    return jnp.dot(features.T, both, preferred_element_type=F32)
+
+
+def late_kernel(edge_ref, late_ref, old_edge_ref, old_late_ref, mate_ref, cross_ref, weight_ref, part_ref, gain_ref,
+                target_ref, feature_ref, more_ref, sums_ref, stage, sem):
     cols, chans = edge_ref.shape[2:]
-    span, half = part_ref.shape[0] // 2, chans // 2
-    stacks = padded_stacks(old_edge_ref, old_mid_ref, mate_ref, cross_ref)
-    sums = jnp.zeros((chans, chans + target_ref.shape[1]), F32)
-    for f in (1, 0):
-        here = slice(f * span, (f + 1) * span)
-        times = [0, 1] if f == 0 else [0]
-        older = joined_columns(column_taps(stacks[f:], weight_ref, times, chans), cols)
-        conv = part_ref[here] + jnp.where(lax.axis_index("tm") == 0, 0.0, older)
-        mean = jnp.mean(conv * conv, axis=1, keepdims=True)
-        normed = conv * lax.rsqrt(mean + 1e-06) * gain_ref[...]
-        silu = 0.5 * normed * (1.0 + jnp.tanh(0.5 * normed))
-        mine = jnp.concatenate(frame_rows(edge_ref, mid_ref, f), axis=0).astype(F32)
-        features = (mine + silu).astype(BF16)
-        feature_ref[here] = features
-        both = jnp.concatenate([features, target_ref[here]], axis=1)
-        sums = sums + jnp.dot(features.T, both, preferred_element_type=F32)
+    span = part_ref.shape[0] // 2
+    stack = padded_stack(old_edge_ref, old_late_ref, mate_ref, cross_ref, 1)
+    conv = part_ref[span:] + older_terms(stack, weight_ref, 0, cols, chans)
+    features = features_of(conv, frame_rows(edge_ref, late_ref, 1), gain_ref)
+    stage[...] = features
+    copy = pltpu.make_async_copy(stage, feature_ref.at[pl.ds(span, span)], sem)
+    copy.start()
+    more_ref[...] = part_ref[:span] + older_terms(stack, weight_ref, 1, cols, chans)
+    sums_ref[...] = moments(features, target_ref[span:])
+    copy.wait()
+
+
+def early_kernel(edge_ref, early_ref, old_edge_ref, old_early_ref, mate_ref, cross_ref, weight_ref, more_ref, sums_ref,
+                 gain_ref, target_ref, late_feature_ref, feature_ref, keep_ref, send_ref, stage, sem):
+    cols, chans = edge_ref.shape[2:]
+    span, half = more_ref.shape[0], chans // 2
+    stack = padded_stack(old_edge_ref, old_early_ref, mate_ref, cross_ref, 0)
+    conv = more_ref[...] + older_terms(stack, weight_ref, 0, cols, chans)
+    features = features_of(conv, frame_rows(edge_ref, early_ref, 0), gain_ref)
+    stage[...] = features
+    copy = pltpu.make_async_copy(stage, feature_ref.at[pl.ds(0, span)], sem)
+    copy.start()
+    sums = sums_ref[...] + moments(features, target_ref[:span])
     row = lax.broadcasted_iota(jnp.int32, (half, half), 0)
     col = lax.broadcasted_iota(jnp.int32, (half, half), 1)
     head, tail = sums[:half, :half], sums[half:, half:chans]
@@ -138,15 +174,17 @@
     low = jnp.concatenate([jnp.where(row <= col, head, tail), sums[:half, half:chans], extra], axis=0)
     high = jnp.concatenate([sums[:half, chans:], sums[half:, chans:], jnp.zeros_like(extra)], axis=0)
 
-    @pl.when(on_even_row())
+    @pl.when(has_low())
     def _():
         keep_ref[...] = low
         send_ref[...] = high
 
-    @pl.when(jnp.logical_not(on_even_row()))
+    @pl.when(jnp.logical_not(has_low()))
     def _():
         keep_ref[...] = high
         send_ref[...] = low
+
+    copy.wait()
 
 
 def unpack_kernel(count, mine_ref, other_ref, gram_ref, cross_ref):
@@ -164,11 +202,11 @@
         gram_ref[half:, half:] = jnp.where(row > col, mixed, jnp.where(row == col, diagonal, flipped))
         cross_ref[...] = high[: 2 * half] / count
 
-    @pl.when(on_even_row())
+    @pl.when(has_low())
     def _():
         fill(mine_ref, other_ref)
 
-    @pl.when(jnp.logical_not(on_even_row()))
+    @pl.when(jnp.logical_not(has_low()))
     def _():
         fill(other_ref, mine_ref)
 
@@ -235,7 +273,10 @@
         other = rounds[s ^ 1] if s ^ 1 < len(rounds) and len(rounds[s ^ 1]) == len(flips) else flips
         messages = [value]
         for pair in zip(flips, other):
-            moves = [((a, b), (a ^ pair[b % 2][0], b ^ pair[b % 2][1])) for a, b in places()]
+            moves = []
+            for a, b in places():
+                c, d = pair[odd_bits(a ^ b)]
+                moves.append(((a, b), (a ^ c, b ^ d ^ odd_bits(c ^ d))))
             messages.append(by_device(value, moves))
         value = joined_messages(messages, s == len(rounds) - 1)
     return value
@@ -248,20 +289,15 @@
     half = chans // 2
     blocks, bands = lax.axis_size("tm"), lax.axis_size("row")
     rim = jax.ShapeDtypeStruct((frames, cols, chans), BF16)
-    edge, mid, to_mate, to_cross = pl.pallas_call(
+    middle = jax.ShapeDtypeStruct((rows - 2, cols, chans), BF16)
+    edge, early, late, to_mate, to_cross = pl.pallas_call(
         cut_kernel,
-        out_shape=(
-            jax.ShapeDtypeStruct((frames, 2, cols, chans), BF16),
-            jax.ShapeDtypeStruct((frames, rows - 2, cols, chans), BF16),
-            rim,
-            rim,
-        ),
+        out_shape=(jax.ShapeDtypeStruct((frames, 2, cols, chans), BF16), middle, middle, rim, rim),
         in_specs=[WHOLE],
-        out_specs=(WHOLE,) * 4,
+        out_specs=(WHOLE,) * 5,
         compiler_params=params(4),
     )(latents)
-    old_edge = later(edge)
-    old_mid = later(mid)
+    old_edge, old_late, old_early = later(edge), later(late), later(early)
     mate, cross = with_mate(to_mate), with_neighbour(to_cross)
     old_to_mate, old_to_cross = pl.pallas_call(
         pick_kernel,
@@ -269,30 +305,44 @@
         in_specs=[WHOLE],
         out_specs=(WHOLE,) * 2,
         compiler_params=params(4),
-        cost_estimate=pl.CostEstimate(flops=4 * 10**9, bytes_accessed=2**20, transcendentals=0),
+        cost_estimate=pl.CostEstimate(flops=2 * 10**9, bytes_accessed=2**20, transcendentals=0),
     )(old_edge)
     old_mate, old_cross = with_mate(old_to_mate), with_neighbour(old_to_cross)
     part = pl.pallas_call(
         own_kernel,
         out_shape=jax.ShapeDtypeStruct((spots, chans), F32),
-        in_specs=[WHOLE] * 5,
+        in_specs=[WHOLE] * 6,
         out_specs=WHOLE,
         compiler_params=params(24),
         cost_estimate=pl.CostEstimate(flops=spots * chans * chans * 27, bytes_accessed=5 * 2**20, transcendentals=0),
-    )(edge, mid, mate, cross, conv_weight)
-    features, keep, send = pl.pallas_call(
-        rest_kernel,
+    )(edge, early, late, mate, cross, conv_weight)
+    gain, targets = norm_gain.reshape(1, chans), depth_target.reshape(spots, bins)
+    half_features = jax.ShapeDtypeStruct((spots, chans), BF16)
+    staging = [pltpu.VMEM((spots // 2, chans), BF16), pltpu.SemaphoreType.DMA]
+    features, more, sums = pl.pallas_call(
+        late_kernel,
         out_shape=(
-            jax.ShapeDtypeStruct((spots, chans), BF16),
-            jax.ShapeDtypeStruct((2 * half + HEAD // 2, half), F32),
-            jax.ShapeDtypeStruct((2 * half + HEAD // 2, half), F32),
+            half_features,
+            jax.ShapeDtypeStruct((spots // 2, chans), F32),
+            jax.ShapeDtypeStruct((chans, chans + bins), F32),
         ),
         in_specs=[WHOLE] * 10,
-        out_specs=(WHOLE,) * 3,
-        compiler_params=params(32),
-        cost_estimate=pl.CostEstimate(flops=spots * chans * chans * 30, bytes_accessed=5 * 2**20, transcendentals=spots * chans),
-    )(edge, mid, old_edge, old_mid, old_mate, old_cross, conv_weight, part,
-      norm_gain.reshape(1, chans), depth_target.reshape(spots, bins))
+        out_specs=(ANY, WHOLE, WHOLE),
+        scratch_shapes=staging,
+        compiler_params=params(24),
+        cost_estimate=pl.CostEstimate(flops=spots * chans * chans * 20, bytes_accessed=5 * 2**20, transcendentals=spots * chans // 2),
+    )(edge, late, old_edge, old_late, old_mate, old_cross, conv_weight, part, gain, targets)
+    share = jax.ShapeDtypeStruct((2 * half + HEAD // 2, half), F32)
+    features, keep, send = pl.pallas_call(
+        early_kernel,
+        out_shape=(half_features, share, share),
+        in_specs=[WHOLE] * 11 + [ANY],
+        out_specs=(ANY, WHOLE, WHOLE),
+        scratch_shapes=staging,
+        input_output_aliases={11: 0},
+        compiler_params=params(24),
+        cost_estimate=pl.CostEstimate(flops=spots * chans * chans * 10, bytes_accessed=5 * 2**20, transcendentals=spots * chans // 2),
+    )(edge, early, old_edge, old_early, old_mate, old_cross, conv_weight, more, sums, gain, targets, features)
     mine = total_over_chips(keep, with_mate(send))
     other = with_mate(mine)
     gram, cross = pl.pallas_call(

time: 42.5 us -> 40.2 us (0.946)
  waiting for transfers between devices: 18.5 us -> 13.9 us
  starting transfers between devices: 14.9 us -> 17.1 us
    ppermute x2 -> x3, waiting for transfers between devices: 7.37 us -> 2.85 us  [later(): lax.ppermute(value, 'tm', [(i, (i + 1) % count) for i in range(count)])]
    ppermute x2 -> x3, starting transfers between devices: 4.59 us -> 6.06 us  [later(): lax.ppermute(value, 'tm', [(i, (i + 1) % count) for i in range(count)])]
    ppermute x12, starting transfers between devices: 10.3 us -> 11.1 us  [by_device(): lax.ppermute(value, ('tm', 'row'), [(a * rows + b, c * rows + d) for (a,...]
    pallas_call x1 -> x2, Pallas kernels: 3.76 us -> 3.74 us  [the longest x1 1.92 us: on_device(): pl.pallas_call(late_kernel, out_shape=(half_features, jax.ShapeDtypeStruc...]
  transfers between devices with their start and end apart: 14 -> 15, of which waited for: 10 -> 10; matrix products, arithmetic and copies ran while one was open for 0% -> 0% of each run, Pallas kernels for 5% -> 10%
where the time goes in v4:
time: 40.2 us; the launch traced here: 40 us
  starting transfers between devices  17.1 us (43%)
  waiting for transfers between devices  13.9 us (35%)
  Pallas kernels  6.73 us (17%)
  local copies, waits for them, and re-layouts  1.04 us (3%)
  between operations  0.84 us (2%)
    ppermute x12, waiting for transfers between devices, by_device(): lax.ppermute(value, ('tm', 'row'), [(a * rows + b, c * rows + d) for (a,...  11.1 us
    ppermute x12, starting transfers between devices, by_device(): lax.ppermute(value, ('tm', 'row'), [(a * rows + b, c * rows + d) for (a,...  11.1 us
    ppermute x3, starting transfers between devices, later(): lax.ppermute(value, 'tm', [(i, (i + 1) % count) for i in range(count)])  6.06 us
    ppermute x3, waiting for transfers between devices, later(): lax.ppermute(value, 'tm', [(i, (i + 1) % count) for i in range(count)])  2.85 us
    pallas_call x1, Pallas kernels, on_device(): pl.pallas_call(own_kernel, out_shape=jax.ShapeDtypeStruct((spots, chans),...  1.96 us
    pallas_call x1, Pallas kernels, on_device(): pl.pallas_call(late_kernel, out_shape=(half_features, jax.ShapeDtypeStruc...  1.92 us
    pallas_call x1, Pallas kernels, on_device(): pl.pallas_call(early_kernel, out_shape=(half_features, share, share), in_...  1.82 us
    unnamed x8, local copies, waits for them, and re-layouts  1.04 us
  transfers between devices with their start and end apart: 15, of which 10 were waited for; matrix products, arithmetic and copies ran while one was open for 0% of the time, Pallas kernels for 10%

profile of v4, /device:TPU:0, one launch (start us, length us, event | category | flops | bytes accessed | tf_op | source)
XLA Modules:
  0.0 40.0 jit_solution(995107493603545316)
XLA Ops:
  0.6 0.0 copy-start.2
  0.6 1.0 %copy-done.2 = bf16[2,6,80,256]{3,2,1,0:T(8,128)(2,1)S(1)} copy-done((bf16[2,6,80,256]{3,2,1,0:T(8,128)(2,1)S(1)}, bf16[2,6,80,256]{3,2,1,0:T(8,128)(2,1)}, u32[]{:S(2)}) %copy-start.2) | copy-done | bytes 491544
  1.7 3.0 %collective-permute-start = (bf16[2,2,80,256]{3,2,1,0:T(8,128)(2,1)S(1)}, bf16[2,2,80,256]{3,2,1,0:T(8,128)(2,1)S(1)}, u32[]{:S(2)}, u32[]{:S(2)}) collective-permute-start(bf16[2,2,80,256]{3,2,1,0:T(8,128)(2,1)S(1)} %get-tuple-element.18.edge_ref), channel_id=1, source_target_pairs={{0,4},{4,8},{8,12},{12,16},{16,20},{20,24},{24,28},{28,0},{1,5},{5... | collective-permute-start | bytes 491528 | tf_op jit(solution)/shard_map/ppermute | solution.py:43
  4.7 0.0 collective-permute-start.5
  4.7 1.6 %collective-permute-start.6 = (bf16[2,80,256]{2,1,0:T(8,128)(2,1)S(1)}, bf16[2,80,256]{2,1,0:T(8,128)(2,1)S(1)}, u32[]{:S(2)}, u32[]{:S(2)}) collective-permute-start(bf16[2,80,256]{2,1,0:T(8,128)(2,1)S(1)} %get-tuple-element.24), channel_id=1, source_target_pairs={{0,3},{1,2},{2,1},{3,0},{4,7},{5,6},{6,5},{7,4},{8,11},{9,10},{10,... | collective-permute-start | bytes 245768 | tf_op jit(solution)/shard_map/ppermute | solution.py:38
  6.3 1.5 %collective-permute-start.4 = (bf16[4,80,256]{2,1,0:T(8,128)(2,1)S(1)}, bf16[4,80,256]{2,1,0:T(8,128)(2,1)S(1)}, u32[]{:S(2)}, u32[]{:S(2)}) collective-permute-start(bf16[4,80,256]{2,1,0:T(8,128)(2,1)S(1)} %get-tuple-element.22.late_ref), channel_id=1, source_target_pairs={{0,4},{4,8},{8,12},{12,16},{16,20},{20,24},{24,28},{28,0},{1,5},{5... | collective-permute-start | bytes 491528 | tf_op jit(solution)/shard_map/ppermute | solution.py:43
  7.9 0.0 copy-start
  7.9 1.5 %collective-permute-start.1 = (bf16[4,80,256]{2,1,0:T(8,128)(2,1)S(1)}, bf16[4,80,256]{2,1,0:T(8,128)(2,1)S(1)}, u32[]{:S(2)}, u32[]{:S(2)}) collective-permute-start(bf16[4,80,256]{2,1,0:T(8,128)(2,1)S(1)} %get-tuple-element.19.early_ref), channel_id=1, source_target_pairs={{0,4},{4,8},{8,12},{12,16},{16,20},{20,24},{24,28},{28,0},{1,5},{5... | collective-permute-start | bytes 491528 | tf_op jit(solution)/shard_map/ppermute | solution.py:43
  9.4 2.8 %collective-permute-done.edge_ref.old_edge_ref = bf16[2,2,80,256]{3,2,1,0:T(8,128)(2,1)S(1)} collective-permute-done((bf16[2,2,80,256]{3,2,1,0:T(8,128)(2,1)S(1)}, bf16[2,2,80,256]{3,2,1,0:T(8,128)(2,1)S(1)}, u32[]{:S(2)}, u32[]{:S(2)}) %collective-permute-start) | collective-permute-done | bytes 163872 | tf_op jit(solution)/shard_map/ppermute | solution.py:43
  12.2 0.0 copy-start.1
  12.3 0.0 copy-start.3
  12.3 0.1 collective-permute-start.2
  12.4 0.0 collective-permute-done.5.mate_ref
  12.4 2.4 %collective-permute-start.3 = (bf16[2,80,256]{2,1,0:T(8,128)(2,1)S(1)}, bf16[2,80,256]{2,1,0:T(8,128)(2,1)S(1)}, u32[]{:S(2)}, u32[]{:S(2)}) collective-permute-start(bf16[2,80,256]{2,1,0:T(8,128)(2,1)S(1)} %get-tuple-element.21), channel_id=1, source_target_pairs={{0,3},{1,2},{2,1},{3,0},{4,7},{5,6},{6,5},{7,4},{8,11},{9,10},{10,... | collective-permute-start | bytes 245768 | tf_op jit(solution)/shard_map/ppermute | solution.py:38
  14.7 0.0 collective-permute-done.6.cross_ref
  14.7 0.0 copy-done
  14.7 2.0 %shard_map.69.part_ref = f32[960,256]{1,0:T(8,128)S(1)} custom-call(bf16[2,2,80,256]{3,2,1,0:T(8,128)(2,1)S(1)} %get-tuple-element.18.edge_ref, bf16[4,80,256]{2,1,0:T(8,128)(2,1)S(1)} %get-tuple-element.19.early_ref, bf16[4,80,256]{2,1,0:T(8,128)(2,1)S(1)} %get-tuple-element.22.late_ref, bf16[2,80,256]{2,1,0:T(8,128)(2,1)S(1)} %collective-permute-done.5.mate_ref, ...), custom_call_target="tpu_custom_call" | custom-call | flops 1698693120 | bytes 5242880 | tf_op jit(solution)/shard_map/pallas_call | solution.py:311
  16.7 0.0 collective-permute-done.4.old_late_ref
  16.7 0.0 collective-permute-done.2.mate_ref
  16.7 0.7 %collective-permute-done.3.cross_ref = bf16[2,80,256]{2,1,0:T(8,128)(2,1)S(1)} collective-permute-done((bf16[2,80,256]{2,1,0:T(8,128)(2,1)S(1)}, bf16[2,80,256]{2,1,0:T(8,128)(2,1)S(1)}, u32[]{:S(2)}, u32[]{:S(2)}) %collective-permute-start.3) | collective-permute-done | bytes 81952 | tf_op jit(solution)/shard_map/ppermute | solution.py:38
  17.4 0.0 copy-done.1
  17.4 0.0 copy-done.3
  17.4 1.9 %shard_map.70 = (bf16[960,256]{1,0:T(8,128)(2,1)}, f32[480,256]{1,0:T(8,128)S(1)}, f32[256,384]{1,0:T(8,128)S(1)}) custom-call(bf16[2,2,80,256]{3,2,1,0:T(8,128)(2,1)S(1)} %get-tuple-element.18.edge_ref, bf16[4,80,256]{2,1,0:T(8,128)(2,1)S(1)} %get-tuple-element.22.late_ref, bf16[2,2,80,256]{3,2,1,0:T(8,128)(2,1)S(1)} %collective-permute-done.edge_ref.old_edge_ref, ...), custom_call_target="tpu_custom_call" | custom-call | flops 1258291200 | bytes 5242880 | tf_op jit(solution)/shard_map/pallas_call | solution.py:322
  19.4 0.0 collective-permute-done.1.old_early_ref
  19.4 1.8 %shard_map.71 = (bf16[960,256]{1,0:T(8,128)(2,1)}, f32[264,128]{1,0:T(8,128)S(1)}, f32[264,128]{1,0:T(8,128)S(1)}) custom-call(bf16[2,2,80,256]{3,2,1,0:T(8,128)(2,1)S(1)} %get-tuple-element.18.edge_ref, bf16[4,80,256]{2,1,0:T(8,128)(2,1)S(1)} %get-tuple-element.19.early_ref, ...), custom_call_target="tpu_custom_call", output_to_operand_aliasing={{0}: (11, {})} | custom-call | flops 629145600 | bytes 5242880 | tf_op jit(solution)/shard_map/pallas_call | solution.py:336
  21.2 0.5 %collective-permute-start.7 = (f32[264,128]{1,0:T(8,128)S(1)}, f32[264,128]{1,0:T(8,128)S(1)}, u32[]{:S(2)}, u32[]{:S(2)}) collective-permute-start(f32[264,128]{1,0:T(8,128)S(1)} %get-tuple-element.30), channel_id=1, source_target_pairs={{0,1},{1,0},{2,3},{3,2},{4,5},{5,4},{6,7},{7,6},{8,9},{9,8},{10,11... | collective-permute-start | bytes 405512 | tf_op jit(solution)/shard_map/ppermute | solution.py:38
  21.7 1.0 %collective-permute-done.7.got_ref = f32[264,128]{1,0:T(8,128)S(1)} collective-permute-done((f32[264,128]{1,0:T(8,128)S(1)}, f32[264,128]{1,0:T(8,128)S(1)}, u32[]{:S(2)}, u32[]{:S(2)}) %collective-permute-start.7) | collective-permute-done | bytes 135200 | tf_op jit(solution)/shard_map/ppermute | solution.py:38
  22.7 0.1 shard_map.72
  22.8 1.7 %collective-permute-start.8 = (f16[272,128]{1,0:T(8,128)(2,1)S(1)}, f16[272,128]{1,0:T(8,128)(2,1)S(1)}, u32[]{:S(2)}, u32[]{:S(2)}) collective-permute-start(f16[272,128]{1,0:T(8,128)(2,1)S(1)} %convert_element_type.30), channel_id=1, source_target_pairs={{0,3},{1,8},{2,11},{3,0},{4,13},{5,6},{6,5},{7,14},{8,1},{9,10},{1... | collective-permute-start | bytes 208904 | tf_op jit(solution)/shard_map/ppermute | solution.py:38
  24.5 0.0 collective-permute-start.9
  24.5 1.5 %collective-permute-start.10 = (f16[272,128]{1,0:T(8,128)(2,1)S(1)}, f16[272,128]{1,0:T(8,128)(2,1)S(1)}, u32[]{:S(2)}, u32[]{:S(2)}) collective-permute-start(f16[272,128]{1,0:T(8,128)(2,1)S(1)} %convert_element_type.30), channel_id=1, source_target_pairs={{0,6},{1,25},{2,26},{3,5},{4,28},{5,3},{6,0},{7,31},{8,16},{9,15},... | collective-permute-start | bytes 208904 | tf_op jit(solution)/shard_map/ppermute | solution.py:38
  26.1 0.5 %collective-permute-done.8 = f16[272,128]{1,0:T(8,128)(2,1)S(1)} collective-permute-done((f16[272,128]{1,0:T(8,128)(2,1)S(1)}, f16[272,128]{1,0:T(8,128)(2,1)S(1)}, u32[]{:S(2)}, u32[]{:S(2)}) %collective-permute-start.8) | collective-permute-done | bytes 69664 | tf_op jit(solution)/shard_map/ppermute | solution.py:38
  26.6 1.7 %collective-permute-done.9 = f16[272,128]{1,0:T(8,128)(2,1)S(1)} collective-permute-done((f16[272,128]{1,0:T(8,128)(2,1)S(1)}, f16[272,128]{1,0:T(8,128)(2,1)S(1)}, u32[]{:S(2)}, u32[]{:S(2)}) %collective-permute-start.9) | collective-permute-done | bytes 69664 | tf_op jit(solution)/shard_map/ppermute | solution.py:38
  28.3 1.5 %collective-permute-done.10 = f16[272,128]{1,0:T(8,128)(2,1)S(1)} collective-permute-done((f16[272,128]{1,0:T(8,128)(2,1)S(1)}, f16[272,128]{1,0:T(8,128)(2,1)S(1)}, u32[]{:S(2)}, u32[]{:S(2)}) %collective-permute-start.10) | collective-permute-done | bytes 69664 | tf_op jit(solution)/shard_map/ppermute | solution.py:38
  29.8 0.1 select_convert_fusion
  29.9 0.1 collective-permute-start.11
  30.0 2.3 %collective-permute-start.13 = (f16[272,128]{1,0:T(8,128)(2,1)S(1)}, f16[272,128]{1,0:T(8,128)(2,1)S(1)}, u32[]{:S(2)}, u32[]{:S(2)}) collective-permute-start(f16[272,128]{1,0:T(8,128)(2,1)S(1)} %select_convert_fusion), channel_id=1, source_target_pairs={{0,24},{1,7},{2,4},{3,27},{4,2},{5,29},{6,30},{7,1},{8,14},{9,17},... | collective-permute-start | bytes 208904 | tf_op jit(solution)/shard_map/ppermute | solution.py:38
  32.3 0.7 %collective-permute-start.12 = (f16[272,128]{1,0:T(8,128)(2,1)S(1)}, f16[272,128]{1,0:T(8,128)(2,1)S(1)}, u32[]{:S(2)}, u32[]{:S(2)}) collective-permute-start(f16[272,128]{1,0:T(8,128)(2,1)S(1)} %select_convert_fusion), channel_id=1, source_target_pairs={{0,17},{1,4},{2,7},{3,18},{4,1},{5,20},{6,23},{7,2},{8,13},{9,24},... | collective-permute-start | bytes 208904 | tf_op jit(solution)/shard_map/ppermute | solution.py:38
  32.9 0.8 %collective-permute-done.11 = f16[272,128]{1,0:T(8,128)(2,1)S(1)} collective-permute-done((f16[272,128]{1,0:T(8,128)(2,1)S(1)}, f16[272,128]{1,0:T(8,128)(2,1)S(1)}, u32[]{:S(2)}, u32[]{:S(2)}) %collective-permute-start.11) | collective-permute-done | bytes 69664 | tf_op jit(solution)/shard_map/ppermute | solution.py:38
  33.8 2.4 %collective-permute-done.13 = f16[272,128]{1,0:T(8,128)(2,1)S(1)} collective-permute-done((f16[272,128]{1,0:T(8,128)(2,1)S(1)}, f16[272,128]{1,0:T(8,128)(2,1)S(1)}, u32[]{:S(2)}, u32[]{:S(2)}) %collective-permute-start.13) | collective-permute-done | bytes 69664 | tf_op jit(solution)/shard_map/ppermute | solution.py:38
  36.2 1.5 %collective-permute-done.12 = f16[272,128]{1,0:T(8,128)(2,1)S(1)} collective-permute-done((f16[272,128]{1,0:T(8,128)(2,1)S(1)}, f16[272,128]{1,0:T(8,128)(2,1)S(1)}, u32[]{:S(2)}, u32[]{:S(2)}) %collective-permute-start.12) | collective-permute-done | bytes 69664 | tf_op jit(solution)/shard_map/ppermute | solution.py:38
  37.7 0.3 collective-permute-start.14
  38.1 1.1 %collective-permute-done.14.other_ref = f32[264,128]{1,0:T(8,128)S(1)} collective-permute-done((f32[264,128]{1,0:T(8,128)S(1)}, f32[264,128]{1,0:T(8,128)S(1)}, u32[]{:S(2)}, u32[]{:S(2)}) %collective-permute-start.14) | collective-permute-done | bytes 135200 | tf_op jit(solution)/shard_map/ppermute | solution.py:38
  39.2 0.8 %shard_map.73 = (f32[256,256]{1,0:T(8,128)}, f32[256,128]{1,0:T(8,128)}) custom-call(f32[264,128]{1,0:T(8,128)S(1)} %fusion.1.mine_ref, f32[264,128]{1,0:T(8,128)S(1)} %collective-permute-done.14.other_ref), custom_call_target="tpu_custom_call" | custom-call | tf_op jit(solution)/shard_map/pallas_call | solution.py:348
  (19 shorter events, 0.3 us)
Async XLA Ops:
  0.6 1.0 %copy-start.2 = (bf16[2,6,80,256]{3,2,1,0:T(8,128)(2,1)S(1)}, bf16[2,6,80,256]{3,2,1,0:T(8,128)(2,1)}, u32[]{:S(2)}) copy-start(bf16[2,6,80,256]{3,2,1,0:T(8,128)(2,1)} %latents_ref.1) | copy-start | bytes 1474564
  1.7 10.5 %collective-permute-start = (bf16[2,2,80,256]{3,2,1,0:T(8,128)(2,1)S(1)}, bf16[2,2,80,256]{3,2,1,0:T(8,128)(2,1)S(1)}, u32[]{:S(2)}, u32[]{:S(2)}) collective-permute-start(bf16[2,2,80,256]{3,2,1,0:T(8,128)(2,1)S(1)} %get-tuple-element.18.edge_ref), channel_id=1, source_target_pairs={{0,4},{4,8},{8,12},{12,16},{16,20},{20,24},{24,28},{28,0},{1,5},{5... | collective-permute-start | bytes 491528 | tf_op jit(solution)/shard_map/ppermute | solution.py:43
  4.7 7.6 %collective-permute-start.5 = (bf16[2,80,256]{2,1,0:T(8,128)(2,1)S(1)}, bf16[2,80,256]{2,1,0:T(8,128)(2,1)S(1)}, u32[]{:S(2)}, u32[]{:S(2)}) collective-permute-start(bf16[2,80,256]{2,1,0:T(8,128)(2,1)S(1)} %get-tuple-element.23), channel_id=1, source_target_pairs={{0,1},{1,0},{2,3},{3,2},{4,5},{5,4},{6,7},{7,6},{8,9},{9,8},{10,11... | collective-permute-start | bytes 245768 | tf_op jit(solution)/shard_map/ppermute | solution.py:38
  4.7 10.0 %collective-permute-start.6 = (bf16[2,80,256]{2,1,0:T(8,128)(2,1)S(1)}, bf16[2,80,256]{2,1,0:T(8,128)(2,1)S(1)}, u32[]{:S(2)}, u32[]{:S(2)}) collective-permute-start(bf16[2,80,256]{2,1,0:T(8,128)(2,1)S(1)} %get-tuple-element.24), channel_id=1, source_target_pairs={{0,3},{1,2},{2,1},{3,0},{4,7},{5,6},{6,5},{7,4},{8,11},{9,10},{10,... | collective-permute-start | bytes 245768 | tf_op jit(solution)/shard_map/ppermute | solution.py:38
  6.3 10.4 %collective-permute-start.4 = (bf16[4,80,256]{2,1,0:T(8,128)(2,1)S(1)}, bf16[4,80,256]{2,1,0:T(8,128)(2,1)S(1)}, u32[]{:S(2)}, u32[]{:S(2)}) collective-permute-start(bf16[4,80,256]{2,1,0:T(8,128)(2,1)S(1)} %get-tuple-element.22.late_ref), channel_id=1, source_target_pairs={{0,4},{4,8},{8,12},{12,16},{16,20},{20,24},{24,28},{28,0},{1,5},{5... | collective-permute-start | bytes 491528 | tf_op jit(solution)/shard_map/ppermute | solution.py:43
  7.9 6.9 %copy-start = (bf16[3,3,768,256]{3,2,1,0:T(8,128)(2,1)S(1)}, bf16[3,3,768,256]{3,2,1,0:T(8,128)(2,1)}, u32[]{:S(2)}) copy-start(bf16[3,3,768,256]{3,2,1,0:T(8,128)(2,1)} %weight_ref.5) | copy-start | bytes 10616836
  7.9 11.5 %collective-permute-start.1 = (bf16[4,80,256]{2,1,0:T(8,128)(2,1)S(1)}, bf16[4,80,256]{2,1,0:T(8,128)(2,1)S(1)}, u32[]{:S(2)}, u32[]{:S(2)}) collective-permute-start(bf16[4,80,256]{2,1,0:T(8,128)(2,1)S(1)} %get-tuple-element.19.early_ref), channel_id=1, source_target_pairs={{0,4},{4,8},{8,12},{12,16},{16,20},{20,24},{24,28},{28,0},{1,5},{5... | collective-permute-start | bytes 491528 | tf_op jit(solution)/shard_map/ppermute | solution.py:43
  12.2 5.2 %copy-start.1 = (bf16[2,6,80,128]{3,2,1,0:T(8,128)(2,1)S(1)}, bf16[2,6,80,128]{3,2,1,0:T(8,128)(2,1)}, u32[]{:S(2)}) copy-start(bf16[2,6,80,128]{3,2,1,0:T(8,128)(2,1)} %param.7) | copy-start | bytes 737284
  12.3 5.2 %copy-start.3 = (f32[256]{0:T(256)S(1)}, f32[256]{0:T(256)}, u32[]{:S(2)}) copy-start(f32[256]{0:T(256)} %param.6) | copy-start | bytes 3076
  12.3 4.4 %collective-permute-start.2 = (bf16[2,80,256]{2,1,0:T(8,128)(2,1)S(1)}, bf16[2,80,256]{2,1,0:T(8,128)(2,1)S(1)}, u32[]{:S(2)}, u32[]{:S(2)}) collective-permute-start(bf16[2,80,256]{2,1,0:T(8,128)(2,1)S(1)} %get-tuple-element.20), channel_id=1, source_target_pairs={{0,1},{1,0},{2,3},{3,2},{4,5},{5,4},{6,7},{7,6},{8,9},{9,8},{10,11... | collective-permute-start | bytes 245768 | tf_op jit(solution)/shard_map/ppermute | solution.py:38
  12.4 5.1 %collective-permute-start.3 = (bf16[2,80,256]{2,1,0:T(8,128)(2,1)S(1)}, bf16[2,80,256]{2,1,0:T(8,128)(2,1)S(1)}, u32[]{:S(2)}, u32[]{:S(2)}) collective-permute-start(bf16[2,80,256]{2,1,0:T(8,128)(2,1)S(1)} %get-tuple-element.21), channel_id=1, source_target_pairs={{0,3},{1,2},{2,1},{3,0},{4,7},{5,6},{6,5},{7,4},{8,11},{9,10},{10,... | collective-permute-start | bytes 245768 | tf_op jit(solution)/shard_map/ppermute | solution.py:38
  21.2 1.4 %collective-permute-start.7 = (f32[264,128]{1,0:T(8,128)S(1)}, f32[264,128]{1,0:T(8,128)S(1)}, u32[]{:S(2)}, u32[]{:S(2)}) collective-permute-start(f32[264,128]{1,0:T(8,128)S(1)} %get-tuple-element.30), channel_id=1, source_target_pairs={{0,1},{1,0},{2,3},{3,2},{4,5},{5,4},{6,7},{7,6},{8,9},{9,8},{10,11... | collective-permute-start | bytes 405512 | tf_op jit(solution)/shard_map/ppermute | solution.py:38
  22.8 3.8 %collective-permute-start.8 = (f16[272,128]{1,0:T(8,128)(2,1)S(1)}, f16[272,128]{1,0:T(8,128)(2,1)S(1)}, u32[]{:S(2)}, u32[]{:S(2)}) collective-permute-start(f16[272,128]{1,0:T(8,128)(2,1)S(1)} %convert_element_type.30), channel_id=1, source_target_pairs={{0,3},{1,8},{2,11},{3,0},{4,13},{5,6},{6,5},{7,14},{8,1},{9,10},{1... | collective-permute-start | bytes 208904 | tf_op jit(solution)/shard_map/ppermute | solution.py:38
  24.5 3.7 %collective-permute-start.9 = (f16[272,128]{1,0:T(8,128)(2,1)S(1)}, f16[272,128]{1,0:T(8,128)(2,1)S(1)}, u32[]{:S(2)}, u32[]{:S(2)}) collective-permute-start(f16[272,128]{1,0:T(8,128)(2,1)S(1)} %convert_element_type.30), channel_id=1, source_target_pairs={{0,5},{1,16},{2,19},{3,6},{4,21},{5,0},{6,3},{7,22},{8,25},{9,12},... | collective-permute-start | bytes 208904 | tf_op jit(solution)/shard_map/ppermute | solution.py:38
  24.5 5.2 %collective-permute-start.10 = (f16[272,128]{1,0:T(8,128)(2,1)S(1)}, f16[272,128]{1,0:T(8,128)(2,1)S(1)}, u32[]{:S(2)}, u32[]{:S(2)}) collective-permute-start(f16[272,128]{1,0:T(8,128)(2,1)S(1)} %convert_element_type.30), channel_id=1, source_target_pairs={{0,6},{1,25},{2,26},{3,5},{4,28},{5,3},{6,0},{7,31},{8,16},{9,15},... | collective-permute-start | bytes 208904 | tf_op jit(solution)/shard_map/ppermute | solution.py:38
  29.9 3.8 %collective-permute-start.11 = (f16[272,128]{1,0:T(8,128)(2,1)S(1)}, f16[272,128]{1,0:T(8,128)(2,1)S(1)}, u32[]{:S(2)}, u32[]{:S(2)}) collective-permute-start(f16[272,128]{1,0:T(8,128)(2,1)S(1)} %select_convert_fusion), channel_id=1, source_target_pairs={{0,9},{1,2},{2,1},{3,10},{4,7},{5,12},{6,15},{7,4},{8,11},{9,0},{1... | collective-permute-start | bytes 208904 | tf_op jit(solution)/shard_map/ppermute | solution.py:38
  30.0 6.2 %collective-permute-start.13 = (f16[272,128]{1,0:T(8,128)(2,1)S(1)}, f16[272,128]{1,0:T(8,128)(2,1)S(1)}, u32[]{:S(2)}, u32[]{:S(2)}) collective-permute-start(f16[272,128]{1,0:T(8,128)(2,1)S(1)} %select_convert_fusion), channel_id=1, source_target_pairs={{0,24},{1,7},{2,4},{3,27},{4,2},{5,29},{6,30},{7,1},{8,14},{9,17},... | collective-permute-start | bytes 208904 | tf_op jit(solution)/shard_map/ppermute | solution.py:38
  32.3 5.4 %collective-permute-start.12 = (f16[272,128]{1,0:T(8,128)(2,1)S(1)}, f16[272,128]{1,0:T(8,128)(2,1)S(1)}, u32[]{:S(2)}, u32[]{:S(2)}) collective-permute-start(f16[272,128]{1,0:T(8,128)(2,1)S(1)} %select_convert_fusion), channel_id=1, source_target_pairs={{0,17},{1,4},{2,7},{3,18},{4,1},{5,20},{6,23},{7,2},{8,13},{9,24},... | collective-permute-start | bytes 208904 | tf_op jit(solution)/shard_map/ppermute | solution.py:38
  37.7 1.4 %collective-permute-start.14 = (f32[264,128]{1,0:T(8,128)S(1)}, f32[264,128]{1,0:T(8,128)S(1)}, u32[]{:S(2)}, u32[]{:S(2)}) collective-permute-start(f32[264,128]{1,0:T(8,128)S(1)} %fusion.1.mine_ref), channel_id=1, source_target_pairs={{0,1},{1,0},{2,3},{3,2},{4,5},{5,4},{6,7},{7,6},{8,9},{9,8},{10,11... | collective-permute-start | bytes 405512 | tf_op jit(solution)/shard_map/ppermute | solution.py:38

commit v5 on v4

--- a/solution.py
+++ b/solution.py
@@ -12,7 +12,6 @@
 F16 = jnp.float16
 HEAD = 16
 WHOLE = pl.BlockSpec(memory_space=pltpu.VMEM)
-ANY = pl.BlockSpec(memory_space=pl.ANY)
 
 
 def params(mebibytes):
@@ -141,30 +140,25 @@
 
 
 def late_kernel(edge_ref, late_ref, old_edge_ref, old_late_ref, mate_ref, cross_ref, weight_ref, part_ref, gain_ref,
-                target_ref, feature_ref, more_ref, sums_ref, stage, sem):
+                target_ref, feature_ref, more_ref, sums_ref):
     cols, chans = edge_ref.shape[2:]
     span = part_ref.shape[0] // 2
     stack = padded_stack(old_edge_ref, old_late_ref, mate_ref, cross_ref, 1)
     conv = part_ref[span:] + older_terms(stack, weight_ref, 0, cols, chans)
     features = features_of(conv, frame_rows(edge_ref, late_ref, 1), gain_ref)
-    stage[...] = features
-    copy = pltpu.make_async_copy(stage, feature_ref.at[pl.ds(span, span)], sem)
-    copy.start()
+    feature_ref[...] = features
     more_ref[...] = part_ref[:span] + older_terms(stack, weight_ref, 1, cols, chans)
     sums_ref[...] = moments(features, target_ref[span:])
-    copy.wait()
 
 
 def early_kernel(edge_ref, early_ref, old_edge_ref, old_early_ref, mate_ref, cross_ref, weight_ref, more_ref, sums_ref,
-                 gain_ref, target_ref, late_feature_ref, feature_ref, keep_ref, send_ref, stage, sem):
+                 gain_ref, target_ref, feature_ref, keep_ref, send_ref):
     cols, chans = edge_ref.shape[2:]
     span, half = more_ref.shape[0], chans // 2
     stack = padded_stack(old_edge_ref, old_early_ref, mate_ref, cross_ref, 0)
     conv = more_ref[...] + older_terms(stack, weight_ref, 0, cols, chans)
     features = features_of(conv, frame_rows(edge_ref, early_ref, 0), gain_ref)
-    stage[...] = features
-    copy = pltpu.make_async_copy(stage, feature_ref.at[pl.ds(0, span)], sem)
-    copy.start()
+    feature_ref[...] = features
     sums = sums_ref[...] + moments(features, target_ref[:span])
     row = lax.broadcasted_iota(jnp.int32, (half, half), 0)
     col = lax.broadcasted_iota(jnp.int32, (half, half), 1)
@@ -183,8 +177,6 @@
     def _():
         keep_ref[...] = high
         send_ref[...] = low
-
-    copy.wait()
 
 
 def unpack_kernel(count, mine_ref, other_ref, gram_ref, cross_ref):
@@ -278,7 +270,7 @@
                 c, d = pair[odd_bits(a ^ b)]
                 moves.append(((a, b), (a ^ c, b ^ d ^ odd_bits(c ^ d))))
             messages.append(by_device(value, moves))
-        value = joined_messages(messages, s == len(rounds) - 1)
+        value = joined_messages(messages[::-1], s == len(rounds) - 1)
     return value
 
 
@@ -317,9 +309,8 @@
         cost_estimate=pl.CostEstimate(flops=spots * chans * chans * 27, bytes_accessed=5 * 2**20, transcendentals=0),
     )(edge, early, late, mate, cross, conv_weight)
     gain, targets = norm_gain.reshape(1, chans), depth_target.reshape(spots, bins)
-    half_features = jax.ShapeDtypeStruct((spots, chans), BF16)
-    staging = [pltpu.VMEM((spots // 2, chans), BF16), pltpu.SemaphoreType.DMA]
-    features, more, sums = pl.pallas_call(
+    half_features = jax.ShapeDtypeStruct((spots // 2, chans), BF16)
+    late_features, more, sums = pl.pallas_call(
         late_kernel,
         out_shape=(
             half_features,
@@ -327,23 +318,22 @@
             jax.ShapeDtypeStruct((chans, chans + bins), F32),
         ),
         in_specs=[WHOLE] * 10,
-        out_specs=(ANY, WHOLE, WHOLE),
-        scratch_shapes=staging,
+        out_specs=(WHOLE,) * 3,
         compiler_params=params(24),
         cost_estimate=pl.CostEstimate(flops=spots * chans * chans * 20, bytes_accessed=5 * 2**20, transcendentals=spots * chans // 2),
     )(edge, late, old_edge, old_late, old_mate, old_cross, conv_weight, part, gain, targets)
     share = jax.ShapeDtypeStruct((2 * half + HEAD // 2, half), F32)
-    features, keep, send = pl.pallas_call(
+    early_features, keep, send = pl.pallas_call(
         early_kernel,
         out_shape=(half_features, share, share),
-        in_specs=[WHOLE] * 11 + [ANY],
-        out_specs=(ANY, WHOLE, WHOLE),
-        scratch_shapes=staging,
-        input_output_aliases={11: 0},
+        in_specs=[WHOLE] * 11,
+        out_specs=(WHOLE,) * 3,
         compiler_params=params(24),
         cost_estimate=pl.CostEstimate(flops=spots * chans * chans * 10, bytes_accessed=5 * 2**20, transcendentals=spots * chans // 2),
-    )(edge, early, old_edge, old_early, old_mate, old_cross, conv_weight, more, sums, gain, targets, features)
+    )(edge, early, old_edge, old_early, old_mate, old_cross, conv_weight, more, sums, gain, targets)
+    features = jnp.stack([early_features, late_features])
     mine = total_over_chips(keep, with_mate(send))
+    mine, features = lax.optimization_barrier((mine, features))
     other = with_mate(mine)
     gram, cross = pl.pallas_call(
         functools.partial(unpack_kernel, spots * blocks * bands),

time: 40.2 us -> 38.9 us (0.968)
  waiting for transfers between devices: 13.9 us -> 12.4 us
  other arithmetic: 0.32 us -> 1.14 us
  Pallas kernels: 6.73 us -> 5.97 us
    ppermute x12, waiting for transfers between devices: 11.1 us -> 9.5 us  [by_device(): lax.ppermute(value, ('tm', 'row'), [(a * rows + b, c * rows + d) for (a,...]
    another operation x0 -> x1, other arithmetic: none -> 0.82 us  [on_device(): features = jnp.stack([early_features, late_features])]
  transfers between devices with their start and end apart: 15 -> 15, of which waited for: 10 -> 9; matrix products, arithmetic and copies ran while one was open for 0% -> 2% of each run, Pallas kernels for 10% -> 9%
where the time goes in v5:
time: 38.9 us; the launch traced here: 38.7 us
  starting transfers between devices  17.4 us (45%)
  waiting for transfers between devices  12.4 us (32%)
  Pallas kernels  5.97 us (15%)
  other arithmetic  1.14 us (3%)
  local copies, waits for them, and re-layouts  1.04 us (3%)
  between operations  0.85 us (2%)
    ppermute x12, starting transfers between devices, by_device(): lax.ppermute(value, ('tm', 'row'), [(a * rows + b, c * rows + d) for (a,...  11.3 us
    ppermute x12, waiting for transfers between devices, by_device(): lax.ppermute(value, ('tm', 'row'), [(a * rows + b, c * rows + d) for (a,...  9.5 us
    ppermute x3, starting transfers between devices, later(): lax.ppermute(value, 'tm', [(i, (i + 1) % count) for i in range(count)])  6.06 us
    ppermute x3, waiting for transfers between devices, later(): lax.ppermute(value, 'tm', [(i, (i + 1) % count) for i in range(count)])  2.86 us
    pallas_call x1, Pallas kernels, on_device(): pl.pallas_call(own_kernel, out_shape=jax.ShapeDtypeStruct((spots, chans),...  1.94 us
    pallas_call x1, Pallas kernels, on_device(): pl.pallas_call(late_kernel, out_shape=(half_features, jax.ShapeDtypeStruc...  1.53 us
    pallas_call x1, Pallas kernels, on_device(): pl.pallas_call(early_kernel, out_shape=(half_features, share, share), in_...  1.47 us
    unnamed x8, local copies, waits for them, and re-layouts  1.04 us
  transfers between devices with their start and end apart: 15, of which 9 were waited for; matrix products, arithmetic and copies ran while one was open for 2% of the time, Pallas kernels for 9%

profile of v5, /device:TPU:0, one launch (start us, length us, event | category | flops | bytes accessed | tf_op | source)
XLA Modules:
  0.0 38.7 jit_solution(8003139851943566033)
XLA Ops:
  0.6 0.0 copy-start.2
  0.6 1.0 %copy-done.2 = bf16[2,6,80,256]{3,2,1,0:T(8,128)(2,1)S(1)} copy-done((bf16[2,6,80,256]{3,2,1,0:T(8,128)(2,1)S(1)}, bf16[2,6,80,256]{3,2,1,0:T(8,128)(2,1)}, u32[]{:S(2)}) %copy-start.2) | copy-done | bytes 491544
  1.7 3.0 %collective-permute-start = (bf16[2,2,80,256]{3,2,1,0:T(8,128)(2,1)S(1)}, bf16[2,2,80,256]{3,2,1,0:T(8,128)(2,1)S(1)}, u32[]{:S(2)}, u32[]{:S(2)}) collective-permute-start(bf16[2,2,80,256]{3,2,1,0:T(8,128)(2,1)S(1)} %get-tuple-element.20.edge_ref), channel_id=1, source_target_pairs={{0,4},{4,8},{8,12},{12,16},{16,20},{20,24},{24,28},{28,0},{1,5},{5... | collective-permute-start | bytes 491528 | tf_op jit(solution)/shard_map/ppermute | solution.py:42
  4.7 0.0 collective-permute-start.5
  4.7 1.6 %collective-permute-start.6 = (bf16[2,80,256]{2,1,0:T(8,128)(2,1)S(1)}, bf16[2,80,256]{2,1,0:T(8,128)(2,1)S(1)}, u32[]{:S(2)}, u32[]{:S(2)}) collective-permute-start(bf16[2,80,256]{2,1,0:T(8,128)(2,1)S(1)} %get-tuple-element.26), channel_id=1, source_target_pairs={{0,3},{1,2},{2,1},{3,0},{4,7},{5,6},{6,5},{7,4},{8,11},{9,10},{10,... | collective-permute-start | bytes 245768 | tf_op jit(solution)/shard_map/ppermute | solution.py:37
  6.3 1.5 %collective-permute-start.4 = (bf16[4,80,256]{2,1,0:T(8,128)(2,1)S(1)}, bf16[4,80,256]{2,1,0:T(8,128)(2,1)S(1)}, u32[]{:S(2)}, u32[]{:S(2)}) collective-permute-start(bf16[4,80,256]{2,1,0:T(8,128)(2,1)S(1)} %get-tuple-element.24.late_ref), channel_id=1, source_target_pairs={{0,4},{4,8},{8,12},{12,16},{16,20},{20,24},{24,28},{28,0},{1,5},{5... | collective-permute-start | bytes 491528 | tf_op jit(solution)/shard_map/ppermute | solution.py:42
  7.9 0.0 copy-start
  7.9 1.5 %collective-permute-start.1 = (bf16[4,80,256]{2,1,0:T(8,128)(2,1)S(1)}, bf16[4,80,256]{2,1,0:T(8,128)(2,1)S(1)}, u32[]{:S(2)}, u32[]{:S(2)}) collective-permute-start(bf16[4,80,256]{2,1,0:T(8,128)(2,1)S(1)} %get-tuple-element.21.early_ref), channel_id=1, source_target_pairs={{0,4},{4,8},{8,12},{12,16},{16,20},{20,24},{24,28},{28,0},{1,5},{5... | collective-permute-start | bytes 491528 | tf_op jit(solution)/shard_map/ppermute | solution.py:42
  9.4 2.8 %collective-permute-done.edge_ref.old_edge_ref = bf16[2,2,80,256]{3,2,1,0:T(8,128)(2,1)S(1)} collective-permute-done((bf16[2,2,80,256]{3,2,1,0:T(8,128)(2,1)S(1)}, bf16[2,2,80,256]{3,2,1,0:T(8,128)(2,1)S(1)}, u32[]{:S(2)}, u32[]{:S(2)}) %collective-permute-start) | collective-permute-done | bytes 163872 | tf_op jit(solution)/shard_map/ppermute | solution.py:42
  12.2 0.0 copy-start.1
  12.3 0.0 copy-start.3
  12.3 0.1 collective-permute-start.2
  12.4 0.0 collective-permute-done.5.mate_ref
  12.4 2.4 %collective-permute-start.3 = (bf16[2,80,256]{2,1,0:T(8,128)(2,1)S(1)}, bf16[2,80,256]{2,1,0:T(8,128)(2,1)S(1)}, u32[]{:S(2)}, u32[]{:S(2)}) collective-permute-start(bf16[2,80,256]{2,1,0:T(8,128)(2,1)S(1)} %get-tuple-element.23), channel_id=1, source_target_pairs={{0,3},{1,2},{2,1},{3,0},{4,7},{5,6},{6,5},{7,4},{8,11},{9,10},{10,... | collective-permute-start | bytes 245768 | tf_op jit(solution)/shard_map/ppermute | solution.py:37
  14.7 0.0 collective-permute-done.6.cross_ref
  14.7 0.0 copy-done
  14.7 1.9 %shard_map.69.part_ref = f32[960,256]{1,0:T(8,128)S(1)} custom-call(bf16[2,2,80,256]{3,2,1,0:T(8,128)(2,1)S(1)} %get-tuple-element.20.edge_ref, bf16[4,80,256]{2,1,0:T(8,128)(2,1)S(1)} %get-tuple-element.21.early_ref, bf16[4,80,256]{2,1,0:T(8,128)(2,1)S(1)} %get-tuple-element.24.late_ref, bf16[2,80,256]{2,1,0:T(8,128)(2,1)S(1)} %collective-permute-done.5.mate_ref, ...), custom_call_target="tpu_custom_call" | custom-call | flops 1698693120 | bytes 5242880 | tf_op jit(solution)/shard_map/pallas_call | solution.py:303
  16.7 0.0 collective-permute-done.4.old_late_ref
  16.7 0.0 collective-permute-done.2.mate_ref
  16.7 0.7 %collective-permute-done.3.cross_ref = bf16[2,80,256]{2,1,0:T(8,128)(2,1)S(1)} collective-permute-done((bf16[2,80,256]{2,1,0:T(8,128)(2,1)S(1)}, bf16[2,80,256]{2,1,0:T(8,128)(2,1)S(1)}, u32[]{:S(2)}, u32[]{:S(2)}) %collective-permute-start.3) | collective-permute-done | bytes 81952 | tf_op jit(solution)/shard_map/ppermute | solution.py:37
  17.4 0.0 copy-done.1
  17.4 0.0 copy-done.3
  17.4 1.5 %shard_map.70 = (bf16[480,256]{1,0:T(8,128)(2,1)S(1)}, f32[480,256]{1,0:T(8,128)S(1)}, f32[256,384]{1,0:T(8,128)S(1)}) custom-call(bf16[2,2,80,256]{3,2,1,0:T(8,128)(2,1)S(1)} %get-tuple-element.20.edge_ref, bf16[4,80,256]{2,1,0:T(8,128)(2,1)S(1)} %get-tuple-element.24.late_ref, bf16[2,2,80,256]{3,2,1,0:T(8,128)(2,1)S(1)} %collective-permute-done.edge_ref.old_edge_ref, ...), custom_call_target="tpu_custom_call" | custom-call | flops 1258291200 | bytes 5242880 | tf_op jit(solution)/shard_map/pallas_call | solution.py:313
  19.0 0.0 collective-permute-done.1.old_early_ref
  19.0 1.5 %shard_map.71 = (bf16[480,256]{1,0:T(8,128)(2,1)S(1)}, f32[264,128]{1,0:T(8,128)S(1)}, f32[264,128]{1,0:T(8,128)S(1)}) custom-call(bf16[2,2,80,256]{3,2,1,0:T(8,128)(2,1)S(1)} %get-tuple-element.20.edge_ref, bf16[4,80,256]{2,1,0:T(8,128)(2,1)S(1)} %get-tuple-element.21.early_ref, bf16[2,2,80,256]{3,2,1,0:T(8,128)(2,1)S(1)} %collective-permute-done.edge_ref.old_edge_ref, ...), custom_call_target="tpu_custom_call" | custom-call | flops 629145600 | bytes 5242880 | tf_op jit(solution)/shard_map/pallas_call | solution.py:326
  20.5 0.5 %collective-permute-start.7 = (f32[264,128]{1,0:T(8,128)S(1)}, f32[264,128]{1,0:T(8,128)S(1)}, u32[]{:S(2)}, u32[]{:S(2)}) collective-permute-start(f32[264,128]{1,0:T(8,128)S(1)} %get-tuple-element.30), channel_id=1, source_target_pairs={{0,1},{1,0},{2,3},{3,2},{4,5},{5,4},{6,7},{7,6},{8,9},{9,8},{10,11... | collective-permute-start | bytes 405512 | tf_op jit(solution)/shard_map/ppermute | solution.py:37
  20.9 1.0 %collective-permute-done.7.got_ref = f32[264,128]{1,0:T(8,128)S(1)} collective-permute-done((f32[264,128]{1,0:T(8,128)S(1)}, f32[264,128]{1,0:T(8,128)S(1)}, u32[]{:S(2)}, u32[]{:S(2)}) %collective-permute-start.7) | collective-permute-done | bytes 135200 | tf_op jit(solution)/shard_map/ppermute | solution.py:37
  21.9 0.1 shard_map.72
  22.1 0.1 collective-permute-start.8
  22.2 2.8 %collective-permute-start.9 = (f16[272,128]{1,0:T(8,128)(2,1)S(1)}, f16[272,128]{1,0:T(8,128)(2,1)S(1)}, u32[]{:S(2)}, u32[]{:S(2)}) collective-permute-start(f16[272,128]{1,0:T(8,128)(2,1)S(1)} %convert_element_type.30), channel_id=1, source_target_pairs={{0,5},{1,16},{2,19},{3,6},{4,21},{5,0},{6,3},{7,22},{8,25},{9,12},... | collective-permute-start | bytes 208904 | tf_op jit(solution)/shard_map/ppermute | solution.py:37
  25.0 0.4 collective-permute-start.10
  25.3 0.8 %pad_maximum_fusion = bf16[2,480,256]{2,1,0:T(8,128)(2,1)} fusion(bf16[1,480,256]{2,1,0:T(8,128)(2,1)S(1)} %bitcast.24, bf16[1,480,256]{2,1,0:T(8,128)(2,1)S(1)} %bitcast.25), kind=kLoop, calls=%fused_computation | loop fusion | flops 245760 | bytes 983040 | tf_op jit(solution)/shard_map/stack | solution.py:334
  26.2 1.3 %collective-permute-done.8 = f16[272,128]{1,0:T(8,128)(2,1)S(1)} collective-permute-done((f16[272,128]{1,0:T(8,128)(2,1)S(1)}, f16[272,128]{1,0:T(8,128)(2,1)S(1)}, u32[]{:S(2)}, u32[]{:S(2)}) %collective-permute-start.8) | collective-permute-done | bytes 69664 | tf_op jit(solution)/shard_map/ppermute | solution.py:37
  27.5 0.3 collective-permute-done.9
  27.7 1.0 %collective-permute-done.10 = f16[272,128]{1,0:T(8,128)(2,1)S(1)} collective-permute-done((f16[272,128]{1,0:T(8,128)(2,1)S(1)}, f16[272,128]{1,0:T(8,128)(2,1)S(1)}, u32[]{:S(2)}, u32[]{:S(2)}) %collective-permute-start.10) | collective-permute-done | bytes 69664 | tf_op jit(solution)/shard_map/ppermute | solution.py:37
  28.8 0.1 select_convert_fusion
  28.9 1.2 %collective-permute-start.12 = (f16[272,128]{1,0:T(8,128)(2,1)S(1)}, f16[272,128]{1,0:T(8,128)(2,1)S(1)}, u32[]{:S(2)}, u32[]{:S(2)}) collective-permute-start(f16[272,128]{1,0:T(8,128)(2,1)S(1)} %select_convert_fusion), channel_id=1, source_target_pairs={{0,17},{1,4},{2,7},{3,18},{4,1},{5,20},{6,23},{7,2},{8,13},{9,24},... | collective-permute-start | bytes 208904 | tf_op jit(solution)/shard_map/ppermute | solution.py:37
  30.1 1.2 %collective-permute-start.11 = (f16[272,128]{1,0:T(8,128)(2,1)S(1)}, f16[272,128]{1,0:T(8,128)(2,1)S(1)}, u32[]{:S(2)}, u32[]{:S(2)}) collective-permute-start(f16[272,128]{1,0:T(8,128)(2,1)S(1)} %select_convert_fusion), channel_id=1, source_target_pairs={{0,24},{1,7},{2,4},{3,27},{4,2},{5,29},{6,30},{7,1},{8,14},{9,17},... | collective-permute-start | bytes 208904 | tf_op jit(solution)/shard_map/ppermute | solution.py:37
  31.3 0.6 %collective-permute-start.13 = (f16[272,128]{1,0:T(8,128)(2,1)S(1)}, f16[272,128]{1,0:T(8,128)(2,1)S(1)}, u32[]{:S(2)}, u32[]{:S(2)}) collective-permute-start(f16[272,128]{1,0:T(8,128)(2,1)S(1)} %select_convert_fusion), channel_id=1, source_target_pairs={{0,9},{1,2},{2,1},{3,10},{4,7},{5,12},{6,15},{7,4},{8,11},{9,0},{1... | collective-permute-start | bytes 208904 | tf_op jit(solution)/shard_map/ppermute | solution.py:37
  31.9 2.4 %collective-permute-done.12 = f16[272,128]{1,0:T(8,128)(2,1)S(1)} collective-permute-done((f16[272,128]{1,0:T(8,128)(2,1)S(1)}, f16[272,128]{1,0:T(8,128)(2,1)S(1)}, u32[]{:S(2)}, u32[]{:S(2)}) %collective-permute-start.12) | collective-permute-done | bytes 69664 | tf_op jit(solution)/shard_map/ppermute | solution.py:37
  34.3 1.9 %collective-permute-done.11 = f16[272,128]{1,0:T(8,128)(2,1)S(1)} collective-permute-done((f16[272,128]{1,0:T(8,128)(2,1)S(1)}, f16[272,128]{1,0:T(8,128)(2,1)S(1)}, u32[]{:S(2)}, u32[]{:S(2)}) %collective-permute-start.11) | collective-permute-done | bytes 69664 | tf_op jit(solution)/shard_map/ppermute | solution.py:37
  36.2 0.0 collective-permute-done.13
  36.3 0.5 %collective-permute-start.14 = (f32[264,128]{1,0:T(8,128)S(1)}, f32[264,128]{1,0:T(8,128)S(1)}, u32[]{:S(2)}, u32[]{:S(2)}) collective-permute-start(f32[264,128]{1,0:T(8,128)S(1)} %fusion.1.mine_ref), channel_id=1, source_target_pairs={{0,1},{1,0},{2,3},{3,2},{4,5},{5,4},{6,7},{7,6},{8,9},{9,8},{10,11... | collective-permute-start | bytes 405512 | tf_op jit(solution)/shard_map/ppermute | solution.py:37
  36.9 1.0 %collective-permute-done.14.other_ref = f32[264,128]{1,0:T(8,128)S(1)} collective-permute-done((f32[264,128]{1,0:T(8,128)S(1)}, f32[264,128]{1,0:T(8,128)S(1)}, u32[]{:S(2)}, u32[]{:S(2)}) %collective-permute-start.14) | collective-permute-done | bytes 135200 | tf_op jit(solution)/shard_map/ppermute | solution.py:37
  37.9 0.8 %shard_map.73 = (f32[256,256]{1,0:T(8,128)}, f32[256,128]{1,0:T(8,128)}) custom-call(f32[264,128]{1,0:T(8,128)S(1)} %fusion.1.mine_ref, f32[264,128]{1,0:T(8,128)S(1)} %collective-permute-done.14.other_ref), custom_call_target="tpu_custom_call" | custom-call | tf_op jit(solution)/shard_map/pallas_call | solution.py:338
  (19 shorter events, 0.3 us)
Async XLA Ops:
  0.6 1.0 %copy-start.2 = (bf16[2,6,80,256]{3,2,1,0:T(8,128)(2,1)S(1)}, bf16[2,6,80,256]{3,2,1,0:T(8,128)(2,1)}, u32[]{:S(2)}) copy-start(bf16[2,6,80,256]{3,2,1,0:T(8,128)(2,1)} %latents_ref.1) | copy-start | bytes 1474564
  1.7 10.5 %collective-permute-start = (bf16[2,2,80,256]{3,2,1,0:T(8,128)(2,1)S(1)}, bf16[2,2,80,256]{3,2,1,0:T(8,128)(2,1)S(1)}, u32[]{:S(2)}, u32[]{:S(2)}) collective-permute-start(bf16[2,2,80,256]{3,2,1,0:T(8,128)(2,1)S(1)} %get-tuple-element.20.edge_ref), channel_id=1, source_target_pairs={{0,4},{4,8},{8,12},{12,16},{16,20},{20,24},{24,28},{28,0},{1,5},{5... | collective-permute-start | bytes 491528 | tf_op jit(solution)/shard_map/ppermute | solution.py:42
  4.7 7.6 %collective-permute-start.5 = (bf16[2,80,256]{2,1,0:T(8,128)(2,1)S(1)}, bf16[2,80,256]{2,1,0:T(8,128)(2,1)S(1)}, u32[]{:S(2)}, u32[]{:S(2)}) collective-permute-start(bf16[2,80,256]{2,1,0:T(8,128)(2,1)S(1)} %get-tuple-element.25), channel_id=1, source_target_pairs={{0,1},{1,0},{2,3},{3,2},{4,5},{5,4},{6,7},{7,6},{8,9},{9,8},{10,11... | collective-permute-start | bytes 245768 | tf_op jit(solution)/shard_map/ppermute | solution.py:37
  4.7 10.0 %collective-permute-start.6 = (bf16[2,80,256]{2,1,0:T(8,128)(2,1)S(1)}, bf16[2,80,256]{2,1,0:T(8,128)(2,1)S(1)}, u32[]{:S(2)}, u32[]{:S(2)}) collective-permute-start(bf16[2,80,256]{2,1,0:T(8,128)(2,1)S(1)} %get-tuple-element.26), channel_id=1, source_target_pairs={{0,3},{1,2},{2,1},{3,0},{4,7},{5,6},{6,5},{7,4},{8,11},{9,10},{10,... | collective-permute-start | bytes 245768 | tf_op jit(solution)/shard_map/ppermute | solution.py:37
  6.3 10.3 %collective-permute-start.4 = (bf16[4,80,256]{2,1,0:T(8,128)(2,1)S(1)}, bf16[4,80,256]{2,1,0:T(8,128)(2,1)S(1)}, u32[]{:S(2)}, u32[]{:S(2)}) collective-permute-start(bf16[4,80,256]{2,1,0:T(8,128)(2,1)S(1)} %get-tuple-element.24.late_ref), channel_id=1, source_target_pairs={{0,4},{4,8},{8,12},{12,16},{16,20},{20,24},{24,28},{28,0},{1,5},{5... | collective-permute-start | bytes 491528 | tf_op jit(solution)/shard_map/ppermute | solution.py:42
  7.9 6.9 %copy-start = (bf16[3,3,768,256]{3,2,1,0:T(8,128)(2,1)S(1)}, bf16[3,3,768,256]{3,2,1,0:T(8,128)(2,1)}, u32[]{:S(2)}) copy-start(bf16[3,3,768,256]{3,2,1,0:T(8,128)(2,1)} %weight_ref.5) | copy-start | bytes 10616836
  7.9 11.1 %collective-permute-start.1 = (bf16[4,80,256]{2,1,0:T(8,128)(2,1)S(1)}, bf16[4,80,256]{2,1,0:T(8,128)(2,1)S(1)}, u32[]{:S(2)}, u32[]{:S(2)}) collective-permute-start(bf16[4,80,256]{2,1,0:T(8,128)(2,1)S(1)} %get-tuple-element.21.early_ref), channel_id=1, source_target_pairs={{0,4},{4,8},{8,12},{12,16},{16,20},{20,24},{24,28},{28,0},{1,5},{5... | collective-permute-start | bytes 491528 | tf_op jit(solution)/shard_map/ppermute | solution.py:42
  12.2 5.2 %copy-start.1 = (bf16[2,6,80,128]{3,2,1,0:T(8,128)(2,1)S(1)}, bf16[2,6,80,128]{3,2,1,0:T(8,128)(2,1)}, u32[]{:S(2)}) copy-start(bf16[2,6,80,128]{3,2,1,0:T(8,128)(2,1)} %param.7) | copy-start | bytes 737284
  12.3 5.2 %copy-start.3 = (f32[256]{0:T(256)S(1)}, f32[256]{0:T(256)}, u32[]{:S(2)}) copy-start(f32[256]{0:T(256)} %param.6) | copy-start | bytes 3076
  12.3 4.4 %collective-permute-start.2 = (bf16[2,80,256]{2,1,0:T(8,128)(2,1)S(1)}, bf16[2,80,256]{2,1,0:T(8,128)(2,1)S(1)}, u32[]{:S(2)}, u32[]{:S(2)}) collective-permute-start(bf16[2,80,256]{2,1,0:T(8,128)(2,1)S(1)} %get-tuple-element.22), channel_id=1, source_target_pairs={{0,1},{1,0},{2,3},{3,2},{4,5},{5,4},{6,7},{7,6},{8,9},{9,8},{10,11... | collective-permute-start | bytes 245768 | tf_op jit(solution)/shard_map/ppermute | solution.py:37
  12.4 5.1 %collective-permute-start.3 = (bf16[2,80,256]{2,1,0:T(8,128)(2,1)S(1)}, bf16[2,80,256]{2,1,0:T(8,128)(2,1)S(1)}, u32[]{:S(2)}, u32[]{:S(2)}) collective-permute-start(bf16[2,80,256]{2,1,0:T(8,128)(2,1)S(1)} %get-tuple-element.23), channel_id=1, source_target_pairs={{0,3},{1,2},{2,1},{3,0},{4,7},{5,6},{6,5},{7,4},{8,11},{9,10},{10,... | collective-permute-start | bytes 245768 | tf_op jit(solution)/shard_map/ppermute | solution.py:37
  20.5 1.5 %collective-permute-start.7 = (f32[264,128]{1,0:T(8,128)S(1)}, f32[264,128]{1,0:T(8,128)S(1)}, u32[]{:S(2)}, u32[]{:S(2)}) collective-permute-start(f32[264,128]{1,0:T(8,128)S(1)} %get-tuple-element.30), channel_id=1, source_target_pairs={{0,1},{1,0},{2,3},{3,2},{4,5},{5,4},{6,7},{7,6},{8,9},{9,8},{10,11... | collective-permute-start | bytes 405512 | tf_op jit(solution)/shard_map/ppermute | solution.py:37
  22.1 5.4 %collective-permute-start.8 = (f16[272,128]{1,0:T(8,128)(2,1)S(1)}, f16[272,128]{1,0:T(8,128)(2,1)S(1)}, u32[]{:S(2)}, u32[]{:S(2)}) collective-permute-start(f16[272,128]{1,0:T(8,128)(2,1)S(1)} %convert_element_type.30), channel_id=1, source_target_pairs={{0,6},{1,25},{2,26},{3,5},{4,28},{5,3},{6,0},{7,31},{8,16},{9,15},... | collective-permute-start | bytes 208904 | tf_op jit(solution)/shard_map/ppermute | solution.py:37
  22.2 5.6 %collective-permute-start.9 = (f16[272,128]{1,0:T(8,128)(2,1)S(1)}, f16[272,128]{1,0:T(8,128)(2,1)S(1)}, u32[]{:S(2)}, u32[]{:S(2)}) collective-permute-start(f16[272,128]{1,0:T(8,128)(2,1)S(1)} %convert_element_type.30), channel_id=1, source_target_pairs={{0,5},{1,16},{2,19},{3,6},{4,21},{5,0},{6,3},{7,22},{8,25},{9,12},... | collective-permute-start | bytes 208904 | tf_op jit(solution)/shard_map/ppermute | solution.py:37
  25.0 3.7 %collective-permute-start.10 = (f16[272,128]{1,0:T(8,128)(2,1)S(1)}, f16[272,128]{1,0:T(8,128)(2,1)S(1)}, u32[]{:S(2)}, u32[]{:S(2)}) collective-permute-start(f16[272,128]{1,0:T(8,128)(2,1)S(1)} %convert_element_type.30), channel_id=1, source_target_pairs={{0,3},{1,8},{2,11},{3,0},{4,13},{5,6},{6,5},{7,14},{8,1},{9,10},{1... | collective-permute-start | bytes 208904 | tf_op jit(solution)/shard_map/ppermute | solution.py:37
  28.9 5.4 %collective-permute-start.12 = (f16[272,128]{1,0:T(8,128)(2,1)S(1)}, f16[272,128]{1,0:T(8,128)(2,1)S(1)}, u32[]{:S(2)}, u32[]{:S(2)}) collective-permute-start(f16[272,128]{1,0:T(8,128)(2,1)S(1)} %select_convert_fusion), channel_id=1, source_target_pairs={{0,17},{1,4},{2,7},{3,18},{4,1},{5,20},{6,23},{7,2},{8,13},{9,24},... | collective-permute-start | bytes 208904 | tf_op jit(solution)/shard_map/ppermute | solution.py:37
  30.1 6.1 %collective-permute-start.11 = (f16[272,128]{1,0:T(8,128)(2,1)S(1)}, f16[272,128]{1,0:T(8,128)(2,1)S(1)}, u32[]{:S(2)}, u32[]{:S(2)}) collective-permute-start(f16[272,128]{1,0:T(8,128)(2,1)S(1)} %select_convert_fusion), channel_id=1, source_target_pairs={{0,24},{1,7},{2,4},{3,27},{4,2},{5,29},{6,30},{7,1},{8,14},{9,17},... | collective-permute-start | bytes 208904 | tf_op jit(solution)/shard_map/ppermute | solution.py:37
  31.3 5.0 %collective-permute-start.13 = (f16[272,128]{1,0:T(8,128)(2,1)S(1)}, f16[272,128]{1,0:T(8,128)(2,1)S(1)}, u32[]{:S(2)}, u32[]{:S(2)}) collective-permute-start(f16[272,128]{1,0:T(8,128)(2,1)S(1)} %select_convert_fusion), channel_id=1, source_target_pairs={{0,9},{1,2},{2,1},{3,10},{4,7},{5,12},{6,15},{7,4},{8,11},{9,0},{1... | collective-permute-start | bytes 208904 | tf_op jit(solution)/shard_map/ppermute | solution.py:37
  36.3 1.5 %collective-permute-start.14 = (f32[264,128]{1,0:T(8,128)S(1)}, f32[264,128]{1,0:T(8,128)S(1)}, u32[]{:S(2)}, u32[]{:S(2)}) collective-permute-start(f32[264,128]{1,0:T(8,128)S(1)} %fusion.1.mine_ref), channel_id=1, source_target_pairs={{0,1},{1,0},{2,3},{3,2},{4,5},{5,4},{6,7},{7,6},{8,9},{9,8},{10,11... | collective-permute-start | bytes 405512 | tf_op jit(solution)/shard_map/ppermute | solution.py:37

commit v6 on v5

--- a/solution.py
+++ b/solution.py
@@ -28,8 +28,27 @@
     return value & 1
 
 
+def rounds_of_flips():
+    blocks, rows = lax.axis_size("tm"), lax.axis_size("row")
+    bits = [(0, 2**k) for k in range(1, rows.bit_length() - 1)]
+    bits += [(2**k, 0) for k in range(blocks.bit_length() - 1)]
+    rounds = []
+    for i in range(0, len(bits), 2):
+        flips = bits[i : i + 2]
+        if len(flips) == 2:
+            flips.append((flips[0][0] ^ flips[1][0], flips[0][1] ^ flips[1][1]))
+        rounds.append(flips)
+    return rounds
+
+
+def side(a, b):
+    counted = [flips[min(1, len(flips) - 1)] for flips in rounds_of_flips()]
+    tm, row = sum(c for c, _ in counted), 1 + sum(d for _, d in counted)
+    return odd_bits(a & tm) ^ odd_bits(b & row)
+
+
 def has_low():
-    return odd_bits(lax.axis_index("tm") ^ lax.axis_index("row")) == 0
+    return side(lax.axis_index("tm"), lax.axis_index("row")) == 0
 
 
 def by_device(value, moves):
@@ -93,10 +112,8 @@
     return products
 
 
-def stacked_rows(rows, cols):
-    wide = jnp.concatenate(rows, axis=0)
-    span = wide.shape[0] - 2 * cols
-    return jnp.concatenate([wide[tap * cols : tap * cols + span] for tap in range(3)], axis=1)
+def stacked_rows(wide, start, span, cols):
+    return jnp.concatenate([wide[start + tap * cols : start + tap * cols + span] for tap in range(3)], axis=1)
 
 
 def joined_columns(products, cols):
@@ -108,30 +125,36 @@
     return left + middle + right
 
 
-def padded_stack(edge_ref, middle_ref, mate_ref, cross_ref, f):
+def padded_frame(edge_ref, middle_ref, mate_ref, cross_ref, f):
     above, below = rims(mate_ref, cross_ref, f)
-    return stacked_rows([above, *frame_rows(edge_ref, middle_ref, f), below], edge_ref.shape[2])
+    return jnp.concatenate([above, *frame_rows(edge_ref, middle_ref, f), below], axis=0)
 
 
 def own_kernel(edge_ref, early_ref, late_ref, mate_ref, cross_ref, weight_ref, part_ref):
     cols, chans = edge_ref.shape[2:]
     span = part_ref.shape[0] // 2
-    early = padded_stack(edge_ref, early_ref, mate_ref, cross_ref, 0)
-    late = padded_stack(edge_ref, late_ref, mate_ref, cross_ref, 1)
+    early = stacked_rows(padded_frame(edge_ref, early_ref, mate_ref, cross_ref, 0), 0, span, cols)
+    late = stacked_rows(padded_frame(edge_ref, late_ref, mate_ref, cross_ref, 1), 0, span, cols)
     part_ref[:span] = joined_columns(column_taps([early], weight_ref, [2], chans), cols)
     part_ref[span:] = joined_columns(column_taps([early, late], weight_ref, [1, 2], chans), cols)
 
 
-def older_terms(stack, weight_ref, time, cols, chans):
-    terms = joined_columns(column_taps([stack], weight_ref, [time], chans), cols)
+def older_terms(wide, start, span, weight_ref, time, cols):
+    stack = stacked_rows(wide, start, span, cols)
+    terms = joined_columns(column_taps([stack], weight_ref, [time], wide.shape[1]), cols)
     return jnp.where(lax.axis_index("tm") == 0, 0.0, terms)
 
 
-def features_of(conv, own_rows, gain_ref):
+def chunks_of(span, cols):
+    size = span // 2 if span % (2 * cols) == 0 else span
+    return [(start, size) for start in range(0, span, size)]
+
+
+def features_of(conv, own, gain_ref):
     mean = jnp.mean(conv * conv, axis=1, keepdims=True)
     normed = conv * lax.rsqrt(mean + 1e-06) * gain_ref[...]
     silu = 0.5 * normed * (1.0 + jnp.tanh(0.5 * normed))
-    return (jnp.concatenate(own_rows, axis=0).astype(F32) + silu).astype(BF16)
+    return (own.astype(F32) + silu).astype(BF16)
 
 
 def moments(features, targets):
@@ -139,27 +162,37 @@
     return jnp.dot(features.T, both, preferred_element_type=F32)
 
 
-def late_kernel(edge_ref, late_ref, old_edge_ref, old_late_ref, mate_ref, cross_ref, weight_ref, part_ref, gain_ref,
+def late_kernel(edge_ref, late_ref, old_edge_ref, old_late_ref, cross_ref, mate_ref, weight_ref, part_ref, gain_ref,
                 target_ref, feature_ref, more_ref, sums_ref):
     cols, chans = edge_ref.shape[2:]
     span = part_ref.shape[0] // 2
-    stack = padded_stack(old_edge_ref, old_late_ref, mate_ref, cross_ref, 1)
-    conv = part_ref[span:] + older_terms(stack, weight_ref, 0, cols, chans)
-    features = features_of(conv, frame_rows(edge_ref, late_ref, 1), gain_ref)
-    feature_ref[...] = features
-    more_ref[...] = part_ref[:span] + older_terms(stack, weight_ref, 1, cols, chans)
-    sums_ref[...] = moments(features, target_ref[span:])
-
-
-def early_kernel(edge_ref, early_ref, old_edge_ref, old_early_ref, mate_ref, cross_ref, weight_ref, more_ref, sums_ref,
+    wide = padded_frame(old_edge_ref, old_late_ref, mate_ref, cross_ref, 1)
+    own = jnp.concatenate(frame_rows(edge_ref, late_ref, 1), axis=0)
+    chunks = chunks_of(span, cols)
+    older = [older_terms(wide, start, size, weight_ref, 0, cols) for start, size in chunks]
+    more_ref[...] = part_ref[:span] + older_terms(wide, 0, span, weight_ref, 1, cols)
+    sums = jnp.zeros(sums_ref.shape, F32)
+    for (start, size), terms in zip(chunks, older):
+        conv = part_ref[span + start : span + start + size] + terms
+        features = features_of(conv, own[start : start + size], gain_ref)
+        feature_ref[start : start + size] = features
+        sums = sums + moments(features, target_ref[span + start : span + start + size])
+    sums_ref[...] = sums
+
+
+def early_kernel(edge_ref, early_ref, old_edge_ref, old_early_ref, cross_ref, mate_ref, weight_ref, more_ref, sums_ref,
                  gain_ref, target_ref, feature_ref, keep_ref, send_ref):
     cols, chans = edge_ref.shape[2:]
     span, half = more_ref.shape[0], chans // 2
-    stack = padded_stack(old_edge_ref, old_early_ref, mate_ref, cross_ref, 0)
-    conv = more_ref[...] + older_terms(stack, weight_ref, 0, cols, chans)
-    features = features_of(conv, frame_rows(edge_ref, early_ref, 0), gain_ref)
-    feature_ref[...] = features
-    sums = sums_ref[...] + moments(features, target_ref[:span])
+    wide = padded_frame(old_edge_ref, old_early_ref, mate_ref, cross_ref, 0)
+    own = jnp.concatenate(frame_rows(edge_ref, early_ref, 0), axis=0)
+    chunks = chunks_of(span, cols)
+    older = [older_terms(wide, start, size, weight_ref, 0, cols) for start, size in chunks]
+    sums = sums_ref[...]
+    for (start, size), terms in zip(chunks, older):
+        features = features_of(more_ref[start : start + size] + terms, own[start : start + size], gain_ref)
+        feature_ref[start : start + size] = features
+        sums = sums + moments(features, target_ref[start : start + size])
     row = lax.broadcasted_iota(jnp.int32, (half, half), 0)
     col = lax.broadcasted_iota(jnp.int32, (half, half), 1)
     head, tail = sums[:half, :half], sums[half:, half:chans]
@@ -243,15 +276,7 @@
 
 
 def total_over_chips(keep, got):
-    blocks, rows = lax.axis_size("tm"), lax.axis_size("row")
-    bits = [(0, 2**k) for k in range(1, rows.bit_length() - 1)]
-    bits += [(2**k, 0) for k in range(blocks.bit_length() - 1)]
-    rounds = []
-    for i in range(0, len(bits), 2):
-        flips = bits[i : i + 2]
-        if len(flips) == 2:
-            flips.append((flips[0][0] ^ flips[1][0], flips[0][1] ^ flips[1][1]))
-        rounds.append(flips)
+    rounds = rounds_of_flips()
     size, lanes = keep.shape
     value = pl.pallas_call(
         pack_kernel,
@@ -267,8 +292,8 @@
         for pair in zip(flips, other):
             moves = []
             for a, b in places():
-                c, d = pair[odd_bits(a ^ b)]
-                moves.append(((a, b), (a ^ c, b ^ d ^ odd_bits(c ^ d))))
+                c, d = pair[side(a, b)]
+                moves.append(((a, b), (a ^ c, b ^ d ^ side(c, d))))
             messages.append(by_device(value, moves))
         value = joined_messages(messages[::-1], s == len(rounds) - 1)
     return value
@@ -321,7 +346,7 @@
         out_specs=(WHOLE,) * 3,
         compiler_params=params(24),
         cost_estimate=pl.CostEstimate(flops=spots * chans * chans * 20, bytes_accessed=5 * 2**20, transcendentals=spots * chans // 2),
-    )(edge, late, old_edge, old_late, old_mate, old_cross, conv_weight, part, gain, targets)
+    )(edge, late, old_edge, old_late, old_cross, old_mate, conv_weight, part, gain, targets)
     share = jax.ShapeDtypeStruct((2 * half + HEAD // 2, half), F32)
     early_features, keep, send = pl.pallas_call(
         early_kernel,
@@ -330,7 +355,7 @@
         out_specs=(WHOLE,) * 3,
         compiler_params=params(24),
         cost_estimate=pl.CostEstimate(flops=spots * chans * chans * 10, bytes_accessed=5 * 2**20, transcendentals=spots * chans // 2),
-    )(edge, early, old_edge, old_early, old_mate, old_cross, conv_weight, more, sums, gain, targets)
+    )(edge, early, old_edge, old_early, old_cross, old_mate, conv_weight, more, sums, gain, targets)
     features = jnp.stack([early_features, late_features])
     mine = total_over_chips(keep, with_mate(send))
     mine, features = lax.optimization_barrier((mine, features))

time: 38.9 us -> 38 us (0.977)
  starting transfers between devices: 17.4 us -> 16.7 us
    ppermute x12, waiting for transfers between devices: 9.5 us -> 8.75 us  [by_device(): lax.ppermute(value, ('tm', 'row'), [(a * rows + b, c * rows + d) for (a,...]
    ppermute x3, waiting for transfers between devices: 2.86 us -> 3.55 us  [later(): lax.ppermute(value, 'tm', [(i, (i + 1) % count) for i in range(count)])]
    ppermute x12, starting transfers between devices: 11.3 us -> 10.7 us  [by_device(): lax.ppermute(value, ('tm', 'row'), [(a * rows + b, c * rows + d) for (a,...]
  transfers between devices with their start and end apart: 15 -> 15, of which waited for: 9 -> 10; matrix products, arithmetic and copies ran while one was open for 2% -> 2% of each run, Pallas kernels for 9% -> 9%
where the time goes in v6:
time: 38 us; the launch traced here: 37.8 us
  starting transfers between devices  16.7 us (44%)
  waiting for transfers between devices  12.3 us (32%)
  Pallas kernels  5.72 us (15%)
  other arithmetic  1.14 us (3%)
  local copies, waits for them, and re-layouts  1.04 us (3%)
  between operations  0.89 us (2%)
    ppermute x12, starting transfers between devices, by_device(): lax.ppermute(value, ('tm', 'row'), [(a * rows + b, c * rows + d) for (a,...  10.7 us
    ppermute x12, waiting for transfers between devices, by_device(): lax.ppermute(value, ('tm', 'row'), [(a * rows + b, c * rows + d) for (a,...  8.75 us
    ppermute x3, starting transfers between devices, later(): lax.ppermute(value, 'tm', [(i, (i + 1) % count) for i in range(count)])  6.06 us
    ppermute x3, waiting for transfers between devices, later(): lax.ppermute(value, 'tm', [(i, (i + 1) % count) for i in range(count)])  3.55 us
    pallas_call x1, Pallas kernels, on_device(): pl.pallas_call(own_kernel, out_shape=jax.ShapeDtypeStruct((spots, chans),...  1.95 us
    pallas_call x1, Pallas kernels, on_device(): pl.pallas_call(late_kernel, out_shape=(half_features, jax.ShapeDtypeStruc...  1.56 us
    pallas_call x1, Pallas kernels, on_device(): pl.pallas_call(early_kernel, out_shape=(half_features, share, share), in_...  1.19 us
    unnamed x8, local copies, waits for them, and re-layouts  1.04 us
  transfers between devices with their start and end apart: 15, of which 10 were waited for; matrix products, arithmetic and copies ran while one was open for 2% of the time, Pallas kernels for 9%

profile of v6, /device:TPU:0, one launch (start us, length us, event | category | flops | bytes accessed | tf_op | source)
XLA Modules:
  0.0 37.8 jit_solution(8052420370387225503)
XLA Ops:
  0.6 0.0 copy-start.2
  0.6 1.0 %copy-done.2 = bf16[2,6,80,256]{3,2,1,0:T(8,128)(2,1)S(1)} copy-done((bf16[2,6,80,256]{3,2,1,0:T(8,128)(2,1)S(1)}, bf16[2,6,80,256]{3,2,1,0:T(8,128)(2,1)}, u32[]{:S(2)}) %copy-start.2) | copy-done | bytes 491544
  1.7 3.0 %collective-permute-start = (bf16[2,2,80,256]{3,2,1,0:T(8,128)(2,1)S(1)}, bf16[2,2,80,256]{3,2,1,0:T(8,128)(2,1)S(1)}, u32[]{:S(2)}, u32[]{:S(2)}) collective-permute-start(bf16[2,2,80,256]{3,2,1,0:T(8,128)(2,1)S(1)} %get-tuple-element.20.edge_ref), channel_id=1, source_target_pairs={{0,4},{4,8},{8,12},{12,16},{16,20},{20,24},{24,28},{28,0},{1,5},{5... | collective-permute-start | bytes 491528 | tf_op jit(solution)/shard_map/ppermute | solution.py:61
  4.7 0.0 collective-permute-start.5
  4.7 1.6 %collective-permute-start.6 = (bf16[2,80,256]{2,1,0:T(8,128)(2,1)S(1)}, bf16[2,80,256]{2,1,0:T(8,128)(2,1)S(1)}, u32[]{:S(2)}, u32[]{:S(2)}) collective-permute-start(bf16[2,80,256]{2,1,0:T(8,128)(2,1)S(1)} %get-tuple-element.26), channel_id=1, source_target_pairs={{0,3},{1,2},{2,1},{3,0},{4,7},{5,6},{6,5},{7,4},{8,11},{9,10},{10,... | collective-permute-start | bytes 245768 | tf_op jit(solution)/shard_map/ppermute | solution.py:56
  6.3 1.5 %collective-permute-start.4 = (bf16[4,80,256]{2,1,0:T(8,128)(2,1)S(1)}, bf16[4,80,256]{2,1,0:T(8,128)(2,1)S(1)}, u32[]{:S(2)}, u32[]{:S(2)}) collective-permute-start(bf16[4,80,256]{2,1,0:T(8,128)(2,1)S(1)} %get-tuple-element.24.late_ref), channel_id=1, source_target_pairs={{0,4},{4,8},{8,12},{12,16},{16,20},{20,24},{24,28},{28,0},{1,5},{5... | collective-permute-start | bytes 491528 | tf_op jit(solution)/shard_map/ppermute | solution.py:61
  7.9 0.0 copy-start
  7.9 1.5 %collective-permute-start.1 = (bf16[4,80,256]{2,1,0:T(8,128)(2,1)S(1)}, bf16[4,80,256]{2,1,0:T(8,128)(2,1)S(1)}, u32[]{:S(2)}, u32[]{:S(2)}) collective-permute-start(bf16[4,80,256]{2,1,0:T(8,128)(2,1)S(1)} %get-tuple-element.21.early_ref), channel_id=1, source_target_pairs={{0,4},{4,8},{8,12},{12,16},{16,20},{20,24},{24,28},{28,0},{1,5},{5... | collective-permute-start | bytes 491528 | tf_op jit(solution)/shard_map/ppermute | solution.py:61
  9.4 2.8 %collective-permute-done.edge_ref.old_edge_ref = bf16[2,2,80,256]{3,2,1,0:T(8,128)(2,1)S(1)} collective-permute-done((bf16[2,2,80,256]{3,2,1,0:T(8,128)(2,1)S(1)}, bf16[2,2,80,256]{3,2,1,0:T(8,128)(2,1)S(1)}, u32[]{:S(2)}, u32[]{:S(2)}) %collective-permute-start) | collective-permute-done | bytes 163872 | tf_op jit(solution)/shard_map/ppermute | solution.py:61
  12.2 0.0 copy-start.1
  12.3 0.0 copy-start.3
  12.3 0.1 collective-permute-start.2
  12.4 0.0 collective-permute-done.5.mate_ref
  12.4 2.3 %collective-permute-start.3 = (bf16[2,80,256]{2,1,0:T(8,128)(2,1)S(1)}, bf16[2,80,256]{2,1,0:T(8,128)(2,1)S(1)}, u32[]{:S(2)}, u32[]{:S(2)}) collective-permute-start(bf16[2,80,256]{2,1,0:T(8,128)(2,1)S(1)} %get-tuple-element.23), channel_id=1, source_target_pairs={{0,1},{1,0},{2,3},{3,2},{4,5},{5,4},{6,7},{7,6},{8,9},{9,8},{10,11... | collective-permute-start | bytes 245768 | tf_op jit(solution)/shard_map/ppermute | solution.py:56
  14.7 0.0 collective-permute-done.6.cross_ref
  14.7 0.0 copy-done
  14.7 1.9 %shard_map.69.part_ref = f32[960,256]{1,0:T(8,128)S(1)} custom-call(bf16[2,2,80,256]{3,2,1,0:T(8,128)(2,1)S(1)} %get-tuple-element.20.edge_ref, bf16[4,80,256]{2,1,0:T(8,128)(2,1)S(1)} %get-tuple-element.21.early_ref, bf16[4,80,256]{2,1,0:T(8,128)(2,1)S(1)} %get-tuple-element.24.late_ref, bf16[2,80,256]{2,1,0:T(8,128)(2,1)S(1)} %collective-permute-done.5.mate_ref, ...), custom_call_target="tpu_custom_call" | custom-call | flops 1698693120 | bytes 5242880 | tf_op jit(solution)/shard_map/pallas_call | solution.py:328
  16.7 0.0 collective-permute-done.4.old_late_ref
  16.7 0.0 collective-permute-done.2.cross_ref
  16.7 0.0 collective-permute-done.3.mate_ref
  16.7 0.0 copy-done.1
  16.7 0.0 copy-done.3
  16.7 1.6 %shard_map.70 = (bf16[480,256]{1,0:T(8,128)(2,1)S(1)}, f32[480,256]{1,0:T(8,128)S(1)}, f32[256,384]{1,0:T(8,128)S(1)}) custom-call(bf16[2,2,80,256]{3,2,1,0:T(8,128)(2,1)S(1)} %get-tuple-element.20.edge_ref, bf16[4,80,256]{2,1,0:T(8,128)(2,1)S(1)} %get-tuple-element.24.late_ref, bf16[2,2,80,256]{3,2,1,0:T(8,128)(2,1)S(1)} %collective-permute-done.edge_ref.old_edge_ref, ...), custom_call_target="tpu_custom_call" | custom-call | flops 1258291200 | bytes 5242880 | tf_op jit(solution)/shard_map/pallas_call | solution.py:338
  18.3 0.7 %collective-permute-done.1.old_early_ref = bf16[4,80,256]{2,1,0:T(8,128)(2,1)S(1)} collective-permute-done((bf16[4,80,256]{2,1,0:T(8,128)(2,1)S(1)}, bf16[4,80,256]{2,1,0:T(8,128)(2,1)S(1)}, u32[]{:S(2)}, u32[]{:S(2)}) %collective-permute-start.1) | collective-permute-done | bytes 163872 | tf_op jit(solution)/shard_map/ppermute | solution.py:61
  19.0 1.2 %shard_map.71 = (bf16[480,256]{1,0:T(8,128)(2,1)S(1)}, f32[264,128]{1,0:T(8,128)S(1)}, f32[264,128]{1,0:T(8,128)S(1)}) custom-call(bf16[2,2,80,256]{3,2,1,0:T(8,128)(2,1)S(1)} %get-tuple-element.20.edge_ref, bf16[4,80,256]{2,1,0:T(8,128)(2,1)S(1)} %get-tuple-element.21.early_ref, bf16[2,2,80,256]{3,2,1,0:T(8,128)(2,1)S(1)} %collective-permute-done.edge_ref.old_edge_ref, ...), custom_call_target="tpu_custom_call" | custom-call | flops 629145600 | bytes 5242880 | tf_op jit(solution)/shard_map/pallas_call | solution.py:351
  20.2 0.1 collective-permute-start.7
  20.3 1.3 %collective-permute-done.7.got_ref = f32[264,128]{1,0:T(8,128)S(1)} collective-permute-done((f32[264,128]{1,0:T(8,128)S(1)}, f32[264,128]{1,0:T(8,128)S(1)}, u32[]{:S(2)}, u32[]{:S(2)}) %collective-permute-start.7) | collective-permute-done | bytes 135200 | tf_op jit(solution)/shard_map/ppermute | solution.py:56
  21.6 0.1 shard_map.72
  21.8 0.1 collective-permute-start.8
  21.8 2.7 %collective-permute-start.9 = (f16[272,128]{1,0:T(8,128)(2,1)S(1)}, f16[272,128]{1,0:T(8,128)(2,1)S(1)}, u32[]{:S(2)}, u32[]{:S(2)}) collective-permute-start(f16[272,128]{1,0:T(8,128)(2,1)S(1)} %convert_element_type.30), channel_id=1, source_target_pairs={{0,5},{1,16},{2,7},{3,18},{4,21},{5,0},{6,23},{7,2},{8,13},{9,24},... | collective-permute-start | bytes 208904 | tf_op jit(solution)/shard_map/ppermute | solution.py:56
  24.5 0.5 %collective-permute-start.10 = (f16[272,128]{1,0:T(8,128)(2,1)S(1)}, f16[272,128]{1,0:T(8,128)(2,1)S(1)}, u32[]{:S(2)}, u32[]{:S(2)}) collective-permute-start(f16[272,128]{1,0:T(8,128)(2,1)S(1)} %convert_element_type.30), channel_id=1, source_target_pairs={{0,2},{1,9},{2,0},{3,11},{4,12},{5,7},{6,14},{7,5},{8,10},{9,1},{1... | collective-permute-start | bytes 208904 | tf_op jit(solution)/shard_map/ppermute | solution.py:56
  25.0 0.8 %pad_maximum_fusion = bf16[2,480,256]{2,1,0:T(8,128)(2,1)} fusion(bf16[1,480,256]{2,1,0:T(8,128)(2,1)S(1)} %bitcast.24, bf16[1,480,256]{2,1,0:T(8,128)(2,1)S(1)} %bitcast.25), kind=kLoop, calls=%fused_computation | loop fusion | flops 245760 | bytes 983040 | tf_op jit(solution)/shard_map/stack | solution.py:359
  25.9 0.7 %collective-permute-done.8 = f16[272,128]{1,0:T(8,128)(2,1)S(1)} collective-permute-done((f16[272,128]{1,0:T(8,128)(2,1)S(1)}, f16[272,128]{1,0:T(8,128)(2,1)S(1)}, u32[]{:S(2)}, u32[]{:S(2)}) %collective-permute-start.8) | collective-permute-done | bytes 69664 | tf_op jit(solution)/shard_map/ppermute | solution.py:56
  26.5 0.7 %collective-permute-done.9 = f16[272,128]{1,0:T(8,128)(2,1)S(1)} collective-permute-done((f16[272,128]{1,0:T(8,128)(2,1)S(1)}, f16[272,128]{1,0:T(8,128)(2,1)S(1)}, u32[]{:S(2)}, u32[]{:S(2)}) %collective-permute-start.9) | collective-permute-done | bytes 69664 | tf_op jit(solution)/shard_map/ppermute | solution.py:56
  27.2 1.6 %collective-permute-done.10 = f16[272,128]{1,0:T(8,128)(2,1)S(1)} collective-permute-done((f16[272,128]{1,0:T(8,128)(2,1)S(1)}, f16[272,128]{1,0:T(8,128)(2,1)S(1)}, u32[]{:S(2)}, u32[]{:S(2)}) %collective-permute-start.10) | collective-permute-done | bytes 69664 | tf_op jit(solution)/shard_map/ppermute | solution.py:56
  28.9 0.1 select_convert_fusion
  29.0 0.1 collective-permute-start.12
  29.1 1.7 %collective-permute-start.11 = (f16[272,128]{1,0:T(8,128)(2,1)S(1)}, f16[272,128]{1,0:T(8,128)(2,1)S(1)}, u32[]{:S(2)}, u32[]{:S(2)}) collective-permute-start(f16[272,128]{1,0:T(8,128)(2,1)S(1)} %select_convert_fusion), channel_id=1, source_target_pairs={{0,25},{1,6},{2,27},{3,4},{4,3},{5,28},{6,1},{7,30},{8,17},{9,14},... | collective-permute-start | bytes 208904 | tf_op jit(solution)/shard_map/ppermute | solution.py:56
  30.8 1.5 %collective-permute-start.13 = (f16[272,128]{1,0:T(8,128)(2,1)S(1)}, f16[272,128]{1,0:T(8,128)(2,1)S(1)}, u32[]{:S(2)}, u32[]{:S(2)}) collective-permute-start(f16[272,128]{1,0:T(8,128)(2,1)S(1)} %select_convert_fusion), channel_id=1, source_target_pairs={{0,8},{1,3},{2,10},{3,1},{4,6},{5,13},{6,4},{7,15},{8,0},{9,11},{1... | collective-permute-start | bytes 208904 | tf_op jit(solution)/shard_map/ppermute | solution.py:56
  32.3 1.4 %collective-permute-done.12 = f16[272,128]{1,0:T(8,128)(2,1)S(1)} collective-permute-done((f16[272,128]{1,0:T(8,128)(2,1)S(1)}, f16[272,128]{1,0:T(8,128)(2,1)S(1)}, u32[]{:S(2)}, u32[]{:S(2)}) %collective-permute-start.12) | collective-permute-done | bytes 69664 | tf_op jit(solution)/shard_map/ppermute | solution.py:56
  33.7 1.1 %collective-permute-done.11 = f16[272,128]{1,0:T(8,128)(2,1)S(1)} collective-permute-done((f16[272,128]{1,0:T(8,128)(2,1)S(1)}, f16[272,128]{1,0:T(8,128)(2,1)S(1)}, u32[]{:S(2)}, u32[]{:S(2)}) %collective-permute-start.11) | collective-permute-done | bytes 69664 | tf_op jit(solution)/shard_map/ppermute | solution.py:56
  34.8 0.7 %collective-permute-done.13 = f16[272,128]{1,0:T(8,128)(2,1)S(1)} collective-permute-done((f16[272,128]{1,0:T(8,128)(2,1)S(1)}, f16[272,128]{1,0:T(8,128)(2,1)S(1)}, u32[]{:S(2)}, u32[]{:S(2)}) %collective-permute-start.13) | collective-permute-done | bytes 69664 | tf_op jit(solution)/shard_map/ppermute | solution.py:56
  35.6 0.1 collective-permute-start.14
  35.7 1.3 %collective-permute-done.14.other_ref = f32[264,128]{1,0:T(8,128)S(1)} collective-permute-done((f32[264,128]{1,0:T(8,128)S(1)}, f32[264,128]{1,0:T(8,128)S(1)}, u32[]{:S(2)}, u32[]{:S(2)}) %collective-permute-start.14) | collective-permute-done | bytes 135200 | tf_op jit(solution)/shard_map/ppermute | solution.py:56
  37.0 0.8 %shard_map.73 = (f32[256,256]{1,0:T(8,128)}, f32[256,128]{1,0:T(8,128)}) custom-call(f32[264,128]{1,0:T(8,128)S(1)} %fusion.1.mine_ref, f32[264,128]{1,0:T(8,128)S(1)} %collective-permute-done.14.other_ref), custom_call_target="tpu_custom_call" | custom-call | tf_op jit(solution)/shard_map/pallas_call | solution.py:363
  (19 shorter events, 0.3 us)
Async XLA Ops:
  0.6 1.0 %copy-start.2 = (bf16[2,6,80,256]{3,2,1,0:T(8,128)(2,1)S(1)}, bf16[2,6,80,256]{3,2,1,0:T(8,128)(2,1)}, u32[]{:S(2)}) copy-start(bf16[2,6,80,256]{3,2,1,0:T(8,128)(2,1)} %latents_ref.1) | copy-start | bytes 1474564
  1.7 10.5 %collective-permute-start = (bf16[2,2,80,256]{3,2,1,0:T(8,128)(2,1)S(1)}, bf16[2,2,80,256]{3,2,1,0:T(8,128)(2,1)S(1)}, u32[]{:S(2)}, u32[]{:S(2)}) collective-permute-start(bf16[2,2,80,256]{3,2,1,0:T(8,128)(2,1)S(1)} %get-tuple-element.20.edge_ref), channel_id=1, source_target_pairs={{0,4},{4,8},{8,12},{12,16},{16,20},{20,24},{24,28},{28,0},{1,5},{5... | collective-permute-start | bytes 491528 | tf_op jit(solution)/shard_map/ppermute | solution.py:61
  4.7 7.6 %collective-permute-start.5 = (bf16[2,80,256]{2,1,0:T(8,128)(2,1)S(1)}, bf16[2,80,256]{2,1,0:T(8,128)(2,1)S(1)}, u32[]{:S(2)}, u32[]{:S(2)}) collective-permute-start(bf16[2,80,256]{2,1,0:T(8,128)(2,1)S(1)} %get-tuple-element.25), channel_id=1, source_target_pairs={{0,1},{1,0},{2,3},{3,2},{4,5},{5,4},{6,7},{7,6},{8,9},{9,8},{10,11... | collective-permute-start | bytes 245768 | tf_op jit(solution)/shard_map/ppermute | solution.py:56
  4.7 10.0 %collective-permute-start.6 = (bf16[2,80,256]{2,1,0:T(8,128)(2,1)S(1)}, bf16[2,80,256]{2,1,0:T(8,128)(2,1)S(1)}, u32[]{:S(2)}, u32[]{:S(2)}) collective-permute-start(bf16[2,80,256]{2,1,0:T(8,128)(2,1)S(1)} %get-tuple-element.26), channel_id=1, source_target_pairs={{0,3},{1,2},{2,1},{3,0},{4,7},{5,6},{6,5},{7,4},{8,11},{9,10},{10,... | collective-permute-start | bytes 245768 | tf_op jit(solution)/shard_map/ppermute | solution.py:56
  6.3 10.3 %collective-permute-start.4 = (bf16[4,80,256]{2,1,0:T(8,128)(2,1)S(1)}, bf16[4,80,256]{2,1,0:T(8,128)(2,1)S(1)}, u32[]{:S(2)}, u32[]{:S(2)}) collective-permute-start(bf16[4,80,256]{2,1,0:T(8,128)(2,1)S(1)} %get-tuple-element.24.late_ref), channel_id=1, source_target_pairs={{0,4},{4,8},{8,12},{12,16},{16,20},{20,24},{24,28},{28,0},{1,5},{5... | collective-permute-start | bytes 491528 | tf_op jit(solution)/shard_map/ppermute | solution.py:61
  7.9 6.8 %copy-start = (bf16[3,3,768,256]{3,2,1,0:T(8,128)(2,1)S(1)}, bf16[3,3,768,256]{3,2,1,0:T(8,128)(2,1)}, u32[]{:S(2)}) copy-start(bf16[3,3,768,256]{3,2,1,0:T(8,128)(2,1)} %weight_ref.5) | copy-start | bytes 10616836
  7.9 11.1 %collective-permute-start.1 = (bf16[4,80,256]{2,1,0:T(8,128)(2,1)S(1)}, bf16[4,80,256]{2,1,0:T(8,128)(2,1)S(1)}, u32[]{:S(2)}, u32[]{:S(2)}) collective-permute-start(bf16[4,80,256]{2,1,0:T(8,128)(2,1)S(1)} %get-tuple-element.21.early_ref), channel_id=1, source_target_pairs={{0,4},{4,8},{8,12},{12,16},{16,20},{20,24},{24,28},{28,0},{1,5},{5... | collective-permute-start | bytes 491528 | tf_op jit(solution)/shard_map/ppermute | solution.py:61
  12.2 4.4 %copy-start.1 = (bf16[2,6,80,128]{3,2,1,0:T(8,128)(2,1)S(1)}, bf16[2,6,80,128]{3,2,1,0:T(8,128)(2,1)}, u32[]{:S(2)}) copy-start(bf16[2,6,80,128]{3,2,1,0:T(8,128)(2,1)} %param.7) | copy-start | bytes 737284
  12.3 4.4 %copy-start.3 = (f32[256]{0:T(256)S(1)}, f32[256]{0:T(256)}, u32[]{:S(2)}) copy-start(f32[256]{0:T(256)} %param.6) | copy-start | bytes 3076
  12.3 4.4 %collective-permute-start.2 = (bf16[2,80,256]{2,1,0:T(8,128)(2,1)S(1)}, bf16[2,80,256]{2,1,0:T(8,128)(2,1)S(1)}, u32[]{:S(2)}, u32[]{:S(2)}) collective-permute-start(bf16[2,80,256]{2,1,0:T(8,128)(2,1)S(1)} %get-tuple-element.22), channel_id=1, source_target_pairs={{0,3},{1,2},{2,1},{3,0},{4,7},{5,6},{6,5},{7,4},{8,11},{9,10},{10,... | collective-permute-start | bytes 245768 | tf_op jit(solution)/shard_map/ppermute | solution.py:56
  12.4 4.3 %collective-permute-start.3 = (bf16[2,80,256]{2,1,0:T(8,128)(2,1)S(1)}, bf16[2,80,256]{2,1,0:T(8,128)(2,1)S(1)}, u32[]{:S(2)}, u32[]{:S(2)}) collective-permute-start(bf16[2,80,256]{2,1,0:T(8,128)(2,1)S(1)} %get-tuple-element.23), channel_id=1, source_target_pairs={{0,1},{1,0},{2,3},{3,2},{4,5},{5,4},{6,7},{7,6},{8,9},{9,8},{10,11... | collective-permute-start | bytes 245768 | tf_op jit(solution)/shard_map/ppermute | solution.py:56
  20.2 1.4 %collective-permute-start.7 = (f32[264,128]{1,0:T(8,128)S(1)}, f32[264,128]{1,0:T(8,128)S(1)}, u32[]{:S(2)}, u32[]{:S(2)}) collective-permute-start(f32[264,128]{1,0:T(8,128)S(1)} %get-tuple-element.30), channel_id=1, source_target_pairs={{0,1},{1,0},{2,3},{3,2},{4,5},{5,4},{6,7},{7,6},{8,9},{9,8},{10,11... | collective-permute-start | bytes 405512 | tf_op jit(solution)/shard_map/ppermute | solution.py:56
  21.8 4.8 %collective-permute-start.8 = (f16[272,128]{1,0:T(8,128)(2,1)S(1)}, f16[272,128]{1,0:T(8,128)(2,1)S(1)}, u32[]{:S(2)}, u32[]{:S(2)}) collective-permute-start(f16[272,128]{1,0:T(8,128)(2,1)S(1)} %convert_element_type.30), channel_id=1, source_target_pairs={{0,7},{1,24},{2,5},{3,26},{4,29},{5,2},{6,31},{7,0},{8,15},{9,16},... | collective-permute-start | bytes 208904 | tf_op jit(solution)/shard_map/ppermute | solution.py:56
  21.8 5.4 %collective-permute-start.9 = (f16[272,128]{1,0:T(8,128)(2,1)S(1)}, f16[272,128]{1,0:T(8,128)(2,1)S(1)}, u32[]{:S(2)}, u32[]{:S(2)}) collective-permute-start(f16[272,128]{1,0:T(8,128)(2,1)S(1)} %convert_element_type.30), channel_id=1, source_target_pairs={{0,5},{1,16},{2,7},{3,18},{4,21},{5,0},{6,23},{7,2},{8,13},{9,24},... | collective-permute-start | bytes 208904 | tf_op jit(solution)/shard_map/ppermute | solution.py:56
  24.5 4.3 %collective-permute-start.10 = (f16[272,128]{1,0:T(8,128)(2,1)S(1)}, f16[272,128]{1,0:T(8,128)(2,1)S(1)}, u32[]{:S(2)}, u32[]{:S(2)}) collective-permute-start(f16[272,128]{1,0:T(8,128)(2,1)S(1)} %convert_element_type.30), channel_id=1, source_target_pairs={{0,2},{1,9},{2,0},{3,11},{4,12},{5,7},{6,14},{7,5},{8,10},{9,1},{1... | collective-permute-start | bytes 208904 | tf_op jit(solution)/shard_map/ppermute | solution.py:56
  29.0 4.7 %collective-permute-start.12 = (f16[272,128]{1,0:T(8,128)(2,1)S(1)}, f16[272,128]{1,0:T(8,128)(2,1)S(1)}, u32[]{:S(2)}, u32[]{:S(2)}) collective-permute-start(f16[272,128]{1,0:T(8,128)(2,1)S(1)} %select_convert_fusion), channel_id=1, source_target_pairs={{0,17},{1,4},{2,19},{3,6},{4,1},{5,20},{6,3},{7,22},{8,25},{9,12},... | collective-permute-start | bytes 208904 | tf_op jit(solution)/shard_map/ppermute | solution.py:56
  29.1 5.7 %collective-permute-start.11 = (f16[272,128]{1,0:T(8,128)(2,1)S(1)}, f16[272,128]{1,0:T(8,128)(2,1)S(1)}, u32[]{:S(2)}, u32[]{:S(2)}) collective-permute-start(f16[272,128]{1,0:T(8,128)(2,1)S(1)} %select_convert_fusion), channel_id=1, source_target_pairs={{0,25},{1,6},{2,27},{3,4},{4,3},{5,28},{6,1},{7,30},{8,17},{9,14},... | collective-permute-start | bytes 208904 | tf_op jit(solution)/shard_map/ppermute | solution.py:56
  30.8 4.7 %collective-permute-start.13 = (f16[272,128]{1,0:T(8,128)(2,1)S(1)}, f16[272,128]{1,0:T(8,128)(2,1)S(1)}, u32[]{:S(2)}, u32[]{:S(2)}) collective-permute-start(f16[272,128]{1,0:T(8,128)(2,1)S(1)} %select_convert_fusion), channel_id=1, source_target_pairs={{0,8},{1,3},{2,10},{3,1},{4,6},{5,13},{6,4},{7,15},{8,0},{9,11},{1... | collective-permute-start | bytes 208904 | tf_op jit(solution)/shard_map/ppermute | solution.py:56
  35.6 1.4 %collective-permute-start.14 = (f32[264,128]{1,0:T(8,128)S(1)}, f32[264,128]{1,0:T(8,128)S(1)}, u32[]{:S(2)}, u32[]{:S(2)}) collective-permute-start(f32[264,128]{1,0:T(8,128)S(1)} %fusion.1.mine_ref), channel_id=1, source_target_pairs={{0,1},{1,0},{2,3},{3,2},{4,5},{5,4},{6,7},{7,6},{8,9},{9,8},{10,11... | collective-permute-start | bytes 405512 | tf_op jit(solution)/shard_map/ppermute | solution.py:56

commit v7 on v6

--- a/solution.py
+++ b/solution.py
@@ -63,8 +63,6 @@
 
 def cut_kernel(latents_ref, edge_ref, early_ref, late_ref, mate_ref, cross_ref):
     last = latents_ref.shape[1] - 1
-    edge_ref[:, 0] = latents_ref[:, 0]
-    edge_ref[:, 1] = latents_ref[:, last]
     early_ref[...] = latents_ref[0, 1:last]
     late_ref[...] = latents_ref[1, 1:last]
     pick_kernel(edge_ref, mate_ref, cross_ref)
@@ -307,13 +305,14 @@
     blocks, bands = lax.axis_size("tm"), lax.axis_size("row")
     rim = jax.ShapeDtypeStruct((frames, cols, chans), BF16)
     middle = jax.ShapeDtypeStruct((rows - 2, cols, chans), BF16)
-    edge, early, late, to_mate, to_cross = pl.pallas_call(
+    edge = latents[:, :: rows - 1]
+    early, late, to_mate, to_cross = pl.pallas_call(
         cut_kernel,
-        out_shape=(jax.ShapeDtypeStruct((frames, 2, cols, chans), BF16), middle, middle, rim, rim),
-        in_specs=[WHOLE],
-        out_specs=(WHOLE,) * 5,
+        out_shape=(middle, middle, rim, rim),
+        in_specs=[WHOLE] * 2,
+        out_specs=(WHOLE,) * 4,
         compiler_params=params(4),
-    )(latents)
+    )(latents, edge)
     old_edge, old_late, old_early = later(edge), later(late), later(early)
     mate, cross = with_mate(to_mate), with_neighbour(to_cross)
     old_to_mate, old_to_cross = pl.pallas_call(

time: 38 us -> 37.9 us (level)
  local copies, waits for them, and re-layouts: 1.04 us -> 1.98 us
  starting transfers between devices: 16.7 us -> 16.2 us
  waiting for transfers between devices: 12.3 us -> 11.8 us
    ppermute x12, waiting for transfers between devices: 8.75 us -> 7.77 us  [by_device(): lax.ppermute(value, ('tm', 'row'), [(a * rows + b, c * rows + d) for (a,...]
    slice x0 -> x1, local copies, waits for them, and re-layouts: none -> 0.93 us  [on_device(): edge = latents[:, ::rows - 1]]
    ppermute x12, starting transfers between devices: 10.7 us -> 10.1 us  [by_device(): lax.ppermute(value, ('tm', 'row'), [(a * rows + b, c * rows + d) for (a,...]
    ppermute x3, waiting for transfers between devices: 3.55 us -> 4.04 us  [later(): lax.ppermute(value, 'tm', [(i, (i + 1) % count) for i in range(count)])]
where the time goes in v7:
time: 37.9 us; the launch traced here: 37.7 us
  starting transfers between devices  16.2 us (43%)
  waiting for transfers between devices  11.8 us (31%)
  Pallas kernels  5.72 us (15%)
  local copies, waits for them, and re-layouts  1.98 us (5%)
  other arithmetic  1.14 us (3%)
  between operations  0.85 us (2%)
    ppermute x12, starting transfers between devices, by_device(): lax.ppermute(value, ('tm', 'row'), [(a * rows + b, c * rows + d) for (a,...  10.1 us
    ppermute x12, waiting for transfers between devices, by_device(): lax.ppermute(value, ('tm', 'row'), [(a * rows + b, c * rows + d) for (a,...  7.77 us
    ppermute x3, starting transfers between devices, later(): lax.ppermute(value, 'tm', [(i, (i + 1) % count) for i in range(count)])  6.06 us
    ppermute x3, waiting for transfers between devices, later(): lax.ppermute(value, 'tm', [(i, (i + 1) % count) for i in range(count)])  4.04 us
    pallas_call x1, Pallas kernels, on_device(): pl.pallas_call(own_kernel, out_shape=jax.ShapeDtypeStruct((spots, chans),...  1.96 us
    pallas_call x1, Pallas kernels, on_device(): pl.pallas_call(late_kernel, out_shape=(half_features, jax.ShapeDtypeStruc...  1.56 us
    pallas_call x1, Pallas kernels, on_device(): pl.pallas_call(early_kernel, out_shape=(half_features, share, share), in_...  1.18 us
    unnamed x8, local copies, waits for them, and re-layouts  1.05 us
  transfers between devices with their start and end apart: 15, of which 10 were waited for; matrix products, arithmetic and copies ran while one was open for 2% of the time, Pallas kernels for 9%

profile of v7, /device:TPU:0, one launch (start us, length us, event | category | flops | bytes accessed | tf_op | source)
XLA Modules:
  0.0 37.7 jit_solution(7623703548610120801)
XLA Ops:
  0.6 0.9 %slice.39.edge_ref = bf16[2,2,80,256]{3,2,1,0:T(8,128)(2,1)S(1)} slice(bf16[2,6,80,256]{3,2,1,0:T(8,128)(2,1)} %latents_ref.1), slice={[0:2:1], [0:6:5], [0:80:1], [0:256:1]} | slice | bytes 327680 | tf_op jit(solution)/shard_map/slice | solution.py:308
  1.6 3.0 %collective-permute-start = (bf16[2,2,80,256]{3,2,1,0:T(8,128)(2,1)S(1)}, bf16[2,2,80,256]{3,2,1,0:T(8,128)(2,1)S(1)}, u32[]{:S(2)}, u32[]{:S(2)}) collective-permute-start(bf16[2,2,80,256]{3,2,1,0:T(8,128)(2,1)S(1)} %slice.39.edge_ref), channel_id=1, source_target_pairs={{0,4},{4,8},{8,12},{12,16},{16,20},{20,24},{24,28},{28,0},{1,5},{5... | collective-permute-start | bytes 491528 | tf_op jit(solution)/shard_map/ppermute | solution.py:61
  4.6 0.0 copy-start.2
  4.6 1.0 %copy-done.2 = bf16[2,6,80,256]{3,2,1,0:T(8,128)(2,1)S(1)} copy-done((bf16[2,6,80,256]{3,2,1,0:T(8,128)(2,1)S(1)}, bf16[2,6,80,256]{3,2,1,0:T(8,128)(2,1)}, u32[]{:S(2)}) %copy-start.2) | copy-done | bytes 491544
  5.7 0.1 collective-permute-start.5
  5.7 1.6 %collective-permute-start.6 = (bf16[2,80,256]{2,1,0:T(8,128)(2,1)S(1)}, bf16[2,80,256]{2,1,0:T(8,128)(2,1)S(1)}, u32[]{:S(2)}, u32[]{:S(2)}) collective-permute-start(bf16[2,80,256]{2,1,0:T(8,128)(2,1)S(1)} %get-tuple-element.24), channel_id=1, source_target_pairs={{0,3},{1,2},{2,1},{3,0},{4,7},{5,6},{6,5},{7,4},{8,11},{9,10},{10,... | collective-permute-start | bytes 245768 | tf_op jit(solution)/shard_map/ppermute | solution.py:56
  7.3 1.5 %collective-permute-start.4 = (bf16[4,80,256]{2,1,0:T(8,128)(2,1)S(1)}, bf16[4,80,256]{2,1,0:T(8,128)(2,1)S(1)}, u32[]{:S(2)}, u32[]{:S(2)}) collective-permute-start(bf16[4,80,256]{2,1,0:T(8,128)(2,1)S(1)} %get-tuple-element.22.late_ref), channel_id=1, source_target_pairs={{0,4},{4,8},{8,12},{12,16},{16,20},{20,24},{24,28},{28,0},{1,5},{5... | collective-permute-start | bytes 491528 | tf_op jit(solution)/shard_map/ppermute | solution.py:61
  8.9 0.0 copy-start
  8.9 1.5 %collective-permute-start.1 = (bf16[4,80,256]{2,1,0:T(8,128)(2,1)S(1)}, bf16[4,80,256]{2,1,0:T(8,128)(2,1)S(1)}, u32[]{:S(2)}, u32[]{:S(2)}) collective-permute-start(bf16[4,80,256]{2,1,0:T(8,128)(2,1)S(1)} %get-tuple-element.19.early_ref), channel_id=1, source_target_pairs={{0,4},{4,8},{8,12},{12,16},{16,20},{20,24},{24,28},{28,0},{1,5},{5... | collective-permute-start | bytes 491528 | tf_op jit(solution)/shard_map/ppermute | solution.py:61
  10.4 1.4 %collective-permute-done.edge_ref.old_edge_ref = bf16[2,2,80,256]{3,2,1,0:T(8,128)(2,1)S(1)} collective-permute-done((bf16[2,2,80,256]{3,2,1,0:T(8,128)(2,1)S(1)}, bf16[2,2,80,256]{3,2,1,0:T(8,128)(2,1)S(1)}, u32[]{:S(2)}, u32[]{:S(2)}) %collective-permute-start) | collective-permute-done | bytes 163872 | tf_op jit(solution)/shard_map/ppermute | solution.py:61
  11.8 0.0 copy-start.1
  11.9 0.0 copy-start.3
  11.9 0.3 collective-permute-start.2
  12.1 0.0 collective-permute-done.5.mate_ref
  12.1 1.4 %collective-permute-start.3 = (bf16[2,80,256]{2,1,0:T(8,128)(2,1)S(1)}, bf16[2,80,256]{2,1,0:T(8,128)(2,1)S(1)}, u32[]{:S(2)}, u32[]{:S(2)}) collective-permute-start(bf16[2,80,256]{2,1,0:T(8,128)(2,1)S(1)} %get-tuple-element.21), channel_id=1, source_target_pairs={{0,1},{1,0},{2,3},{3,2},{4,5},{5,4},{6,7},{7,6},{8,9},{9,8},{10,11... | collective-permute-start | bytes 245768 | tf_op jit(solution)/shard_map/ppermute | solution.py:56
  13.6 0.0 collective-permute-done.6.cross_ref
  13.6 0.0 copy-done
  13.6 2.0 %shard_map.69.part_ref = f32[960,256]{1,0:T(8,128)S(1)} custom-call(bf16[2,2,80,256]{3,2,1,0:T(8,128)(2,1)S(1)} %slice.39.edge_ref, bf16[4,80,256]{2,1,0:T(8,128)(2,1)S(1)} %get-tuple-element.19.early_ref, bf16[4,80,256]{2,1,0:T(8,128)(2,1)S(1)} %get-tuple-element.22.late_ref, bf16[2,80,256]{2,1,0:T(8,128)(2,1)S(1)} %collective-permute-done.5.mate_ref, ...), custom_call_target="tpu_custom_call" | custom-call | flops 1698693120 | bytes 5242880 | tf_op jit(solution)/shard_map/pallas_call | solution.py:327
  15.5 1.6 %collective-permute-done.4.old_late_ref = bf16[4,80,256]{2,1,0:T(8,128)(2,1)S(1)} collective-permute-done((bf16[4,80,256]{2,1,0:T(8,128)(2,1)S(1)}, bf16[4,80,256]{2,1,0:T(8,128)(2,1)S(1)}, u32[]{:S(2)}, u32[]{:S(2)}) %collective-permute-start.4) | collective-permute-done | bytes 163872 | tf_op jit(solution)/shard_map/ppermute | solution.py:61
  17.1 0.0 collective-permute-done.2.cross_ref
  17.1 0.0 collective-permute-done.3.mate_ref
  17.1 0.0 copy-done.1
  17.1 0.0 copy-done.3
  17.1 1.6 %shard_map.70 = (bf16[480,256]{1,0:T(8,128)(2,1)S(1)}, f32[480,256]{1,0:T(8,128)S(1)}, f32[256,384]{1,0:T(8,128)S(1)}) custom-call(bf16[2,2,80,256]{3,2,1,0:T(8,128)(2,1)S(1)} %slice.39.edge_ref, bf16[4,80,256]{2,1,0:T(8,128)(2,1)S(1)} %get-tuple-element.22.late_ref, bf16[2,2,80,256]{3,2,1,0:T(8,128)(2,1)S(1)} %collective-permute-done.edge_ref.old_edge_ref, ...), custom_call_target="tpu_custom_call" | custom-call | flops 1258291200 | bytes 5242880 | tf_op jit(solution)/shard_map/pallas_call | solution.py:337
  18.7 1.0 %collective-permute-done.1.old_early_ref = bf16[4,80,256]{2,1,0:T(8,128)(2,1)S(1)} collective-permute-done((bf16[4,80,256]{2,1,0:T(8,128)(2,1)S(1)}, bf16[4,80,256]{2,1,0:T(8,128)(2,1)S(1)}, u32[]{:S(2)}, u32[]{:S(2)}) %collective-permute-start.1) | collective-permute-done | bytes 163872 | tf_op jit(solution)/shard_map/ppermute | solution.py:61
  19.7 1.2 %shard_map.71 = (bf16[480,256]{1,0:T(8,128)(2,1)S(1)}, f32[264,128]{1,0:T(8,128)S(1)}, f32[264,128]{1,0:T(8,128)S(1)}) custom-call(bf16[2,2,80,256]{3,2,1,0:T(8,128)(2,1)S(1)} %slice.39.edge_ref, bf16[4,80,256]{2,1,0:T(8,128)(2,1)S(1)} %get-tuple-element.19.early_ref, bf16[2,2,80,256]{3,2,1,0:T(8,128)(2,1)S(1)} %collective-permute-done.edge_ref.old_edge_ref, ...), custom_call_target="tpu_custom_call" | custom-call | flops 629145600 | bytes 5242880 | tf_op jit(solution)/shard_map/pallas_call | solution.py:350
  20.9 0.1 collective-permute-start.7
  21.0 1.3 %collective-permute-done.7.got_ref = f32[264,128]{1,0:T(8,128)S(1)} collective-permute-done((f32[264,128]{1,0:T(8,128)S(1)}, f32[264,128]{1,0:T(8,128)S(1)}, u32[]{:S(2)}, u32[]{:S(2)}) %collective-permute-start.7) | collective-permute-done | bytes 135200 | tf_op jit(solution)/shard_map/ppermute | solution.py:56
  22.3 0.1 shard_map.72
  22.5 0.1 collective-permute-start.8
  22.6 1.8 %collective-permute-start.9 = (f16[272,128]{1,0:T(8,128)(2,1)S(1)}, f16[272,128]{1,0:T(8,128)(2,1)S(1)}, u32[]{:S(2)}, u32[]{:S(2)}) collective-permute-start(f16[272,128]{1,0:T(8,128)(2,1)S(1)} %convert_element_type.30), channel_id=1, source_target_pairs={{0,5},{1,16},{2,7},{3,18},{4,21},{5,0},{6,23},{7,2},{8,13},{9,24},... | collective-permute-start | bytes 208904 | tf_op jit(solution)/shard_map/ppermute | solution.py:56
  24.4 1.4 %collective-permute-start.10 = (f16[272,128]{1,0:T(8,128)(2,1)S(1)}, f16[272,128]{1,0:T(8,128)(2,1)S(1)}, u32[]{:S(2)}, u32[]{:S(2)}) collective-permute-start(f16[272,128]{1,0:T(8,128)(2,1)S(1)} %convert_element_type.30), channel_id=1, source_target_pairs={{0,2},{1,9},{2,0},{3,11},{4,12},{5,7},{6,14},{7,5},{8,10},{9,1},{1... | collective-permute-start | bytes 208904 | tf_op jit(solution)/shard_map/ppermute | solution.py:56
  25.8 0.8 %pad_maximum_fusion = bf16[2,480,256]{2,1,0:T(8,128)(2,1)} fusion(bf16[1,480,256]{2,1,0:T(8,128)(2,1)S(1)} %bitcast.24, bf16[1,480,256]{2,1,0:T(8,128)(2,1)S(1)} %bitcast.25), kind=kLoop, calls=%fused_computation | loop fusion | flops 245760 | bytes 983040 | tf_op jit(solution)/shard_map/stack | solution.py:358
  26.6 0.6 %collective-permute-done.8 = f16[272,128]{1,0:T(8,128)(2,1)S(1)} collective-permute-done((f16[272,128]{1,0:T(8,128)(2,1)S(1)}, f16[272,128]{1,0:T(8,128)(2,1)S(1)}, u32[]{:S(2)}, u32[]{:S(2)}) %collective-permute-start.8) | collective-permute-done | bytes 69664 | tf_op jit(solution)/shard_map/ppermute | solution.py:56
  27.2 0.0 collective-permute-done.9
  27.2 1.4 %collective-permute-done.10 = f16[272,128]{1,0:T(8,128)(2,1)S(1)} collective-permute-done((f16[272,128]{1,0:T(8,128)(2,1)S(1)}, f16[272,128]{1,0:T(8,128)(2,1)S(1)}, u32[]{:S(2)}, u32[]{:S(2)}) %collective-permute-start.10) | collective-permute-done | bytes 69664 | tf_op jit(solution)/shard_map/ppermute | solution.py:56
  28.7 0.1 select_convert_fusion
  28.8 0.1 collective-permute-start.12
  28.9 1.8 %collective-permute-start.11 = (f16[272,128]{1,0:T(8,128)(2,1)S(1)}, f16[272,128]{1,0:T(8,128)(2,1)S(1)}, u32[]{:S(2)}, u32[]{:S(2)}) collective-permute-start(f16[272,128]{1,0:T(8,128)(2,1)S(1)} %select_convert_fusion), channel_id=1, source_target_pairs={{0,25},{1,6},{2,27},{3,4},{4,3},{5,28},{6,1},{7,30},{8,17},{9,14},... | collective-permute-start | bytes 208904 | tf_op jit(solution)/shard_map/ppermute | solution.py:56
  30.7 1.4 %collective-permute-start.13 = (f16[272,128]{1,0:T(8,128)(2,1)S(1)}, f16[272,128]{1,0:T(8,128)(2,1)S(1)}, u32[]{:S(2)}, u32[]{:S(2)}) collective-permute-start(f16[272,128]{1,0:T(8,128)(2,1)S(1)} %select_convert_fusion), channel_id=1, source_target_pairs={{0,8},{1,3},{2,10},{3,1},{4,6},{5,13},{6,4},{7,15},{8,0},{9,11},{1... | collective-permute-start | bytes 208904 | tf_op jit(solution)/shard_map/ppermute | solution.py:56
  32.1 1.4 %collective-permute-done.12 = f16[272,128]{1,0:T(8,128)(2,1)S(1)} collective-permute-done((f16[272,128]{1,0:T(8,128)(2,1)S(1)}, f16[272,128]{1,0:T(8,128)(2,1)S(1)}, u32[]{:S(2)}, u32[]{:S(2)}) %collective-permute-start.12) | collective-permute-done | bytes 69664 | tf_op jit(solution)/shard_map/ppermute | solution.py:56
  33.6 1.1 %collective-permute-done.11 = f16[272,128]{1,0:T(8,128)(2,1)S(1)} collective-permute-done((f16[272,128]{1,0:T(8,128)(2,1)S(1)}, f16[272,128]{1,0:T(8,128)(2,1)S(1)}, u32[]{:S(2)}, u32[]{:S(2)}) %collective-permute-start.11) | collective-permute-done | bytes 69664 | tf_op jit(solution)/shard_map/ppermute | solution.py:56
  34.7 0.7 %collective-permute-done.13 = f16[272,128]{1,0:T(8,128)(2,1)S(1)} collective-permute-done((f16[272,128]{1,0:T(8,128)(2,1)S(1)}, f16[272,128]{1,0:T(8,128)(2,1)S(1)}, u32[]{:S(2)}, u32[]{:S(2)}) %collective-permute-start.13) | collective-permute-done | bytes 69664 | tf_op jit(solution)/shard_map/ppermute | solution.py:56
  35.4 0.2 collective-permute-start.14
  35.6 1.2 %collective-permute-done.14.other_ref = f32[264,128]{1,0:T(8,128)S(1)} collective-permute-done((f32[264,128]{1,0:T(8,128)S(1)}, f32[264,128]{1,0:T(8,128)S(1)}, u32[]{:S(2)}, u32[]{:S(2)}) %collective-permute-start.14) | collective-permute-done | bytes 135200 | tf_op jit(solution)/shard_map/ppermute | solution.py:56
  36.9 0.8 %shard_map.73 = (f32[256,256]{1,0:T(8,128)}, f32[256,128]{1,0:T(8,128)}) custom-call(f32[264,128]{1,0:T(8,128)S(1)} %fusion.1.mine_ref, f32[264,128]{1,0:T(8,128)S(1)} %collective-permute-done.14.other_ref), custom_call_target="tpu_custom_call" | custom-call | tf_op jit(solution)/shard_map/pallas_call | solution.py:362
  (19 shorter events, 0.3 us)
Async XLA Ops:
  1.6 10.3 %collective-permute-start = (bf16[2,2,80,256]{3,2,1,0:T(8,128)(2,1)S(1)}, bf16[2,2,80,256]{3,2,1,0:T(8,128)(2,1)S(1)}, u32[]{:S(2)}, u32[]{:S(2)}) collective-permute-start(bf16[2,2,80,256]{3,2,1,0:T(8,128)(2,1)S(1)} %slice.39.edge_ref), channel_id=1, source_target_pairs={{0,4},{4,8},{8,12},{12,16},{16,20},{20,24},{24,28},{28,0},{1,5},{5... | collective-permute-start | bytes 491528 | tf_op jit(solution)/shard_map/ppermute | solution.py:61
  4.6 1.0 %copy-start.2 = (bf16[2,6,80,256]{3,2,1,0:T(8,128)(2,1)S(1)}, bf16[2,6,80,256]{3,2,1,0:T(8,128)(2,1)}, u32[]{:S(2)}) copy-start(bf16[2,6,80,256]{3,2,1,0:T(8,128)(2,1)} %latents_ref.1) | copy-start | bytes 1474564
  5.7 6.5 %collective-permute-start.5 = (bf16[2,80,256]{2,1,0:T(8,128)(2,1)S(1)}, bf16[2,80,256]{2,1,0:T(8,128)(2,1)S(1)}, u32[]{:S(2)}, u32[]{:S(2)}) collective-permute-start(bf16[2,80,256]{2,1,0:T(8,128)(2,1)S(1)} %get-tuple-element.23), channel_id=1, source_target_pairs={{0,1},{1,0},{2,3},{3,2},{4,5},{5,4},{6,7},{7,6},{8,9},{9,8},{10,11... | collective-permute-start | bytes 245768 | tf_op jit(solution)/shard_map/ppermute | solution.py:56
  5.7 7.8 %collective-permute-start.6 = (bf16[2,80,256]{2,1,0:T(8,128)(2,1)S(1)}, bf16[2,80,256]{2,1,0:T(8,128)(2,1)S(1)}, u32[]{:S(2)}, u32[]{:S(2)}) collective-permute-start(bf16[2,80,256]{2,1,0:T(8,128)(2,1)S(1)} %get-tuple-element.24), channel_id=1, source_target_pairs={{0,3},{1,2},{2,1},{3,0},{4,7},{5,6},{6,5},{7,4},{8,11},{9,10},{10,... | collective-permute-start | bytes 245768 | tf_op jit(solution)/shard_map/ppermute | solution.py:56
  7.3 9.8 %collective-permute-start.4 = (bf16[4,80,256]{2,1,0:T(8,128)(2,1)S(1)}, bf16[4,80,256]{2,1,0:T(8,128)(2,1)S(1)}, u32[]{:S(2)}, u32[]{:S(2)}) collective-permute-start(bf16[4,80,256]{2,1,0:T(8,128)(2,1)S(1)} %get-tuple-element.22.late_ref), channel_id=1, source_target_pairs={{0,4},{4,8},{8,12},{12,16},{16,20},{20,24},{24,28},{28,0},{1,5},{5... | collective-permute-start | bytes 491528 | tf_op jit(solution)/shard_map/ppermute | solution.py:61
  8.9 4.7 %copy-start = (bf16[3,3,768,256]{3,2,1,0:T(8,128)(2,1)S(1)}, bf16[3,3,768,256]{3,2,1,0:T(8,128)(2,1)}, u32[]{:S(2)}) copy-start(bf16[3,3,768,256]{3,2,1,0:T(8,128)(2,1)} %weight_ref.5) | copy-start | bytes 10616836
  8.9 10.9 %collective-permute-start.1 = (bf16[4,80,256]{2,1,0:T(8,128)(2,1)S(1)}, bf16[4,80,256]{2,1,0:T(8,128)(2,1)S(1)}, u32[]{:S(2)}, u32[]{:S(2)}) collective-permute-start(bf16[4,80,256]{2,1,0:T(8,128)(2,1)S(1)} %get-tuple-element.19.early_ref), channel_id=1, source_target_pairs={{0,4},{4,8},{8,12},{12,16},{16,20},{20,24},{24,28},{28,0},{1,5},{5... | collective-permute-start | bytes 491528 | tf_op jit(solution)/shard_map/ppermute | solution.py:61
  11.8 5.3 %copy-start.1 = (bf16[2,6,80,128]{3,2,1,0:T(8,128)(2,1)S(1)}, bf16[2,6,80,128]{3,2,1,0:T(8,128)(2,1)}, u32[]{:S(2)}) copy-start(bf16[2,6,80,128]{3,2,1,0:T(8,128)(2,1)} %param.7) | copy-start | bytes 737284
  11.9 5.3 %copy-start.3 = (f32[256]{0:T(256)S(1)}, f32[256]{0:T(256)}, u32[]{:S(2)}) copy-start(f32[256]{0:T(256)} %param.6) | copy-start | bytes 3076
  11.9 5.2 %collective-permute-start.2 = (bf16[2,80,256]{2,1,0:T(8,128)(2,1)S(1)}, bf16[2,80,256]{2,1,0:T(8,128)(2,1)S(1)}, u32[]{:S(2)}, u32[]{:S(2)}) collective-permute-start(bf16[2,80,256]{2,1,0:T(8,128)(2,1)S(1)} %get-tuple-element.20), channel_id=1, source_target_pairs={{0,3},{1,2},{2,1},{3,0},{4,7},{5,6},{6,5},{7,4},{8,11},{9,10},{10,... | collective-permute-start | bytes 245768 | tf_op jit(solution)/shard_map/ppermute | solution.py:56
  12.1 5.0 %collective-permute-start.3 = (bf16[2,80,256]{2,1,0:T(8,128)(2,1)S(1)}, bf16[2,80,256]{2,1,0:T(8,128)(2,1)S(1)}, u32[]{:S(2)}, u32[]{:S(2)}) collective-permute-start(bf16[2,80,256]{2,1,0:T(8,128)(2,1)S(1)} %get-tuple-element.21), channel_id=1, source_target_pairs={{0,1},{1,0},{2,3},{3,2},{4,5},{5,4},{6,7},{7,6},{8,9},{9,8},{10,11... | collective-permute-start | bytes 245768 | tf_op jit(solution)/shard_map/ppermute | solution.py:56
  20.9 1.4 %collective-permute-start.7 = (f32[264,128]{1,0:T(8,128)S(1)}, f32[264,128]{1,0:T(8,128)S(1)}, u32[]{:S(2)}, u32[]{:S(2)}) collective-permute-start(f32[264,128]{1,0:T(8,128)S(1)} %get-tuple-element.28), channel_id=1, source_target_pairs={{0,1},{1,0},{2,3},{3,2},{4,5},{5,4},{6,7},{7,6},{8,9},{9,8},{10,11... | collective-permute-start | bytes 405512 | tf_op jit(solution)/shard_map/ppermute | solution.py:56
  22.5 4.7 %collective-permute-start.8 = (f16[272,128]{1,0:T(8,128)(2,1)S(1)}, f16[272,128]{1,0:T(8,128)(2,1)S(1)}, u32[]{:S(2)}, u32[]{:S(2)}) collective-permute-start(f16[272,128]{1,0:T(8,128)(2,1)S(1)} %convert_element_type.30), channel_id=1, source_target_pairs={{0,7},{1,24},{2,5},{3,26},{4,29},{5,2},{6,31},{7,0},{8,15},{9,16},... | collective-permute-start | bytes 208904 | tf_op jit(solution)/shard_map/ppermute | solution.py:56
  22.6 4.6 %collective-permute-start.9 = (f16[272,128]{1,0:T(8,128)(2,1)S(1)}, f16[272,128]{1,0:T(8,128)(2,1)S(1)}, u32[]{:S(2)}, u32[]{:S(2)}) collective-permute-start(f16[272,128]{1,0:T(8,128)(2,1)S(1)} %convert_element_type.30), channel_id=1, source_target_pairs={{0,5},{1,16},{2,7},{3,18},{4,21},{5,0},{6,23},{7,2},{8,13},{9,24},... | collective-permute-start | bytes 208904 | tf_op jit(solution)/shard_map/ppermute | solution.py:56
  24.4 4.3 %collective-permute-start.10 = (f16[272,128]{1,0:T(8,128)(2,1)S(1)}, f16[272,128]{1,0:T(8,128)(2,1)S(1)}, u32[]{:S(2)}, u32[]{:S(2)}) collective-permute-start(f16[272,128]{1,0:T(8,128)(2,1)S(1)} %convert_element_type.30), channel_id=1, source_target_pairs={{0,2},{1,9},{2,0},{3,11},{4,12},{5,7},{6,14},{7,5},{8,10},{9,1},{1... | collective-permute-start | bytes 208904 | tf_op jit(solution)/shard_map/ppermute | solution.py:56
  28.8 4.7 %collective-permute-start.12 = (f16[272,128]{1,0:T(8,128)(2,1)S(1)}, f16[272,128]{1,0:T(8,128)(2,1)S(1)}, u32[]{:S(2)}, u32[]{:S(2)}) collective-permute-start(f16[272,128]{1,0:T(8,128)(2,1)S(1)} %select_convert_fusion), channel_id=1, source_target_pairs={{0,17},{1,4},{2,19},{3,6},{4,1},{5,20},{6,3},{7,22},{8,25},{9,12},... | collective-permute-start | bytes 208904 | tf_op jit(solution)/shard_map/ppermute | solution.py:56
  28.9 5.7 %collective-permute-start.11 = (f16[272,128]{1,0:T(8,128)(2,1)S(1)}, f16[272,128]{1,0:T(8,128)(2,1)S(1)}, u32[]{:S(2)}, u32[]{:S(2)}) collective-permute-start(f16[272,128]{1,0:T(8,128)(2,1)S(1)} %select_convert_fusion), channel_id=1, source_target_pairs={{0,25},{1,6},{2,27},{3,4},{4,3},{5,28},{6,1},{7,30},{8,17},{9,14},... | collective-permute-start | bytes 208904 | tf_op jit(solution)/shard_map/ppermute | solution.py:56
  30.7 4.7 %collective-permute-start.13 = (f16[272,128]{1,0:T(8,128)(2,1)S(1)}, f16[272,128]{1,0:T(8,128)(2,1)S(1)}, u32[]{:S(2)}, u32[]{:S(2)}) collective-permute-start(f16[272,128]{1,0:T(8,128)(2,1)S(1)} %select_convert_fusion), channel_id=1, source_target_pairs={{0,8},{1,3},{2,10},{3,1},{4,6},{5,13},{6,4},{7,15},{8,0},{9,11},{1... | collective-permute-start | bytes 208904 | tf_op jit(solution)/shard_map/ppermute | solution.py:56
  35.4 1.4 %collective-permute-start.14 = (f32[264,128]{1,0:T(8,128)S(1)}, f32[264,128]{1,0:T(8,128)S(1)}, u32[]{:S(2)}, u32[]{:S(2)}) collective-permute-start(f32[264,128]{1,0:T(8,128)S(1)} %fusion.1.mine_ref), channel_id=1, source_target_pairs={{0,1},{1,0},{2,3},{3,2},{4,5},{5,4},{6,7},{7,6},{8,9},{9,8},{10,11... | collective-permute-start | bytes 405512 | tf_op jit(solution)/shard_map/ppermute | solution.py:56

commit v8 on v7

--- a/solution.py
+++ b/solution.py
@@ -258,8 +258,8 @@
 
 def joined_messages(messages, last):
     rows = messages[0].shape[0] - HEAD // 2
+    exponents = [message[rows : rows + 1].astype(F32) for message in messages]
     messages = [message.astype(F32) for message in messages]
-    exponents = [message[rows : rows + 1] for message in messages]
     e = functools.reduce(jnp.maximum, exponents) + len(messages) // 2
     if last:
         terms = [message[:rows] * power(p) for message, p in zip(messages, exponents)]
@@ -293,7 +293,8 @@
                 c, d = pair[side(a, b)]
                 moves.append(((a, b), (a ^ c, b ^ d ^ side(c, d))))
             messages.append(by_device(value, moves))
-        value = joined_messages(messages[::-1], s == len(rounds) - 1)
+        order = messages[::-1] if s == len(rounds) - 1 else [value, *messages[1:]]
+        value = joined_messages(order, s == len(rounds) - 1)
     return value
 
 

time: 37.9 us -> 37.8 us (level)
  starting transfers between devices: 16.2 us -> 15.8 us
  waiting for transfers between devices: 11.8 us -> 12.2 us
    ppermute x12, waiting for transfers between devices: 7.77 us -> 8.2 us  [by_device(): lax.ppermute(value, ('tm', 'row'), [(a * rows + b, c * rows + d) for (a,...]
    ppermute x12, starting transfers between devices: 10.1 us -> 9.76 us  [by_device(): lax.ppermute(value, ('tm', 'row'), [(a * rows + b, c * rows + d) for (a,...]
where the time goes in v8:
time: 37.8 us; the launch traced here: 37.6 us
  starting transfers between devices  15.8 us (42%)
  waiting for transfers between devices  12.2 us (32%)
  Pallas kernels  5.72 us (15%)
  local copies, waits for them, and re-layouts  1.98 us (5%)
  other arithmetic  1.06 us (3%)
  between operations  0.79 us (2%)
    ppermute x12, starting transfers between devices, by_device(): lax.ppermute(value, ('tm', 'row'), [(a * rows + b, c * rows + d) for (a,...  9.76 us
    ppermute x12, waiting for transfers between devices, by_device(): lax.ppermute(value, ('tm', 'row'), [(a * rows + b, c * rows + d) for (a,...  8.2 us
    ppermute x3, starting transfers between devices, later(): lax.ppermute(value, 'tm', [(i, (i + 1) % count) for i in range(count)])  6.06 us
    ppermute x3, waiting for transfers between devices, later(): lax.ppermute(value, 'tm', [(i, (i + 1) % count) for i in range(count)])  4.04 us
    pallas_call x1, Pallas kernels, on_device(): pl.pallas_call(own_kernel, out_shape=jax.ShapeDtypeStruct((spots, chans),...  1.96 us
    pallas_call x1, Pallas kernels, on_device(): pl.pallas_call(late_kernel, out_shape=(half_features, jax.ShapeDtypeStruc...  1.56 us
    pallas_call x1, Pallas kernels, on_device(): pl.pallas_call(early_kernel, out_shape=(half_features, share, share), in_...  1.18 us
    unnamed x8, local copies, waits for them, and re-layouts  1.05 us
  transfers between devices with their start and end apart: 15, of which 10 were waited for; matrix products, arithmetic and copies ran while one was open for 2% of the time, Pallas kernels for 9%

profile of v8, /device:TPU:0, one launch (start us, length us, event | category | flops | bytes accessed | tf_op | source)
XLA Modules:
  0.0 37.6 jit_solution(7522293055017745570)
XLA Ops:
  0.6 0.9 %slice.51.edge_ref = bf16[2,2,80,256]{3,2,1,0:T(8,128)(2,1)S(1)} slice(bf16[2,6,80,256]{3,2,1,0:T(8,128)(2,1)} %latents_ref.1), slice={[0:2:1], [0:6:5], [0:80:1], [0:256:1]} | slice | bytes 327680 | tf_op jit(solution)/shard_map/slice | solution.py:309
  1.6 3.0 %collective-permute-start = (bf16[2,2,80,256]{3,2,1,0:T(8,128)(2,1)S(1)}, bf16[2,2,80,256]{3,2,1,0:T(8,128)(2,1)S(1)}, u32[]{:S(2)}, u32[]{:S(2)}) collective-permute-start(bf16[2,2,80,256]{3,2,1,0:T(8,128)(2,1)S(1)} %slice.51.edge_ref), channel_id=1, source_target_pairs={{0,4},{4,8},{8,12},{12,16},{16,20},{20,24},{24,28},{28,0},{1,5},{5... | collective-permute-start | bytes 491528 | tf_op jit(solution)/shard_map/ppermute | solution.py:61
  4.6 0.0 copy-start.2
  4.6 1.0 %copy-done.2 = bf16[2,6,80,256]{3,2,1,0:T(8,128)(2,1)S(1)} copy-done((bf16[2,6,80,256]{3,2,1,0:T(8,128)(2,1)S(1)}, bf16[2,6,80,256]{3,2,1,0:T(8,128)(2,1)}, u32[]{:S(2)}) %copy-start.2) | copy-done | bytes 491544
  5.7 0.1 collective-permute-start.5
  5.7 1.6 %collective-permute-start.6 = (bf16[2,80,256]{2,1,0:T(8,128)(2,1)S(1)}, bf16[2,80,256]{2,1,0:T(8,128)(2,1)S(1)}, u32[]{:S(2)}, u32[]{:S(2)}) collective-permute-start(bf16[2,80,256]{2,1,0:T(8,128)(2,1)S(1)} %get-tuple-element.24), channel_id=1, source_target_pairs={{0,3},{1,2},{2,1},{3,0},{4,7},{5,6},{6,5},{7,4},{8,11},{9,10},{10,... | collective-permute-start | bytes 245768 | tf_op jit(solution)/shard_map/ppermute | solution.py:56
  7.3 1.5 %collective-permute-start.4 = (bf16[4,80,256]{2,1,0:T(8,128)(2,1)S(1)}, bf16[4,80,256]{2,1,0:T(8,128)(2,1)S(1)}, u32[]{:S(2)}, u32[]{:S(2)}) collective-permute-start(bf16[4,80,256]{2,1,0:T(8,128)(2,1)S(1)} %get-tuple-element.22.late_ref), channel_id=1, source_target_pairs={{0,4},{4,8},{8,12},{12,16},{16,20},{20,24},{24,28},{28,0},{1,5},{5... | collective-permute-start | bytes 491528 | tf_op jit(solution)/shard_map/ppermute | solution.py:61
  8.9 0.0 copy-start
  8.9 1.5 %collective-permute-start.1 = (bf16[4,80,256]{2,1,0:T(8,128)(2,1)S(1)}, bf16[4,80,256]{2,1,0:T(8,128)(2,1)S(1)}, u32[]{:S(2)}, u32[]{:S(2)}) collective-permute-start(bf16[4,80,256]{2,1,0:T(8,128)(2,1)S(1)} %get-tuple-element.19.early_ref), channel_id=1, source_target_pairs={{0,4},{4,8},{8,12},{12,16},{16,20},{20,24},{24,28},{28,0},{1,5},{5... | collective-permute-start | bytes 491528 | tf_op jit(solution)/shard_map/ppermute | solution.py:61
  10.4 1.4 %collective-permute-done.edge_ref.old_edge_ref = bf16[2,2,80,256]{3,2,1,0:T(8,128)(2,1)S(1)} collective-permute-done((bf16[2,2,80,256]{3,2,1,0:T(8,128)(2,1)S(1)}, bf16[2,2,80,256]{3,2,1,0:T(8,128)(2,1)S(1)}, u32[]{:S(2)}, u32[]{:S(2)}) %collective-permute-start) | collective-permute-done | bytes 163872 | tf_op jit(solution)/shard_map/ppermute | solution.py:61
  11.8 0.0 copy-start.1
  11.9 0.0 copy-start.3
  11.9 0.3 collective-permute-start.2
  12.1 0.0 collective-permute-done.5.mate_ref
  12.1 1.4 %collective-permute-start.3 = (bf16[2,80,256]{2,1,0:T(8,128)(2,1)S(1)}, bf16[2,80,256]{2,1,0:T(8,128)(2,1)S(1)}, u32[]{:S(2)}, u32[]{:S(2)}) collective-permute-start(bf16[2,80,256]{2,1,0:T(8,128)(2,1)S(1)} %get-tuple-element.21), channel_id=1, source_target_pairs={{0,1},{1,0},{2,3},{3,2},{4,5},{5,4},{6,7},{7,6},{8,9},{9,8},{10,11... | collective-permute-start | bytes 245768 | tf_op jit(solution)/shard_map/ppermute | solution.py:56
  13.6 0.0 collective-permute-done.6.cross_ref
  13.6 0.0 copy-done
  13.6 2.0 %shard_map.69.part_ref = f32[960,256]{1,0:T(8,128)S(1)} custom-call(bf16[2,2,80,256]{3,2,1,0:T(8,128)(2,1)S(1)} %slice.51.edge_ref, bf16[4,80,256]{2,1,0:T(8,128)(2,1)S(1)} %get-tuple-element.19.early_ref, bf16[4,80,256]{2,1,0:T(8,128)(2,1)S(1)} %get-tuple-element.22.late_ref, bf16[2,80,256]{2,1,0:T(8,128)(2,1)S(1)} %collective-permute-done.5.mate_ref, ...), custom_call_target="tpu_custom_call" | custom-call | flops 1698693120 | bytes 5242880 | tf_op jit(solution)/shard_map/pallas_call | solution.py:328
  15.5 1.6 %collective-permute-done.4.old_late_ref = bf16[4,80,256]{2,1,0:T(8,128)(2,1)S(1)} collective-permute-done((bf16[4,80,256]{2,1,0:T(8,128)(2,1)S(1)}, bf16[4,80,256]{2,1,0:T(8,128)(2,1)S(1)}, u32[]{:S(2)}, u32[]{:S(2)}) %collective-permute-start.4) | collective-permute-done | bytes 163872 | tf_op jit(solution)/shard_map/ppermute | solution.py:61
  17.1 0.0 collective-permute-done.2.cross_ref
  17.1 0.0 collective-permute-done.3.mate_ref
  17.1 0.0 copy-done.1
  17.1 0.0 copy-done.3
  17.1 1.6 %shard_map.70 = (bf16[480,256]{1,0:T(8,128)(2,1)S(1)}, f32[480,256]{1,0:T(8,128)S(1)}, f32[256,384]{1,0:T(8,128)S(1)}) custom-call(bf16[2,2,80,256]{3,2,1,0:T(8,128)(2,1)S(1)} %slice.51.edge_ref, bf16[4,80,256]{2,1,0:T(8,128)(2,1)S(1)} %get-tuple-element.22.late_ref, bf16[2,2,80,256]{3,2,1,0:T(8,128)(2,1)S(1)} %collective-permute-done.edge_ref.old_edge_ref, ...), custom_call_target="tpu_custom_call" | custom-call | flops 1258291200 | bytes 5242880 | tf_op jit(solution)/shard_map/pallas_call | solution.py:338
  18.7 1.0 %collective-permute-done.1.old_early_ref = bf16[4,80,256]{2,1,0:T(8,128)(2,1)S(1)} collective-permute-done((bf16[4,80,256]{2,1,0:T(8,128)(2,1)S(1)}, bf16[4,80,256]{2,1,0:T(8,128)(2,1)S(1)}, u32[]{:S(2)}, u32[]{:S(2)}) %collective-permute-start.1) | collective-permute-done | bytes 163872 | tf_op jit(solution)/shard_map/ppermute | solution.py:61
  19.7 1.2 %shard_map.71 = (bf16[480,256]{1,0:T(8,128)(2,1)S(1)}, f32[264,128]{1,0:T(8,128)S(1)}, f32[264,128]{1,0:T(8,128)S(1)}) custom-call(bf16[2,2,80,256]{3,2,1,0:T(8,128)(2,1)S(1)} %slice.51.edge_ref, bf16[4,80,256]{2,1,0:T(8,128)(2,1)S(1)} %get-tuple-element.19.early_ref, bf16[2,2,80,256]{3,2,1,0:T(8,128)(2,1)S(1)} %collective-permute-done.edge_ref.old_edge_ref, ...), custom_call_target="tpu_custom_call" | custom-call | flops 629145600 | bytes 5242880 | tf_op jit(solution)/shard_map/pallas_call | solution.py:351
  20.9 0.1 collective-permute-start.7
  21.0 1.3 %collective-permute-done.7.got_ref = f32[264,128]{1,0:T(8,128)S(1)} collective-permute-done((f32[264,128]{1,0:T(8,128)S(1)}, f32[264,128]{1,0:T(8,128)S(1)}, u32[]{:S(2)}, u32[]{:S(2)}) %collective-permute-start.7) | collective-permute-done | bytes 135200 | tf_op jit(solution)/shard_map/ppermute | solution.py:56
  22.3 0.1 shard_map.72
  22.5 0.1 collective-permute-start.10
  22.6 0.7 %collective-permute-start.8 = (f16[272,128]{1,0:T(8,128)(2,1)S(1)}, f16[272,128]{1,0:T(8,128)(2,1)S(1)}, u32[]{:S(2)}, u32[]{:S(2)}) collective-permute-start(f16[272,128]{1,0:T(8,128)(2,1)S(1)} %convert_element_type.46), channel_id=1, source_target_pairs={{0,2},{1,9},{2,0},{3,11},{4,12},{5,7},{6,14},{7,5},{8,10},{9,1},{1... | collective-permute-start | bytes 208904 | tf_op jit(solution)/shard_map/ppermute | solution.py:56
  23.2 2.2 %collective-permute-start.9 = (f16[272,128]{1,0:T(8,128)(2,1)S(1)}, f16[272,128]{1,0:T(8,128)(2,1)S(1)}, u32[]{:S(2)}, u32[]{:S(2)}) collective-permute-start(f16[272,128]{1,0:T(8,128)(2,1)S(1)} %convert_element_type.46), channel_id=1, source_target_pairs={{0,5},{1,16},{2,7},{3,18},{4,21},{5,0},{6,23},{7,2},{8,13},{9,24},... | collective-permute-start | bytes 208904 | tf_op jit(solution)/shard_map/ppermute | solution.py:56
  25.5 0.8 %pad_maximum_fusion = bf16[2,480,256]{2,1,0:T(8,128)(2,1)} fusion(bf16[1,480,256]{2,1,0:T(8,128)(2,1)S(1)} %bitcast.24, bf16[1,480,256]{2,1,0:T(8,128)(2,1)S(1)} %bitcast.25), kind=kLoop, calls=%fused_computation | loop fusion | flops 245760 | bytes 983040 | tf_op jit(solution)/shard_map/stack | solution.py:359
  26.3 0.9 %collective-permute-done.10 = f16[272,128]{1,0:T(8,128)(2,1)S(1)} collective-permute-done((f16[272,128]{1,0:T(8,128)(2,1)S(1)}, f16[272,128]{1,0:T(8,128)(2,1)S(1)}, u32[]{:S(2)}, u32[]{:S(2)}) %collective-permute-start.10) | collective-permute-done | bytes 69664 | tf_op jit(solution)/shard_map/ppermute | solution.py:56
  27.2 0.0 collective-permute-done.8
  27.2 0.7 %collective-permute-done.9 = f16[272,128]{1,0:T(8,128)(2,1)S(1)} collective-permute-done((f16[272,128]{1,0:T(8,128)(2,1)S(1)}, f16[272,128]{1,0:T(8,128)(2,1)S(1)}, u32[]{:S(2)}, u32[]{:S(2)}) %collective-permute-start.9) | collective-permute-done | bytes 69664 | tf_op jit(solution)/shard_map/ppermute | solution.py:56
  28.0 0.1 select_convert_fusion
  28.1 1.0 %collective-permute-start.12 = (f16[272,128]{1,0:T(8,128)(2,1)S(1)}, f16[272,128]{1,0:T(8,128)(2,1)S(1)}, u32[]{:S(2)}, u32[]{:S(2)}) collective-permute-start(f16[272,128]{1,0:T(8,128)(2,1)S(1)} %select_convert_fusion), channel_id=1, source_target_pairs={{0,17},{1,4},{2,19},{3,6},{4,1},{5,20},{6,3},{7,22},{8,25},{9,12},... | collective-permute-start | bytes 208904 | tf_op jit(solution)/shard_map/ppermute | solution.py:56
  29.1 1.1 %collective-permute-start.11 = (f16[272,128]{1,0:T(8,128)(2,1)S(1)}, f16[272,128]{1,0:T(8,128)(2,1)S(1)}, u32[]{:S(2)}, u32[]{:S(2)}) collective-permute-start(f16[272,128]{1,0:T(8,128)(2,1)S(1)} %select_convert_fusion), channel_id=1, source_target_pairs={{0,25},{1,6},{2,27},{3,4},{4,3},{5,28},{6,1},{7,30},{8,17},{9,14},... | collective-permute-start | bytes 208904 | tf_op jit(solution)/shard_map/ppermute | solution.py:56
  30.2 1.1 %collective-permute-start.13 = (f16[272,128]{1,0:T(8,128)(2,1)S(1)}, f16[272,128]{1,0:T(8,128)(2,1)S(1)}, u32[]{:S(2)}, u32[]{:S(2)}) collective-permute-start(f16[272,128]{1,0:T(8,128)(2,1)S(1)} %select_convert_fusion), channel_id=1, source_target_pairs={{0,8},{1,3},{2,10},{3,1},{4,6},{5,13},{6,4},{7,15},{8,0},{9,11},{1... | collective-permute-start | bytes 208904 | tf_op jit(solution)/shard_map/ppermute | solution.py:56
  31.4 1.6 %collective-permute-done.12 = f16[272,128]{1,0:T(8,128)(2,1)S(1)} collective-permute-done((f16[272,128]{1,0:T(8,128)(2,1)S(1)}, f16[272,128]{1,0:T(8,128)(2,1)S(1)}, u32[]{:S(2)}, u32[]{:S(2)}) %collective-permute-start.12) | collective-permute-done | bytes 69664 | tf_op jit(solution)/shard_map/ppermute | solution.py:56
  33.0 1.8 %collective-permute-done.11 = f16[272,128]{1,0:T(8,128)(2,1)S(1)} collective-permute-done((f16[272,128]{1,0:T(8,128)(2,1)S(1)}, f16[272,128]{1,0:T(8,128)(2,1)S(1)}, u32[]{:S(2)}, u32[]{:S(2)}) %collective-permute-start.11) | collective-permute-done | bytes 69664 | tf_op jit(solution)/shard_map/ppermute | solution.py:56
  34.8 0.5 %collective-permute-done.13 = f16[272,128]{1,0:T(8,128)(2,1)S(1)} collective-permute-done((f16[272,128]{1,0:T(8,128)(2,1)S(1)}, f16[272,128]{1,0:T(8,128)(2,1)S(1)}, u32[]{:S(2)}, u32[]{:S(2)}) %collective-permute-start.13) | collective-permute-done | bytes 69664 | tf_op jit(solution)/shard_map/ppermute | solution.py:56
  35.3 0.1 add_add_fusion.mine_ref
  35.3 0.1 collective-permute-start.14
  35.4 1.3 %collective-permute-done.14.other_ref = f32[264,128]{1,0:T(8,128)S(1)} collective-permute-done((f32[264,128]{1,0:T(8,128)S(1)}, f32[264,128]{1,0:T(8,128)S(1)}, u32[]{:S(2)}, u32[]{:S(2)}) %collective-permute-start.14) | collective-permute-done | bytes 135200 | tf_op jit(solution)/shard_map/ppermute | solution.py:56
  36.8 0.8 %shard_map.73 = (f32[256,256]{1,0:T(8,128)}, f32[256,128]{1,0:T(8,128)}) custom-call(f32[264,128]{1,0:T(8,128)S(1)} %add_add_fusion.mine_ref, f32[264,128]{1,0:T(8,128)S(1)} %collective-permute-done.14.other_ref), custom_call_target="tpu_custom_call" | custom-call | tf_op jit(solution)/shard_map/pallas_call | solution.py:363
  (10 shorter events, 0.1 us)
Async XLA Ops:
  1.6 10.3 %collective-permute-start = (bf16[2,2,80,256]{3,2,1,0:T(8,128)(2,1)S(1)}, bf16[2,2,80,256]{3,2,1,0:T(8,128)(2,1)S(1)}, u32[]{:S(2)}, u32[]{:S(2)}) collective-permute-start(bf16[2,2,80,256]{3,2,1,0:T(8,128)(2,1)S(1)} %slice.51.edge_ref), channel_id=1, source_target_pairs={{0,4},{4,8},{8,12},{12,16},{16,20},{20,24},{24,28},{28,0},{1,5},{5... | collective-permute-start | bytes 491528 | tf_op jit(solution)/shard_map/ppermute | solution.py:61
  4.6 1.0 %copy-start.2 = (bf16[2,6,80,256]{3,2,1,0:T(8,128)(2,1)S(1)}, bf16[2,6,80,256]{3,2,1,0:T(8,128)(2,1)}, u32[]{:S(2)}) copy-start(bf16[2,6,80,256]{3,2,1,0:T(8,128)(2,1)} %latents_ref.1) | copy-start | bytes 1474564
  5.7 6.5 %collective-permute-start.5 = (bf16[2,80,256]{2,1,0:T(8,128)(2,1)S(1)}, bf16[2,80,256]{2,1,0:T(8,128)(2,1)S(1)}, u32[]{:S(2)}, u32[]{:S(2)}) collective-permute-start(bf16[2,80,256]{2,1,0:T(8,128)(2,1)S(1)} %get-tuple-element.23), channel_id=1, source_target_pairs={{0,1},{1,0},{2,3},{3,2},{4,5},{5,4},{6,7},{7,6},{8,9},{9,8},{10,11... | collective-permute-start | bytes 245768 | tf_op jit(solution)/shard_map/ppermute | solution.py:56
  5.7 7.8 %collective-permute-start.6 = (bf16[2,80,256]{2,1,0:T(8,128)(2,1)S(1)}, bf16[2,80,256]{2,1,0:T(8,128)(2,1)S(1)}, u32[]{:S(2)}, u32[]{:S(2)}) collective-permute-start(bf16[2,80,256]{2,1,0:T(8,128)(2,1)S(1)} %get-tuple-element.24), channel_id=1, source_target_pairs={{0,3},{1,2},{2,1},{3,0},{4,7},{5,6},{6,5},{7,4},{8,11},{9,10},{10,... | collective-permute-start | bytes 245768 | tf_op jit(solution)/shard_map/ppermute | solution.py:56
  7.3 9.8 %collective-permute-start.4 = (bf16[4,80,256]{2,1,0:T(8,128)(2,1)S(1)}, bf16[4,80,256]{2,1,0:T(8,128)(2,1)S(1)}, u32[]{:S(2)}, u32[]{:S(2)}) collective-permute-start(bf16[4,80,256]{2,1,0:T(8,128)(2,1)S(1)} %get-tuple-element.22.late_ref), channel_id=1, source_target_pairs={{0,4},{4,8},{8,12},{12,16},{16,20},{20,24},{24,28},{28,0},{1,5},{5... | collective-permute-start | bytes 491528 | tf_op jit(solution)/shard_map/ppermute | solution.py:61
  8.9 4.7 %copy-start = (bf16[3,3,768,256]{3,2,1,0:T(8,128)(2,1)S(1)}, bf16[3,3,768,256]{3,2,1,0:T(8,128)(2,1)}, u32[]{:S(2)}) copy-start(bf16[3,3,768,256]{3,2,1,0:T(8,128)(2,1)} %weight_ref.5) | copy-start | bytes 10616836
  8.9 10.9 %collective-permute-start.1 = (bf16[4,80,256]{2,1,0:T(8,128)(2,1)S(1)}, bf16[4,80,256]{2,1,0:T(8,128)(2,1)S(1)}, u32[]{:S(2)}, u32[]{:S(2)}) collective-permute-start(bf16[4,80,256]{2,1,0:T(8,128)(2,1)S(1)} %get-tuple-element.19.early_ref), channel_id=1, source_target_pairs={{0,4},{4,8},{8,12},{12,16},{16,20},{20,24},{24,28},{28,0},{1,5},{5... | collective-permute-start | bytes 491528 | tf_op jit(solution)/shard_map/ppermute | solution.py:61
  11.8 5.3 %copy-start.1 = (bf16[2,6,80,128]{3,2,1,0:T(8,128)(2,1)S(1)}, bf16[2,6,80,128]{3,2,1,0:T(8,128)(2,1)}, u32[]{:S(2)}) copy-start(bf16[2,6,80,128]{3,2,1,0:T(8,128)(2,1)} %param.7) | copy-start | bytes 737284
  11.9 5.3 %copy-start.3 = (f32[256]{0:T(256)S(1)}, f32[256]{0:T(256)}, u32[]{:S(2)}) copy-start(f32[256]{0:T(256)} %param.6) | copy-start | bytes 3076
  11.9 5.2 %collective-permute-start.2 = (bf16[2,80,256]{2,1,0:T(8,128)(2,1)S(1)}, bf16[2,80,256]{2,1,0:T(8,128)(2,1)S(1)}, u32[]{:S(2)}, u32[]{:S(2)}) collective-permute-start(bf16[2,80,256]{2,1,0:T(8,128)(2,1)S(1)} %get-tuple-element.20), channel_id=1, source_target_pairs={{0,3},{1,2},{2,1},{3,0},{4,7},{5,6},{6,5},{7,4},{8,11},{9,10},{10,... | collective-permute-start | bytes 245768 | tf_op jit(solution)/shard_map/ppermute | solution.py:56
  12.1 5.0 %collective-permute-start.3 = (bf16[2,80,256]{2,1,0:T(8,128)(2,1)S(1)}, bf16[2,80,256]{2,1,0:T(8,128)(2,1)S(1)}, u32[]{:S(2)}, u32[]{:S(2)}) collective-permute-start(bf16[2,80,256]{2,1,0:T(8,128)(2,1)S(1)} %get-tuple-element.21), channel_id=1, source_target_pairs={{0,1},{1,0},{2,3},{3,2},{4,5},{5,4},{6,7},{7,6},{8,9},{9,8},{10,11... | collective-permute-start | bytes 245768 | tf_op jit(solution)/shard_map/ppermute | solution.py:56
  20.9 1.4 %collective-permute-start.7 = (f32[264,128]{1,0:T(8,128)S(1)}, f32[264,128]{1,0:T(8,128)S(1)}, u32[]{:S(2)}, u32[]{:S(2)}) collective-permute-start(f32[264,128]{1,0:T(8,128)S(1)} %get-tuple-element.28), channel_id=1, source_target_pairs={{0,1},{1,0},{2,3},{3,2},{4,5},{5,4},{6,7},{7,6},{8,9},{9,8},{10,11... | collective-permute-start | bytes 405512 | tf_op jit(solution)/shard_map/ppermute | solution.py:56
  22.5 4.7 %collective-permute-start.10 = (f16[272,128]{1,0:T(8,128)(2,1)S(1)}, f16[272,128]{1,0:T(8,128)(2,1)S(1)}, u32[]{:S(2)}, u32[]{:S(2)}) collective-permute-start(f16[272,128]{1,0:T(8,128)(2,1)S(1)} %convert_element_type.46), channel_id=1, source_target_pairs={{0,7},{1,24},{2,5},{3,26},{4,29},{5,2},{6,31},{7,0},{8,15},{9,16},... | collective-permute-start | bytes 208904 | tf_op jit(solution)/shard_map/ppermute | solution.py:56
  22.6 4.7 %collective-permute-start.8 = (f16[272,128]{1,0:T(8,128)(2,1)S(1)}, f16[272,128]{1,0:T(8,128)(2,1)S(1)}, u32[]{:S(2)}, u32[]{:S(2)}) collective-permute-start(f16[272,128]{1,0:T(8,128)(2,1)S(1)} %convert_element_type.46), channel_id=1, source_target_pairs={{0,2},{1,9},{2,0},{3,11},{4,12},{5,7},{6,14},{7,5},{8,10},{9,1},{1... | collective-permute-start | bytes 208904 | tf_op jit(solution)/shard_map/ppermute | solution.py:56
  23.2 4.7 %collective-permute-start.9 = (f16[272,128]{1,0:T(8,128)(2,1)S(1)}, f16[272,128]{1,0:T(8,128)(2,1)S(1)}, u32[]{:S(2)}, u32[]{:S(2)}) collective-permute-start(f16[272,128]{1,0:T(8,128)(2,1)S(1)} %convert_element_type.46), channel_id=1, source_target_pairs={{0,5},{1,16},{2,7},{3,18},{4,21},{5,0},{6,23},{7,2},{8,13},{9,24},... | collective-permute-start | bytes 208904 | tf_op jit(solution)/shard_map/ppermute | solution.py:56
  28.1 4.9 %collective-permute-start.12 = (f16[272,128]{1,0:T(8,128)(2,1)S(1)}, f16[272,128]{1,0:T(8,128)(2,1)S(1)}, u32[]{:S(2)}, u32[]{:S(2)}) collective-permute-start(f16[272,128]{1,0:T(8,128)(2,1)S(1)} %select_convert_fusion), channel_id=1, source_target_pairs={{0,17},{1,4},{2,19},{3,6},{4,1},{5,20},{6,3},{7,22},{8,25},{9,12},... | collective-permute-start | bytes 208904 | tf_op jit(solution)/shard_map/ppermute | solution.py:56
  29.1 5.6 %collective-permute-start.11 = (f16[272,128]{1,0:T(8,128)(2,1)S(1)}, f16[272,128]{1,0:T(8,128)(2,1)S(1)}, u32[]{:S(2)}, u32[]{:S(2)}) collective-permute-start(f16[272,128]{1,0:T(8,128)(2,1)S(1)} %select_convert_fusion), channel_id=1, source_target_pairs={{0,25},{1,6},{2,27},{3,4},{4,3},{5,28},{6,1},{7,30},{8,17},{9,14},... | collective-permute-start | bytes 208904 | tf_op jit(solution)/shard_map/ppermute | solution.py:56
  30.2 5.1 %collective-permute-start.13 = (f16[272,128]{1,0:T(8,128)(2,1)S(1)}, f16[272,128]{1,0:T(8,128)(2,1)S(1)}, u32[]{:S(2)}, u32[]{:S(2)}) collective-permute-start(f16[272,128]{1,0:T(8,128)(2,1)S(1)} %select_convert_fusion), channel_id=1, source_target_pairs={{0,8},{1,3},{2,10},{3,1},{4,6},{5,13},{6,4},{7,15},{8,0},{9,11},{1... | collective-permute-start | bytes 208904 | tf_op jit(solution)/shard_map/ppermute | solution.py:56
  35.3 1.4 %collective-permute-start.14 = (f32[264,128]{1,0:T(8,128)S(1)}, f32[264,128]{1,0:T(8,128)S(1)}, u32[]{:S(2)}, u32[]{:S(2)}) collective-permute-start(f32[264,128]{1,0:T(8,128)S(1)} %add_add_fusion.mine_ref), channel_id=1, source_target_pairs={{0,1},{1,0},{2,3},{3,2},{4,5},{5,4},{6,7},{7,6},{8,9},{9,8},{10,11... | collective-permute-start | bytes 405512 | tf_op jit(solution)/shard_map/ppermute | solution.py:56

commit v9 on v8

--- a/solution.py
+++ b/solution.py
@@ -61,11 +61,10 @@
     return lax.ppermute(value, "tm", [(i, (i + 1) % count) for i in range(count)])
 
 
-def cut_kernel(latents_ref, edge_ref, early_ref, late_ref, mate_ref, cross_ref):
+def cut_kernel(latents_ref, early_ref, late_ref):
     last = latents_ref.shape[1] - 1
     early_ref[...] = latents_ref[0, 1:last]
     late_ref[...] = latents_ref[1, 1:last]
-    pick_kernel(edge_ref, mate_ref, cross_ref)
 
 
 def pick_kernel(edge_ref, mate_ref, cross_ref):
@@ -80,6 +79,19 @@
     @pl.when(jnp.logical_not(on_even_row()))
     def _():
         fill(0, 1)
+
+
+def picked(edge):
+    frames, _, cols, chans = edge.shape
+    rim = jax.ShapeDtypeStruct((frames, cols, chans), BF16)
+    return pl.pallas_call(
+        pick_kernel,
+        out_shape=(rim, rim),
+        in_specs=[WHOLE],
+        out_specs=(WHOLE,) * 2,
+        compiler_params=params(4),
+        cost_estimate=pl.CostEstimate(flops=2 * 10**9, bytes_accessed=2**20, transcendentals=0),
+    )(edge)
 
 
 def with_neighbour(value):
@@ -304,26 +316,19 @@
     bins = depth_target.shape[3]
     half = chans // 2
     blocks, bands = lax.axis_size("tm"), lax.axis_size("row")
-    rim = jax.ShapeDtypeStruct((frames, cols, chans), BF16)
     middle = jax.ShapeDtypeStruct((rows - 2, cols, chans), BF16)
     edge = latents[:, :: rows - 1]
-    early, late, to_mate, to_cross = pl.pallas_call(
+    to_mate, to_cross = picked(edge)
+    early, late = pl.pallas_call(
         cut_kernel,
-        out_shape=(middle, middle, rim, rim),
-        in_specs=[WHOLE] * 2,
-        out_specs=(WHOLE,) * 4,
-        compiler_params=params(4),
-    )(latents, edge)
-    old_edge, old_late, old_early = later(edge), later(late), later(early)
-    mate, cross = with_mate(to_mate), with_neighbour(to_cross)
-    old_to_mate, old_to_cross = pl.pallas_call(
-        pick_kernel,
-        out_shape=(rim, rim),
+        out_shape=(middle, middle),
         in_specs=[WHOLE],
         out_specs=(WHOLE,) * 2,
         compiler_params=params(4),
-        cost_estimate=pl.CostEstimate(flops=2 * 10**9, bytes_accessed=2**20, transcendentals=0),
-    )(old_edge)
+    )(latents)
+    old_edge, old_late, old_early = later(edge), later(late), later(early)
+    mate, cross = with_mate(to_mate), with_neighbour(to_cross)
+    old_to_mate, old_to_cross = picked(old_edge)
     old_mate, old_cross = with_mate(old_to_mate), with_neighbour(old_to_cross)
     part = pl.pallas_call(
         own_kernel,

time: 37.8 us -> 37 us (0.979)
  local copies, waits for them, and re-layouts: 1.98 us -> 0.96 us
  starting transfers between devices: 15.8 us -> 16.8 us
  waiting for transfers between devices: 12.2 us -> 11.4 us
    unnamed x8, local copies, waits for them, and re-layouts: 1.05 us -> 0.02 us
    ppermute x12, starting transfers between devices: 9.76 us -> 10.7 us  [by_device(): lax.ppermute(value, ('tm', 'row'), [(a * rows + b, c * rows + d) for (a,...]
    ppermute x3, waiting for transfers between devices: 4.04 us -> 3.13 us  [later(): lax.ppermute(value, 'tm', [(i, (i + 1) % count) for i in range(count)])]
  transfers between devices with their start and end apart: 15 -> 15, of which waited for: 10 -> 9; matrix products, arithmetic and copies ran while one was open for 2% -> 2% of each run, Pallas kernels for 9% -> 10%
where the time goes in v9:
time: 37 us; the launch traced here: 36.9 us
  starting transfers between devices  16.8 us (45%)
  waiting for transfers between devices  11.4 us (31%)
  Pallas kernels  5.73 us (15%)
  other arithmetic  1.06 us (3%)
  local copies, waits for them, and re-layouts  0.96 us (3%)
  between operations  0.83 us (2%)
    ppermute x12, starting transfers between devices, by_device(): lax.ppermute(value, ('tm', 'row'), [(a * rows + b, c * rows + d) for (a,...  10.7 us
    ppermute x12, waiting for transfers between devices, by_device(): lax.ppermute(value, ('tm', 'row'), [(a * rows + b, c * rows + d) for (a,...  8.32 us
    ppermute x3, starting transfers between devices, later(): lax.ppermute(value, 'tm', [(i, (i + 1) % count) for i in range(count)])  6.11 us
    ppermute x3, waiting for transfers between devices, later(): lax.ppermute(value, 'tm', [(i, (i + 1) % count) for i in range(count)])  3.13 us
    pallas_call x1, Pallas kernels, on_device(): pl.pallas_call(own_kernel, out_shape=jax.ShapeDtypeStruct((spots, chans),...  1.96 us
    pallas_call x1, Pallas kernels, on_device(): pl.pallas_call(late_kernel, out_shape=(half_features, jax.ShapeDtypeStruc...  1.56 us
    pallas_call x1, Pallas kernels, on_device(): pl.pallas_call(early_kernel, out_shape=(half_features, share, share), in_...  1.19 us
    slice x1, local copies, waits for them, and re-layouts, on_device(): edge = latents[:, ::rows - 1]  0.93 us
  transfers between devices with their start and end apart: 15, of which 9 were waited for; matrix products, arithmetic and copies ran while one was open for 2% of the time, Pallas kernels for 10%

profile of v9, /device:TPU:0, one launch (start us, length us, event | category | flops | bytes accessed | tf_op | source)
XLA Modules:
  0.0 36.9 jit_solution(18180860057787862733)
XLA Ops:
  0.6 0.9 %slice.51.edge_ref = bf16[2,2,80,256]{3,2,1,0:T(8,128)(2,1)S(1)} slice(bf16[2,6,80,256]{3,2,1,0:T(8,128)(2,1)} %latents_ref.1), slice={[0:2:1], [0:6:5], [0:80:1], [0:256:1]} | slice | bytes 327680 | tf_op jit(solution)/shard_map/slice | solution.py:320
  1.6 0.0 copy-start.2
  1.6 3.0 %collective-permute-start = (bf16[2,2,80,256]{3,2,1,0:T(8,128)(2,1)S(1)}, bf16[2,2,80,256]{3,2,1,0:T(8,128)(2,1)S(1)}, u32[]{:S(2)}, u32[]{:S(2)}) collective-permute-start(bf16[2,2,80,256]{3,2,1,0:T(8,128)(2,1)S(1)} %slice.51.edge_ref), channel_id=1, source_target_pairs={{0,4},{4,8},{8,12},{12,16},{16,20},{20,24},{24,28},{28,0},{1,5},{5... | collective-permute-start | bytes 491528 | tf_op jit(solution)/shard_map/ppermute | solution.py:61
  4.6 0.1 collective-permute-start.5
  4.7 1.6 %collective-permute-start.6 = (bf16[2,80,256]{2,1,0:T(8,128)(2,1)S(1)}, bf16[2,80,256]{2,1,0:T(8,128)(2,1)S(1)}, u32[]{:S(2)}, u32[]{:S(2)}) collective-permute-start(bf16[2,80,256]{2,1,0:T(8,128)(2,1)S(1)} %get-tuple-element.24), channel_id=1, source_target_pairs={{0,3},{1,2},{2,1},{3,0},{4,7},{5,6},{6,5},{7,4},{8,11},{9,10},{10,... | collective-permute-start | bytes 245768 | tf_op jit(solution)/shard_map/ppermute | solution.py:56
  6.3 0.0 copy-done.2
  6.3 1.6 %collective-permute-start.4 = (bf16[4,80,256]{2,1,0:T(8,128)(2,1)S(1)}, bf16[4,80,256]{2,1,0:T(8,128)(2,1)S(1)}, u32[]{:S(2)}, u32[]{:S(2)}) collective-permute-start(bf16[4,80,256]{2,1,0:T(8,128)(2,1)S(1)} %get-tuple-element.22.late_ref), channel_id=1, source_target_pairs={{0,4},{4,8},{8,12},{12,16},{16,20},{20,24},{24,28},{28,0},{1,5},{5... | collective-permute-start | bytes 491528 | tf_op jit(solution)/shard_map/ppermute | solution.py:61
  7.9 0.0 copy-start
  7.9 1.5 %collective-permute-start.1 = (bf16[4,80,256]{2,1,0:T(8,128)(2,1)S(1)}, bf16[4,80,256]{2,1,0:T(8,128)(2,1)S(1)}, u32[]{:S(2)}, u32[]{:S(2)}) collective-permute-start(bf16[4,80,256]{2,1,0:T(8,128)(2,1)S(1)} %get-tuple-element.19.early_ref), channel_id=1, source_target_pairs={{0,4},{4,8},{8,12},{12,16},{16,20},{20,24},{24,28},{28,0},{1,5},{5... | collective-permute-start | bytes 491528 | tf_op jit(solution)/shard_map/ppermute | solution.py:61
  9.4 2.4 %collective-permute-done.edge_ref.old_edge_ref = bf16[2,2,80,256]{3,2,1,0:T(8,128)(2,1)S(1)} collective-permute-done((bf16[2,2,80,256]{3,2,1,0:T(8,128)(2,1)S(1)}, bf16[2,2,80,256]{3,2,1,0:T(8,128)(2,1)S(1)}, u32[]{:S(2)}, u32[]{:S(2)}) %collective-permute-start) | collective-permute-done | bytes 163872 | tf_op jit(solution)/shard_map/ppermute | solution.py:61
  11.9 0.0 copy-start.1
  11.9 0.0 copy-start.3
  11.9 0.2 collective-permute-start.2
  12.1 0.0 collective-permute-done.5.mate_ref
  12.1 2.4 %collective-permute-start.3 = (bf16[2,80,256]{2,1,0:T(8,128)(2,1)S(1)}, bf16[2,80,256]{2,1,0:T(8,128)(2,1)S(1)}, u32[]{:S(2)}, u32[]{:S(2)}) collective-permute-start(bf16[2,80,256]{2,1,0:T(8,128)(2,1)S(1)} %get-tuple-element.21), channel_id=1, source_target_pairs={{0,1},{1,0},{2,3},{3,2},{4,5},{5,4},{6,7},{7,6},{8,9},{9,8},{10,11... | collective-permute-start | bytes 245768 | tf_op jit(solution)/shard_map/ppermute | solution.py:56
  14.6 0.0 collective-permute-done.6.cross_ref
  14.6 0.0 copy-done
  14.6 2.0 %shard_map.70.part_ref = f32[960,256]{1,0:T(8,128)S(1)} custom-call(bf16[2,2,80,256]{3,2,1,0:T(8,128)(2,1)S(1)} %slice.51.edge_ref, bf16[4,80,256]{2,1,0:T(8,128)(2,1)S(1)} %get-tuple-element.19.early_ref, bf16[4,80,256]{2,1,0:T(8,128)(2,1)S(1)} %get-tuple-element.22.late_ref, bf16[2,80,256]{2,1,0:T(8,128)(2,1)S(1)} %collective-permute-done.5.mate_ref, ...), custom_call_target="tpu_custom_call" | custom-call | flops 1698693120 | bytes 5242880 | tf_op jit(solution)/shard_map/pallas_call | solution.py:333
  16.5 0.0 collective-permute-done.4.old_late_ref
  16.6 0.0 collective-permute-done.2.cross_ref
  16.6 0.0 collective-permute-done.3.mate_ref
  16.6 0.0 copy-done.1
  16.6 0.0 copy-done.3
  16.6 1.6 %shard_map.71 = (bf16[480,256]{1,0:T(8,128)(2,1)S(1)}, f32[480,256]{1,0:T(8,128)S(1)}, f32[256,384]{1,0:T(8,128)S(1)}) custom-call(bf16[2,2,80,256]{3,2,1,0:T(8,128)(2,1)S(1)} %slice.51.edge_ref, bf16[4,80,256]{2,1,0:T(8,128)(2,1)S(1)} %get-tuple-element.22.late_ref, bf16[2,2,80,256]{3,2,1,0:T(8,128)(2,1)S(1)} %collective-permute-done.edge_ref.old_edge_ref, ...), custom_call_target="tpu_custom_call" | custom-call | flops 1258291200 | bytes 5242880 | tf_op jit(solution)/shard_map/pallas_call | solution.py:343
  18.2 0.7 %collective-permute-done.1.old_early_ref = bf16[4,80,256]{2,1,0:T(8,128)(2,1)S(1)} collective-permute-done((bf16[4,80,256]{2,1,0:T(8,128)(2,1)S(1)}, bf16[4,80,256]{2,1,0:T(8,128)(2,1)S(1)}, u32[]{:S(2)}, u32[]{:S(2)}) %collective-permute-start.1) | collective-permute-done | bytes 163872 | tf_op jit(solution)/shard_map/ppermute | solution.py:61
  18.9 1.2 %shard_map.72 = (bf16[480,256]{1,0:T(8,128)(2,1)S(1)}, f32[264,128]{1,0:T(8,128)S(1)}, f32[264,128]{1,0:T(8,128)S(1)}) custom-call(bf16[2,2,80,256]{3,2,1,0:T(8,128)(2,1)S(1)} %slice.51.edge_ref, bf16[4,80,256]{2,1,0:T(8,128)(2,1)S(1)} %get-tuple-element.19.early_ref, bf16[2,2,80,256]{3,2,1,0:T(8,128)(2,1)S(1)} %collective-permute-done.edge_ref.old_edge_ref, ...), custom_call_target="tpu_custom_call" | custom-call | flops 629145600 | bytes 5242880 | tf_op jit(solution)/shard_map/pallas_call | solution.py:356
  20.1 0.1 collective-permute-start.7
  20.1 1.3 %collective-permute-done.7.got_ref = f32[264,128]{1,0:T(8,128)S(1)} collective-permute-done((f32[264,128]{1,0:T(8,128)S(1)}, f32[264,128]{1,0:T(8,128)S(1)}, u32[]{:S(2)}, u32[]{:S(2)}) %collective-permute-start.7) | collective-permute-done | bytes 135200 | tf_op jit(solution)/shard_map/ppermute | solution.py:56
  21.5 0.1 shard_map.73
  21.6 0.1 collective-permute-start.10
  21.7 1.6 %collective-permute-start.8 = (f16[272,128]{1,0:T(8,128)(2,1)S(1)}, f16[272,128]{1,0:T(8,128)(2,1)S(1)}, u32[]{:S(2)}, u32[]{:S(2)}) collective-permute-start(f16[272,128]{1,0:T(8,128)(2,1)S(1)} %convert_element_type.46), channel_id=1, source_target_pairs={{0,2},{1,9},{2,0},{3,11},{4,12},{5,7},{6,14},{7,5},{8,10},{9,1},{1... | collective-permute-start | bytes 208904 | tf_op jit(solution)/shard_map/ppermute | solution.py:56
  23.3 1.4 %collective-permute-start.9 = (f16[272,128]{1,0:T(8,128)(2,1)S(1)}, f16[272,128]{1,0:T(8,128)(2,1)S(1)}, u32[]{:S(2)}, u32[]{:S(2)}) collective-permute-start(f16[272,128]{1,0:T(8,128)(2,1)S(1)} %convert_element_type.46), channel_id=1, source_target_pairs={{0,5},{1,16},{2,7},{3,18},{4,21},{5,0},{6,23},{7,2},{8,13},{9,24},... | collective-permute-start | bytes 208904 | tf_op jit(solution)/shard_map/ppermute | solution.py:56
  24.6 0.8 %pad_maximum_fusion = bf16[2,480,256]{2,1,0:T(8,128)(2,1)} fusion(bf16[1,480,256]{2,1,0:T(8,128)(2,1)S(1)} %bitcast.24, bf16[1,480,256]{2,1,0:T(8,128)(2,1)S(1)} %bitcast.25), kind=kLoop, calls=%fused_computation | loop fusion | flops 245760 | bytes 983040 | tf_op jit(solution)/shard_map/stack | solution.py:364
  25.4 0.9 %collective-permute-done.10 = f16[272,128]{1,0:T(8,128)(2,1)S(1)} collective-permute-done((f16[272,128]{1,0:T(8,128)(2,1)S(1)}, f16[272,128]{1,0:T(8,128)(2,1)S(1)}, u32[]{:S(2)}, u32[]{:S(2)}) %collective-permute-start.10) | collective-permute-done | bytes 69664 | tf_op jit(solution)/shard_map/ppermute | solution.py:56
  26.3 0.0 collective-permute-done.8
  26.3 0.7 %collective-permute-done.9 = f16[272,128]{1,0:T(8,128)(2,1)S(1)} collective-permute-done((f16[272,128]{1,0:T(8,128)(2,1)S(1)}, f16[272,128]{1,0:T(8,128)(2,1)S(1)}, u32[]{:S(2)}, u32[]{:S(2)}) %collective-permute-start.9) | collective-permute-done | bytes 69664 | tf_op jit(solution)/shard_map/ppermute | solution.py:56
  27.1 0.1 select_convert_fusion
  27.2 0.9 %collective-permute-start.12 = (f16[272,128]{1,0:T(8,128)(2,1)S(1)}, f16[272,128]{1,0:T(8,128)(2,1)S(1)}, u32[]{:S(2)}, u32[]{:S(2)}) collective-permute-start(f16[272,128]{1,0:T(8,128)(2,1)S(1)} %select_convert_fusion), channel_id=1, source_target_pairs={{0,17},{1,4},{2,19},{3,6},{4,1},{5,20},{6,3},{7,22},{8,25},{9,12},... | collective-permute-start | bytes 208904 | tf_op jit(solution)/shard_map/ppermute | solution.py:56
  28.1 1.6 %collective-permute-start.11 = (f16[272,128]{1,0:T(8,128)(2,1)S(1)}, f16[272,128]{1,0:T(8,128)(2,1)S(1)}, u32[]{:S(2)}, u32[]{:S(2)}) collective-permute-start(f16[272,128]{1,0:T(8,128)(2,1)S(1)} %select_convert_fusion), channel_id=1, source_target_pairs={{0,25},{1,6},{2,27},{3,4},{4,3},{5,28},{6,1},{7,30},{8,17},{9,14},... | collective-permute-start | bytes 208904 | tf_op jit(solution)/shard_map/ppermute | solution.py:56
  29.7 0.8 %collective-permute-start.13 = (f16[272,128]{1,0:T(8,128)(2,1)S(1)}, f16[272,128]{1,0:T(8,128)(2,1)S(1)}, u32[]{:S(2)}, u32[]{:S(2)}) collective-permute-start(f16[272,128]{1,0:T(8,128)(2,1)S(1)} %select_convert_fusion), channel_id=1, source_target_pairs={{0,8},{1,3},{2,10},{3,1},{4,6},{5,13},{6,4},{7,15},{8,0},{9,11},{1... | collective-permute-start | bytes 208904 | tf_op jit(solution)/shard_map/ppermute | solution.py:56
  30.5 1.9 %collective-permute-done.12 = f16[272,128]{1,0:T(8,128)(2,1)S(1)} collective-permute-done((f16[272,128]{1,0:T(8,128)(2,1)S(1)}, f16[272,128]{1,0:T(8,128)(2,1)S(1)}, u32[]{:S(2)}, u32[]{:S(2)}) %collective-permute-start.12) | collective-permute-done | bytes 69664 | tf_op jit(solution)/shard_map/ppermute | solution.py:56
  32.4 1.4 %collective-permute-done.11 = f16[272,128]{1,0:T(8,128)(2,1)S(1)} collective-permute-done((f16[272,128]{1,0:T(8,128)(2,1)S(1)}, f16[272,128]{1,0:T(8,128)(2,1)S(1)}, u32[]{:S(2)}, u32[]{:S(2)}) %collective-permute-start.11) | collective-permute-done | bytes 69664 | tf_op jit(solution)/shard_map/ppermute | solution.py:56
  33.8 0.7 %collective-permute-done.13 = f16[272,128]{1,0:T(8,128)(2,1)S(1)} collective-permute-done((f16[272,128]{1,0:T(8,128)(2,1)S(1)}, f16[272,128]{1,0:T(8,128)(2,1)S(1)}, u32[]{:S(2)}, u32[]{:S(2)}) %collective-permute-start.13) | collective-permute-done | bytes 69664 | tf_op jit(solution)/shard_map/ppermute | solution.py:56
  34.5 0.1 add_add_fusion.mine_ref
  34.6 0.1 collective-permute-start.14
  34.7 1.3 %collective-permute-done.14.other_ref = f32[264,128]{1,0:T(8,128)S(1)} collective-permute-done((f32[264,128]{1,0:T(8,128)S(1)}, f32[264,128]{1,0:T(8,128)S(1)}, u32[]{:S(2)}, u32[]{:S(2)}) %collective-permute-start.14) | collective-permute-done | bytes 135200 | tf_op jit(solution)/shard_map/ppermute | solution.py:56
  36.0 0.8 %shard_map.74 = (f32[256,256]{1,0:T(8,128)}, f32[256,128]{1,0:T(8,128)}) custom-call(f32[264,128]{1,0:T(8,128)S(1)} %add_add_fusion.mine_ref, f32[264,128]{1,0:T(8,128)S(1)} %collective-permute-done.14.other_ref), custom_call_target="tpu_custom_call" | custom-call | tf_op jit(solution)/shard_map/pallas_call | solution.py:368
  (11 shorter events, 0.1 us)
Async XLA Ops:
  1.6 4.7 %copy-start.2 = (bf16[2,6,80,256]{3,2,1,0:T(8,128)(2,1)S(1)}, bf16[2,6,80,256]{3,2,1,0:T(8,128)(2,1)}, u32[]{:S(2)}) copy-start(bf16[2,6,80,256]{3,2,1,0:T(8,128)(2,1)} %latents_ref.1) | copy-start | bytes 1474564
  1.6 10.3 %collective-permute-start = (bf16[2,2,80,256]{3,2,1,0:T(8,128)(2,1)S(1)}, bf16[2,2,80,256]{3,2,1,0:T(8,128)(2,1)S(1)}, u32[]{:S(2)}, u32[]{:S(2)}) collective-permute-start(bf16[2,2,80,256]{3,2,1,0:T(8,128)(2,1)S(1)} %slice.51.edge_ref), channel_id=1, source_target_pairs={{0,4},{4,8},{8,12},{12,16},{16,20},{20,24},{24,28},{28,0},{1,5},{5... | collective-permute-start | bytes 491528 | tf_op jit(solution)/shard_map/ppermute | solution.py:61
  4.6 7.5 %collective-permute-start.5 = (bf16[2,80,256]{2,1,0:T(8,128)(2,1)S(1)}, bf16[2,80,256]{2,1,0:T(8,128)(2,1)S(1)}, u32[]{:S(2)}, u32[]{:S(2)}) collective-permute-start(bf16[2,80,256]{2,1,0:T(8,128)(2,1)S(1)} %get-tuple-element.23), channel_id=1, source_target_pairs={{0,1},{1,0},{2,3},{3,2},{4,5},{5,4},{6,7},{7,6},{8,9},{9,8},{10,11... | collective-permute-start | bytes 245768 | tf_op jit(solution)/shard_map/ppermute | solution.py:56
  4.7 9.9 %collective-permute-start.6 = (bf16[2,80,256]{2,1,0:T(8,128)(2,1)S(1)}, bf16[2,80,256]{2,1,0:T(8,128)(2,1)S(1)}, u32[]{:S(2)}, u32[]{:S(2)}) collective-permute-start(bf16[2,80,256]{2,1,0:T(8,128)(2,1)S(1)} %get-tuple-element.24), channel_id=1, source_target_pairs={{0,3},{1,2},{2,1},{3,0},{4,7},{5,6},{6,5},{7,4},{8,11},{9,10},{10,... | collective-permute-start | bytes 245768 | tf_op jit(solution)/shard_map/ppermute | solution.py:56
  6.3 10.2 %collective-permute-start.4 = (bf16[4,80,256]{2,1,0:T(8,128)(2,1)S(1)}, bf16[4,80,256]{2,1,0:T(8,128)(2,1)S(1)}, u32[]{:S(2)}, u32[]{:S(2)}) collective-permute-start(bf16[4,80,256]{2,1,0:T(8,128)(2,1)S(1)} %get-tuple-element.22.late_ref), channel_id=1, source_target_pairs={{0,4},{4,8},{8,12},{12,16},{16,20},{20,24},{24,28},{28,0},{1,5},{5... | collective-permute-start | bytes 491528 | tf_op jit(solution)/shard_map/ppermute | solution.py:61
  7.9 6.7 %copy-start = (bf16[3,3,768,256]{3,2,1,0:T(8,128)(2,1)S(1)}, bf16[3,3,768,256]{3,2,1,0:T(8,128)(2,1)}, u32[]{:S(2)}) copy-start(bf16[3,3,768,256]{3,2,1,0:T(8,128)(2,1)} %weight_ref.5) | copy-start | bytes 10616836
  7.9 10.9 %collective-permute-start.1 = (bf16[4,80,256]{2,1,0:T(8,128)(2,1)S(1)}, bf16[4,80,256]{2,1,0:T(8,128)(2,1)S(1)}, u32[]{:S(2)}, u32[]{:S(2)}) collective-permute-start(bf16[4,80,256]{2,1,0:T(8,128)(2,1)S(1)} %get-tuple-element.19.early_ref), channel_id=1, source_target_pairs={{0,4},{4,8},{8,12},{12,16},{16,20},{20,24},{24,28},{28,0},{1,5},{5... | collective-permute-start | bytes 491528 | tf_op jit(solution)/shard_map/ppermute | solution.py:61
  11.9 4.7 %copy-start.1 = (bf16[2,6,80,128]{3,2,1,0:T(8,128)(2,1)S(1)}, bf16[2,6,80,128]{3,2,1,0:T(8,128)(2,1)}, u32[]{:S(2)}) copy-start(bf16[2,6,80,128]{3,2,1,0:T(8,128)(2,1)} %param.7) | copy-start | bytes 737284
  11.9 4.7 %copy-start.3 = (f32[256]{0:T(256)S(1)}, f32[256]{0:T(256)}, u32[]{:S(2)}) copy-start(f32[256]{0:T(256)} %param.6) | copy-start | bytes 3076
  11.9 4.6 %collective-permute-start.2 = (bf16[2,80,256]{2,1,0:T(8,128)(2,1)S(1)}, bf16[2,80,256]{2,1,0:T(8,128)(2,1)S(1)}, u32[]{:S(2)}, u32[]{:S(2)}) collective-permute-start(bf16[2,80,256]{2,1,0:T(8,128)(2,1)S(1)} %get-tuple-element.20), channel_id=1, source_target_pairs={{0,3},{1,2},{2,1},{3,0},{4,7},{5,6},{6,5},{7,4},{8,11},{9,10},{10,... | collective-permute-start | bytes 245768 | tf_op jit(solution)/shard_map/ppermute | solution.py:56
  12.1 4.4 %collective-permute-start.3 = (bf16[2,80,256]{2,1,0:T(8,128)(2,1)S(1)}, bf16[2,80,256]{2,1,0:T(8,128)(2,1)S(1)}, u32[]{:S(2)}, u32[]{:S(2)}) collective-permute-start(bf16[2,80,256]{2,1,0:T(8,128)(2,1)S(1)} %get-tuple-element.21), channel_id=1, source_target_pairs={{0,1},{1,0},{2,3},{3,2},{4,5},{5,4},{6,7},{7,6},{8,9},{9,8},{10,11... | collective-permute-start | bytes 245768 | tf_op jit(solution)/shard_map/ppermute | solution.py:56
  20.1 1.4 %collective-permute-start.7 = (f32[264,128]{1,0:T(8,128)S(1)}, f32[264,128]{1,0:T(8,128)S(1)}, u32[]{:S(2)}, u32[]{:S(2)}) collective-permute-start(f32[264,128]{1,0:T(8,128)S(1)} %get-tuple-element.28), channel_id=1, source_target_pairs={{0,1},{1,0},{2,3},{3,2},{4,5},{5,4},{6,7},{7,6},{8,9},{9,8},{10,11... | collective-permute-start | bytes 405512 | tf_op jit(solution)/shard_map/ppermute | solution.py:56
  21.6 4.7 %collective-permute-start.10 = (f16[272,128]{1,0:T(8,128)(2,1)S(1)}, f16[272,128]{1,0:T(8,128)(2,1)S(1)}, u32[]{:S(2)}, u32[]{:S(2)}) collective-permute-start(f16[272,128]{1,0:T(8,128)(2,1)S(1)} %convert_element_type.46), channel_id=1, source_target_pairs={{0,7},{1,24},{2,5},{3,26},{4,29},{5,2},{6,31},{7,0},{8,15},{9,16},... | collective-permute-start | bytes 208904 | tf_op jit(solution)/shard_map/ppermute | solution.py:56
  21.7 4.6 %collective-permute-start.8 = (f16[272,128]{1,0:T(8,128)(2,1)S(1)}, f16[272,128]{1,0:T(8,128)(2,1)S(1)}, u32[]{:S(2)}, u32[]{:S(2)}) collective-permute-start(f16[272,128]{1,0:T(8,128)(2,1)S(1)} %convert_element_type.46), channel_id=1, source_target_pairs={{0,2},{1,9},{2,0},{3,11},{4,12},{5,7},{6,14},{7,5},{8,10},{9,1},{1... | collective-permute-start | bytes 208904 | tf_op jit(solution)/shard_map/ppermute | solution.py:56
  23.3 3.8 %collective-permute-start.9 = (f16[272,128]{1,0:T(8,128)(2,1)S(1)}, f16[272,128]{1,0:T(8,128)(2,1)S(1)}, u32[]{:S(2)}, u32[]{:S(2)}) collective-permute-start(f16[272,128]{1,0:T(8,128)(2,1)S(1)} %convert_element_type.46), channel_id=1, source_target_pairs={{0,5},{1,16},{2,7},{3,18},{4,21},{5,0},{6,23},{7,2},{8,13},{9,24},... | collective-permute-start | bytes 208904 | tf_op jit(solution)/shard_map/ppermute | solution.py:56
  27.2 5.2 %collective-permute-start.12 = (f16[272,128]{1,0:T(8,128)(2,1)S(1)}, f16[272,128]{1,0:T(8,128)(2,1)S(1)}, u32[]{:S(2)}, u32[]{:S(2)}) collective-permute-start(f16[272,128]{1,0:T(8,128)(2,1)S(1)} %select_convert_fusion), channel_id=1, source_target_pairs={{0,17},{1,4},{2,19},{3,6},{4,1},{5,20},{6,3},{7,22},{8,25},{9,12},... | collective-permute-start | bytes 208904 | tf_op jit(solution)/shard_map/ppermute | solution.py:56
  28.1 5.7 %collective-permute-start.11 = (f16[272,128]{1,0:T(8,128)(2,1)S(1)}, f16[272,128]{1,0:T(8,128)(2,1)S(1)}, u32[]{:S(2)}, u32[]{:S(2)}) collective-permute-start(f16[272,128]{1,0:T(8,128)(2,1)S(1)} %select_convert_fusion), channel_id=1, source_target_pairs={{0,25},{1,6},{2,27},{3,4},{4,3},{5,28},{6,1},{7,30},{8,17},{9,14},... | collective-permute-start | bytes 208904 | tf_op jit(solution)/shard_map/ppermute | solution.py:56
  29.7 4.8 %collective-permute-start.13 = (f16[272,128]{1,0:T(8,128)(2,1)S(1)}, f16[272,128]{1,0:T(8,128)(2,1)S(1)}, u32[]{:S(2)}, u32[]{:S(2)}) collective-permute-start(f16[272,128]{1,0:T(8,128)(2,1)S(1)} %select_convert_fusion), channel_id=1, source_target_pairs={{0,8},{1,3},{2,10},{3,1},{4,6},{5,13},{6,4},{7,15},{8,0},{9,11},{1... | collective-permute-start | bytes 208904 | tf_op jit(solution)/shard_map/ppermute | solution.py:56
  34.6 1.4 %collective-permute-start.14 = (f32[264,128]{1,0:T(8,128)S(1)}, f32[264,128]{1,0:T(8,128)S(1)}, u32[]{:S(2)}, u32[]{:S(2)}) collective-permute-start(f32[264,128]{1,0:T(8,128)S(1)} %add_add_fusion.mine_ref), channel_id=1, source_target_pairs={{0,1},{1,0},{2,3},{3,2},{4,5},{5,4},{6,7},{7,6},{8,9},{9,8},{10,11... | collective-permute-start | bytes 405512 | tf_op jit(solution)/shard_map/ppermute | solution.py:56

commit v10 on v9

--- a/solution.py
+++ b/solution.py
@@ -140,7 +140,7 @@
     return jnp.concatenate([above, *frame_rows(edge_ref, middle_ref, f), below], axis=0)
 
 
-def own_kernel(edge_ref, early_ref, late_ref, mate_ref, cross_ref, weight_ref, part_ref):
+def own_kernel(edge_ref, early_ref, late_ref, cross_ref, mate_ref, weight_ref, part_ref):
     cols, chans = edge_ref.shape[2:]
     span = part_ref.shape[0] // 2
     early = stacked_rows(padded_frame(edge_ref, early_ref, mate_ref, cross_ref, 0), 0, span, cols)
@@ -337,7 +337,7 @@
         out_specs=WHOLE,
         compiler_params=params(24),
         cost_estimate=pl.CostEstimate(flops=spots * chans * chans * 27, bytes_accessed=5 * 2**20, transcendentals=0),
-    )(edge, early, late, mate, cross, conv_weight)
+    )(edge, early, late, cross, mate, conv_weight)
     gain, targets = norm_gain.reshape(1, chans), depth_target.reshape(spots, bins)
     half_features = jax.ShapeDtypeStruct((spots // 2, chans), BF16)
     late_features, more, sums = pl.pallas_call(

time: 37 us -> 37 us (level)
  no operation moved by 1% of the time
where the time goes in v10:
time: 37 us; the launch traced here: 36.8 us
  starting transfers between devices  16.8 us (45%)
  waiting for transfers between devices  11.5 us (31%)
  Pallas kernels  5.73 us (15%)
  other arithmetic  1.06 us (3%)
  local copies, waits for them, and re-layouts  0.96 us (3%)
  between operations  0.82 us (2%)
    ppermute x12, starting transfers between devices, by_device(): lax.ppermute(value, ('tm', 'row'), [(a * rows + b, c * rows + d) for (a,...  10.7 us
    ppermute x12, waiting for transfers between devices, by_device(): lax.ppermute(value, ('tm', 'row'), [(a * rows + b, c * rows + d) for (a,...  8.29 us
    ppermute x3, starting transfers between devices, later(): lax.ppermute(value, 'tm', [(i, (i + 1) % count) for i in range(count)])  6.11 us
    ppermute x3, waiting for transfers between devices, later(): lax.ppermute(value, 'tm', [(i, (i + 1) % count) for i in range(count)])  3.22 us
    pallas_call x1, Pallas kernels, on_device(): pl.pallas_call(own_kernel, out_shape=jax.ShapeDtypeStruct((spots, chans),...  1.96 us
    pallas_call x1, Pallas kernels, on_device(): pl.pallas_call(late_kernel, out_shape=(half_features, jax.ShapeDtypeStruc...  1.56 us
    pallas_call x1, Pallas kernels, on_device(): pl.pallas_call(early_kernel, out_shape=(half_features, share, share), in_...  1.19 us
    slice x1, local copies, waits for them, and re-layouts, on_device(): edge = latents[:, ::rows - 1]  0.93 us
  transfers between devices with their start and end apart: 15, of which 9 were waited for; matrix products, arithmetic and copies ran while one was open for 2% of the time, Pallas kernels for 10%

profile of v10, /device:TPU:0, one launch (start us, length us, event | category | flops | bytes accessed | tf_op | source)
XLA Modules:
  0.0 36.8 jit_solution(397053489083370948)
XLA Ops:
  0.6 0.9 %slice.51.edge_ref = bf16[2,2,80,256]{3,2,1,0:T(8,128)(2,1)S(1)} slice(bf16[2,6,80,256]{3,2,1,0:T(8,128)(2,1)} %latents_ref.1), slice={[0:2:1], [0:6:5], [0:80:1], [0:256:1]} | slice | bytes 327680 | tf_op jit(solution)/shard_map/slice | solution.py:320
  1.6 0.0 copy-start.2
  1.6 3.0 %collective-permute-start = (bf16[2,2,80,256]{3,2,1,0:T(8,128)(2,1)S(1)}, bf16[2,2,80,256]{3,2,1,0:T(8,128)(2,1)S(1)}, u32[]{:S(2)}, u32[]{:S(2)}) collective-permute-start(bf16[2,2,80,256]{3,2,1,0:T(8,128)(2,1)S(1)} %slice.51.edge_ref), channel_id=1, source_target_pairs={{0,4},{4,8},{8,12},{12,16},{16,20},{20,24},{24,28},{28,0},{1,5},{5... | collective-permute-start | bytes 491528 | tf_op jit(solution)/shard_map/ppermute | solution.py:61
  4.6 0.7 %collective-permute-start.5 = (bf16[2,80,256]{2,1,0:T(8,128)(2,1)S(1)}, bf16[2,80,256]{2,1,0:T(8,128)(2,1)S(1)}, u32[]{:S(2)}, u32[]{:S(2)}) collective-permute-start(bf16[2,80,256]{2,1,0:T(8,128)(2,1)S(1)} %get-tuple-element.23), channel_id=1, source_target_pairs={{0,3},{1,2},{2,1},{3,0},{4,7},{5,6},{6,5},{7,4},{8,11},{9,10},{10,... | collective-permute-start | bytes 245768 | tf_op jit(solution)/shard_map/ppermute | solution.py:56
  5.3 1.0 %collective-permute-start.6 = (bf16[2,80,256]{2,1,0:T(8,128)(2,1)S(1)}, bf16[2,80,256]{2,1,0:T(8,128)(2,1)S(1)}, u32[]{:S(2)}, u32[]{:S(2)}) collective-permute-start(bf16[2,80,256]{2,1,0:T(8,128)(2,1)S(1)} %get-tuple-element.24), channel_id=1, source_target_pairs={{0,1},{1,0},{2,3},{3,2},{4,5},{5,4},{6,7},{7,6},{8,9},{9,8},{10,11... | collective-permute-start | bytes 245768 | tf_op jit(solution)/shard_map/ppermute | solution.py:56
  6.3 0.0 copy-done.2
  6.3 1.6 %collective-permute-start.4 = (bf16[4,80,256]{2,1,0:T(8,128)(2,1)S(1)}, bf16[4,80,256]{2,1,0:T(8,128)(2,1)S(1)}, u32[]{:S(2)}, u32[]{:S(2)}) collective-permute-start(bf16[4,80,256]{2,1,0:T(8,128)(2,1)S(1)} %get-tuple-element.22.late_ref), channel_id=1, source_target_pairs={{0,4},{4,8},{8,12},{12,16},{16,20},{20,24},{24,28},{28,0},{1,5},{5... | collective-permute-start | bytes 491528 | tf_op jit(solution)/shard_map/ppermute | solution.py:61
  7.9 0.0 copy-start
  7.9 1.5 %collective-permute-start.1 = (bf16[4,80,256]{2,1,0:T(8,128)(2,1)S(1)}, bf16[4,80,256]{2,1,0:T(8,128)(2,1)S(1)}, u32[]{:S(2)}, u32[]{:S(2)}) collective-permute-start(bf16[4,80,256]{2,1,0:T(8,128)(2,1)S(1)} %get-tuple-element.19.early_ref), channel_id=1, source_target_pairs={{0,4},{4,8},{8,12},{12,16},{16,20},{20,24},{24,28},{28,0},{1,5},{5... | collective-permute-start | bytes 491528 | tf_op jit(solution)/shard_map/ppermute | solution.py:61
  9.4 2.5 %collective-permute-done.edge_ref.old_edge_ref = bf16[2,2,80,256]{3,2,1,0:T(8,128)(2,1)S(1)} collective-permute-done((bf16[2,2,80,256]{3,2,1,0:T(8,128)(2,1)S(1)}, bf16[2,2,80,256]{3,2,1,0:T(8,128)(2,1)S(1)}, u32[]{:S(2)}, u32[]{:S(2)}) %collective-permute-start) | collective-permute-done | bytes 163872 | tf_op jit(solution)/shard_map/ppermute | solution.py:61
  12.0 0.0 copy-start.1
  12.0 0.0 copy-start.3
  12.0 0.2 collective-permute-start.2
  12.1 0.0 collective-permute-done.5.cross_ref
  12.1 2.4 %collective-permute-start.3 = (bf16[2,80,256]{2,1,0:T(8,128)(2,1)S(1)}, bf16[2,80,256]{2,1,0:T(8,128)(2,1)S(1)}, u32[]{:S(2)}, u32[]{:S(2)}) collective-permute-start(bf16[2,80,256]{2,1,0:T(8,128)(2,1)S(1)} %get-tuple-element.21), channel_id=1, source_target_pairs={{0,1},{1,0},{2,3},{3,2},{4,5},{5,4},{6,7},{7,6},{8,9},{9,8},{10,11... | collective-permute-start | bytes 245768 | tf_op jit(solution)/shard_map/ppermute | solution.py:56
  14.6 0.0 collective-permute-done.6.mate_ref
  14.6 0.0 copy-done
  14.6 2.0 %shard_map.70.part_ref = f32[960,256]{1,0:T(8,128)S(1)} custom-call(bf16[2,2,80,256]{3,2,1,0:T(8,128)(2,1)S(1)} %slice.51.edge_ref, bf16[4,80,256]{2,1,0:T(8,128)(2,1)S(1)} %get-tuple-element.19.early_ref, bf16[4,80,256]{2,1,0:T(8,128)(2,1)S(1)} %get-tuple-element.22.late_ref, bf16[2,80,256]{2,1,0:T(8,128)(2,1)S(1)} %collective-permute-done.5.cross_ref, ...), custom_call_target="tpu_custom_call" | custom-call | flops 1698693120 | bytes 5242880 | tf_op jit(solution)/shard_map/pallas_call | solution.py:333
  16.5 0.0 collective-permute-done.4.old_late_ref
  16.6 0.0 collective-permute-done.2.cross_ref
  16.6 0.0 collective-permute-done.3.mate_ref
  16.6 0.0 copy-done.1
  16.6 0.0 copy-done.3
  16.6 1.6 %shard_map.71 = (bf16[480,256]{1,0:T(8,128)(2,1)S(1)}, f32[480,256]{1,0:T(8,128)S(1)}, f32[256,384]{1,0:T(8,128)S(1)}) custom-call(bf16[2,2,80,256]{3,2,1,0:T(8,128)(2,1)S(1)} %slice.51.edge_ref, bf16[4,80,256]{2,1,0:T(8,128)(2,1)S(1)} %get-tuple-element.22.late_ref, bf16[2,2,80,256]{3,2,1,0:T(8,128)(2,1)S(1)} %collective-permute-done.edge_ref.old_edge_ref, ...), custom_call_target="tpu_custom_call" | custom-call | flops 1258291200 | bytes 5242880 | tf_op jit(solution)/shard_map/pallas_call | solution.py:343
  18.2 0.7 %collective-permute-done.1.old_early_ref = bf16[4,80,256]{2,1,0:T(8,128)(2,1)S(1)} collective-permute-done((bf16[4,80,256]{2,1,0:T(8,128)(2,1)S(1)}, bf16[4,80,256]{2,1,0:T(8,128)(2,1)S(1)}, u32[]{:S(2)}, u32[]{:S(2)}) %collective-permute-start.1) | collective-permute-done | bytes 163872 | tf_op jit(solution)/shard_map/ppermute | solution.py:61
  18.9 1.2 %shard_map.72 = (bf16[480,256]{1,0:T(8,128)(2,1)S(1)}, f32[264,128]{1,0:T(8,128)S(1)}, f32[264,128]{1,0:T(8,128)S(1)}) custom-call(bf16[2,2,80,256]{3,2,1,0:T(8,128)(2,1)S(1)} %slice.51.edge_ref, bf16[4,80,256]{2,1,0:T(8,128)(2,1)S(1)} %get-tuple-element.19.early_ref, bf16[2,2,80,256]{3,2,1,0:T(8,128)(2,1)S(1)} %collective-permute-done.edge_ref.old_edge_ref, ...), custom_call_target="tpu_custom_call" | custom-call | flops 629145600 | bytes 5242880 | tf_op jit(solution)/shard_map/pallas_call | solution.py:356
  20.1 0.1 collective-permute-start.7
  20.1 1.3 %collective-permute-done.7.got_ref = f32[264,128]{1,0:T(8,128)S(1)} collective-permute-done((f32[264,128]{1,0:T(8,128)S(1)}, f32[264,128]{1,0:T(8,128)S(1)}, u32[]{:S(2)}, u32[]{:S(2)}) %collective-permute-start.7) | collective-permute-done | bytes 135200 | tf_op jit(solution)/shard_map/ppermute | solution.py:56
  21.5 0.1 shard_map.73
  21.6 0.1 collective-permute-start.10
  21.7 1.6 %collective-permute-start.8 = (f16[272,128]{1,0:T(8,128)(2,1)S(1)}, f16[272,128]{1,0:T(8,128)(2,1)S(1)}, u32[]{:S(2)}, u32[]{:S(2)}) collective-permute-start(f16[272,128]{1,0:T(8,128)(2,1)S(1)} %convert_element_type.46), channel_id=1, source_target_pairs={{0,2},{1,9},{2,0},{3,11},{4,12},{5,7},{6,14},{7,5},{8,10},{9,1},{1... | collective-permute-start | bytes 208904 | tf_op jit(solution)/shard_map/ppermute | solution.py:56
  23.3 1.4 %collective-permute-start.9 = (f16[272,128]{1,0:T(8,128)(2,1)S(1)}, f16[272,128]{1,0:T(8,128)(2,1)S(1)}, u32[]{:S(2)}, u32[]{:S(2)}) collective-permute-start(f16[272,128]{1,0:T(8,128)(2,1)S(1)} %convert_element_type.46), channel_id=1, source_target_pairs={{0,5},{1,16},{2,7},{3,18},{4,21},{5,0},{6,23},{7,2},{8,13},{9,24},... | collective-permute-start | bytes 208904 | tf_op jit(solution)/shard_map/ppermute | solution.py:56
  24.6 0.8 %pad_maximum_fusion = bf16[2,480,256]{2,1,0:T(8,128)(2,1)} fusion(bf16[1,480,256]{2,1,0:T(8,128)(2,1)S(1)} %bitcast.24, bf16[1,480,256]{2,1,0:T(8,128)(2,1)S(1)} %bitcast.25), kind=kLoop, calls=%fused_computation | loop fusion | flops 245760 | bytes 983040 | tf_op jit(solution)/shard_map/stack | solution.py:364
  25.4 0.9 %collective-permute-done.10 = f16[272,128]{1,0:T(8,128)(2,1)S(1)} collective-permute-done((f16[272,128]{1,0:T(8,128)(2,1)S(1)}, f16[272,128]{1,0:T(8,128)(2,1)S(1)}, u32[]{:S(2)}, u32[]{:S(2)}) %collective-permute-start.10) | collective-permute-done | bytes 69664 | tf_op jit(solution)/shard_map/ppermute | solution.py:56
  26.3 0.0 collective-permute-done.8
  26.3 0.7 %collective-permute-done.9 = f16[272,128]{1,0:T(8,128)(2,1)S(1)} collective-permute-done((f16[272,128]{1,0:T(8,128)(2,1)S(1)}, f16[272,128]{1,0:T(8,128)(2,1)S(1)}, u32[]{:S(2)}, u32[]{:S(2)}) %collective-permute-start.9) | collective-permute-done | bytes 69664 | tf_op jit(solution)/shard_map/ppermute | solution.py:56
  27.1 0.1 select_convert_fusion
  27.2 0.9 %collective-permute-start.12 = (f16[272,128]{1,0:T(8,128)(2,1)S(1)}, f16[272,128]{1,0:T(8,128)(2,1)S(1)}, u32[]{:S(2)}, u32[]{:S(2)}) collective-permute-start(f16[272,128]{1,0:T(8,128)(2,1)S(1)} %select_convert_fusion), channel_id=1, source_target_pairs={{0,17},{1,4},{2,19},{3,6},{4,1},{5,20},{6,3},{7,22},{8,25},{9,12},... | collective-permute-start | bytes 208904 | tf_op jit(solution)/shard_map/ppermute | solution.py:56
  28.1 1.6 %collective-permute-start.11 = (f16[272,128]{1,0:T(8,128)(2,1)S(1)}, f16[272,128]{1,0:T(8,128)(2,1)S(1)}, u32[]{:S(2)}, u32[]{:S(2)}) collective-permute-start(f16[272,128]{1,0:T(8,128)(2,1)S(1)} %select_convert_fusion), channel_id=1, source_target_pairs={{0,25},{1,6},{2,27},{3,4},{4,3},{5,28},{6,1},{7,30},{8,17},{9,14},... | collective-permute-start | bytes 208904 | tf_op jit(solution)/shard_map/ppermute | solution.py:56
  29.7 0.8 %collective-permute-start.13 = (f16[272,128]{1,0:T(8,128)(2,1)S(1)}, f16[272,128]{1,0:T(8,128)(2,1)S(1)}, u32[]{:S(2)}, u32[]{:S(2)}) collective-permute-start(f16[272,128]{1,0:T(8,128)(2,1)S(1)} %select_convert_fusion), channel_id=1, source_target_pairs={{0,8},{1,3},{2,10},{3,1},{4,6},{5,13},{6,4},{7,15},{8,0},{9,11},{1... | collective-permute-start | bytes 208904 | tf_op jit(solution)/shard_map/ppermute | solution.py:56
  30.5 1.9 %collective-permute-done.12 = f16[272,128]{1,0:T(8,128)(2,1)S(1)} collective-permute-done((f16[272,128]{1,0:T(8,128)(2,1)S(1)}, f16[272,128]{1,0:T(8,128)(2,1)S(1)}, u32[]{:S(2)}, u32[]{:S(2)}) %collective-permute-start.12) | collective-permute-done | bytes 69664 | tf_op jit(solution)/shard_map/ppermute | solution.py:56
  32.4 1.4 %collective-permute-done.11 = f16[272,128]{1,0:T(8,128)(2,1)S(1)} collective-permute-done((f16[272,128]{1,0:T(8,128)(2,1)S(1)}, f16[272,128]{1,0:T(8,128)(2,1)S(1)}, u32[]{:S(2)}, u32[]{:S(2)}) %collective-permute-start.11) | collective-permute-done | bytes 69664 | tf_op jit(solution)/shard_map/ppermute | solution.py:56
  33.8 0.7 %collective-permute-done.13 = f16[272,128]{1,0:T(8,128)(2,1)S(1)} collective-permute-done((f16[272,128]{1,0:T(8,128)(2,1)S(1)}, f16[272,128]{1,0:T(8,128)(2,1)S(1)}, u32[]{:S(2)}, u32[]{:S(2)}) %collective-permute-start.13) | collective-permute-done | bytes 69664 | tf_op jit(solution)/shard_map/ppermute | solution.py:56
  34.5 0.1 add_add_fusion.mine_ref
  34.6 0.1 collective-permute-start.14
  34.7 1.3 %collective-permute-done.14.other_ref = f32[264,128]{1,0:T(8,128)S(1)} collective-permute-done((f32[264,128]{1,0:T(8,128)S(1)}, f32[264,128]{1,0:T(8,128)S(1)}, u32[]{:S(2)}, u32[]{:S(2)}) %collective-permute-start.14) | collective-permute-done | bytes 135200 | tf_op jit(solution)/shard_map/ppermute | solution.py:56
  36.0 0.8 %shard_map.74 = (f32[256,256]{1,0:T(8,128)}, f32[256,128]{1,0:T(8,128)}) custom-call(f32[264,128]{1,0:T(8,128)S(1)} %add_add_fusion.mine_ref, f32[264,128]{1,0:T(8,128)S(1)} %collective-permute-done.14.other_ref), custom_call_target="tpu_custom_call" | custom-call | tf_op jit(solution)/shard_map/pallas_call | solution.py:368
  (11 shorter events, 0.1 us)
Async XLA Ops:
  1.6 4.7 %copy-start.2 = (bf16[2,6,80,256]{3,2,1,0:T(8,128)(2,1)S(1)}, bf16[2,6,80,256]{3,2,1,0:T(8,128)(2,1)}, u32[]{:S(2)}) copy-start(bf16[2,6,80,256]{3,2,1,0:T(8,128)(2,1)} %latents_ref.1) | copy-start | bytes 1474564
  1.6 10.4 %collective-permute-start = (bf16[2,2,80,256]{3,2,1,0:T(8,128)(2,1)S(1)}, bf16[2,2,80,256]{3,2,1,0:T(8,128)(2,1)S(1)}, u32[]{:S(2)}, u32[]{:S(2)}) collective-permute-start(bf16[2,2,80,256]{3,2,1,0:T(8,128)(2,1)S(1)} %slice.51.edge_ref), channel_id=1, source_target_pairs={{0,4},{4,8},{8,12},{12,16},{16,20},{20,24},{24,28},{28,0},{1,5},{5... | collective-permute-start | bytes 491528 | tf_op jit(solution)/shard_map/ppermute | solution.py:61
  4.6 7.5 %collective-permute-start.5 = (bf16[2,80,256]{2,1,0:T(8,128)(2,1)S(1)}, bf16[2,80,256]{2,1,0:T(8,128)(2,1)S(1)}, u32[]{:S(2)}, u32[]{:S(2)}) collective-permute-start(bf16[2,80,256]{2,1,0:T(8,128)(2,1)S(1)} %get-tuple-element.23), channel_id=1, source_target_pairs={{0,3},{1,2},{2,1},{3,0},{4,7},{5,6},{6,5},{7,4},{8,11},{9,10},{10,... | collective-permute-start | bytes 245768 | tf_op jit(solution)/shard_map/ppermute | solution.py:56
  5.3 9.2 %collective-permute-start.6 = (bf16[2,80,256]{2,1,0:T(8,128)(2,1)S(1)}, bf16[2,80,256]{2,1,0:T(8,128)(2,1)S(1)}, u32[]{:S(2)}, u32[]{:S(2)}) collective-permute-start(bf16[2,80,256]{2,1,0:T(8,128)(2,1)S(1)} %get-tuple-element.24), channel_id=1, source_target_pairs={{0,1},{1,0},{2,3},{3,2},{4,5},{5,4},{6,7},{7,6},{8,9},{9,8},{10,11... | collective-permute-start | bytes 245768 | tf_op jit(solution)/shard_map/ppermute | solution.py:56
  6.3 10.2 %collective-permute-start.4 = (bf16[4,80,256]{2,1,0:T(8,128)(2,1)S(1)}, bf16[4,80,256]{2,1,0:T(8,128)(2,1)S(1)}, u32[]{:S(2)}, u32[]{:S(2)}) collective-permute-start(bf16[4,80,256]{2,1,0:T(8,128)(2,1)S(1)} %get-tuple-element.22.late_ref), channel_id=1, source_target_pairs={{0,4},{4,8},{8,12},{12,16},{16,20},{20,24},{24,28},{28,0},{1,5},{5... | collective-permute-start | bytes 491528 | tf_op jit(solution)/shard_map/ppermute | solution.py:61
  7.9 6.7 %copy-start = (bf16[3,3,768,256]{3,2,1,0:T(8,128)(2,1)S(1)}, bf16[3,3,768,256]{3,2,1,0:T(8,128)(2,1)}, u32[]{:S(2)}) copy-start(bf16[3,3,768,256]{3,2,1,0:T(8,128)(2,1)} %weight_ref.5) | copy-start | bytes 10616836
  7.9 11.0 %collective-permute-start.1 = (bf16[4,80,256]{2,1,0:T(8,128)(2,1)S(1)}, bf16[4,80,256]{2,1,0:T(8,128)(2,1)S(1)}, u32[]{:S(2)}, u32[]{:S(2)}) collective-permute-start(bf16[4,80,256]{2,1,0:T(8,128)(2,1)S(1)} %get-tuple-element.19.early_ref), channel_id=1, source_target_pairs={{0,4},{4,8},{8,12},{12,16},{16,20},{20,24},{24,28},{28,0},{1,5},{5... | collective-permute-start | bytes 491528 | tf_op jit(solution)/shard_map/ppermute | solution.py:61
  12.0 4.6 %copy-start.1 = (bf16[2,6,80,128]{3,2,1,0:T(8,128)(2,1)S(1)}, bf16[2,6,80,128]{3,2,1,0:T(8,128)(2,1)}, u32[]{:S(2)}) copy-start(bf16[2,6,80,128]{3,2,1,0:T(8,128)(2,1)} %param.7) | copy-start | bytes 737284
  12.0 4.6 %copy-start.3 = (f32[256]{0:T(256)S(1)}, f32[256]{0:T(256)}, u32[]{:S(2)}) copy-start(f32[256]{0:T(256)} %param.6) | copy-start | bytes 3076
  12.0 4.6 %collective-permute-start.2 = (bf16[2,80,256]{2,1,0:T(8,128)(2,1)S(1)}, bf16[2,80,256]{2,1,0:T(8,128)(2,1)S(1)}, u32[]{:S(2)}, u32[]{:S(2)}) collective-permute-start(bf16[2,80,256]{2,1,0:T(8,128)(2,1)S(1)} %get-tuple-element.20), channel_id=1, source_target_pairs={{0,3},{1,2},{2,1},{3,0},{4,7},{5,6},{6,5},{7,4},{8,11},{9,10},{10,... | collective-permute-start | bytes 245768 | tf_op jit(solution)/shard_map/ppermute | solution.py:56
  12.1 4.4 %collective-permute-start.3 = (bf16[2,80,256]{2,1,0:T(8,128)(2,1)S(1)}, bf16[2,80,256]{2,1,0:T(8,128)(2,1)S(1)}, u32[]{:S(2)}, u32[]{:S(2)}) collective-permute-start(bf16[2,80,256]{2,1,0:T(8,128)(2,1)S(1)} %get-tuple-element.21), channel_id=1, source_target_pairs={{0,1},{1,0},{2,3},{3,2},{4,5},{5,4},{6,7},{7,6},{8,9},{9,8},{10,11... | collective-permute-start | bytes 245768 | tf_op jit(solution)/shard_map/ppermute | solution.py:56
  20.1 1.4 %collective-permute-start.7 = (f32[264,128]{1,0:T(8,128)S(1)}, f32[264,128]{1,0:T(8,128)S(1)}, u32[]{:S(2)}, u32[]{:S(2)}) collective-permute-start(f32[264,128]{1,0:T(8,128)S(1)} %get-tuple-element.28), channel_id=1, source_target_pairs={{0,1},{1,0},{2,3},{3,2},{4,5},{5,4},{6,7},{7,6},{8,9},{9,8},{10,11... | collective-permute-start | bytes 405512 | tf_op jit(solution)/shard_map/ppermute | solution.py:56
  21.6 4.7 %collective-permute-start.10 = (f16[272,128]{1,0:T(8,128)(2,1)S(1)}, f16[272,128]{1,0:T(8,128)(2,1)S(1)}, u32[]{:S(2)}, u32[]{:S(2)}) collective-permute-start(f16[272,128]{1,0:T(8,128)(2,1)S(1)} %convert_element_type.46), channel_id=1, source_target_pairs={{0,7},{1,24},{2,5},{3,26},{4,29},{5,2},{6,31},{7,0},{8,15},{9,16},... | collective-permute-start | bytes 208904 | tf_op jit(solution)/shard_map/ppermute | solution.py:56
  21.7 4.6 %collective-permute-start.8 = (f16[272,128]{1,0:T(8,128)(2,1)S(1)}, f16[272,128]{1,0:T(8,128)(2,1)S(1)}, u32[]{:S(2)}, u32[]{:S(2)}) collective-permute-start(f16[272,128]{1,0:T(8,128)(2,1)S(1)} %convert_element_type.46), channel_id=1, source_target_pairs={{0,2},{1,9},{2,0},{3,11},{4,12},{5,7},{6,14},{7,5},{8,10},{9,1},{1... | collective-permute-start | bytes 208904 | tf_op jit(solution)/shard_map/ppermute | solution.py:56
  23.3 3.8 %collective-permute-start.9 = (f16[272,128]{1,0:T(8,128)(2,1)S(1)}, f16[272,128]{1,0:T(8,128)(2,1)S(1)}, u32[]{:S(2)}, u32[]{:S(2)}) collective-permute-start(f16[272,128]{1,0:T(8,128)(2,1)S(1)} %convert_element_type.46), channel_id=1, source_target_pairs={{0,5},{1,16},{2,7},{3,18},{4,21},{5,0},{6,23},{7,2},{8,13},{9,24},... | collective-permute-start | bytes 208904 | tf_op jit(solution)/shard_map/ppermute | solution.py:56
  27.2 5.2 %collective-permute-start.12 = (f16[272,128]{1,0:T(8,128)(2,1)S(1)}, f16[272,128]{1,0:T(8,128)(2,1)S(1)}, u32[]{:S(2)}, u32[]{:S(2)}) collective-permute-start(f16[272,128]{1,0:T(8,128)(2,1)S(1)} %select_convert_fusion), channel_id=1, source_target_pairs={{0,17},{1,4},{2,19},{3,6},{4,1},{5,20},{6,3},{7,22},{8,25},{9,12},... | collective-permute-start | bytes 208904 | tf_op jit(solution)/shard_map/ppermute | solution.py:56
  28.1 5.7 %collective-permute-start.11 = (f16[272,128]{1,0:T(8,128)(2,1)S(1)}, f16[272,128]{1,0:T(8,128)(2,1)S(1)}, u32[]{:S(2)}, u32[]{:S(2)}) collective-permute-start(f16[272,128]{1,0:T(8,128)(2,1)S(1)} %select_convert_fusion), channel_id=1, source_target_pairs={{0,25},{1,6},{2,27},{3,4},{4,3},{5,28},{6,1},{7,30},{8,17},{9,14},... | collective-permute-start | bytes 208904 | tf_op jit(solution)/shard_map/ppermute | solution.py:56
  29.7 4.8 %collective-permute-start.13 = (f16[272,128]{1,0:T(8,128)(2,1)S(1)}, f16[272,128]{1,0:T(8,128)(2,1)S(1)}, u32[]{:S(2)}, u32[]{:S(2)}) collective-permute-start(f16[272,128]{1,0:T(8,128)(2,1)S(1)} %select_convert_fusion), channel_id=1, source_target_pairs={{0,8},{1,3},{2,10},{3,1},{4,6},{5,13},{6,4},{7,15},{8,0},{9,11},{1... | collective-permute-start | bytes 208904 | tf_op jit(solution)/shard_map/ppermute | solution.py:56
  34.6 1.4 %collective-permute-start.14 = (f32[264,128]{1,0:T(8,128)S(1)}, f32[264,128]{1,0:T(8,128)S(1)}, u32[]{:S(2)}, u32[]{:S(2)}) collective-permute-start(f32[264,128]{1,0:T(8,128)S(1)} %add_add_fusion.mine_ref), channel_id=1, source_target_pairs={{0,1},{1,0},{2,3},{3,2},{4,5},{5,4},{6,7},{7,6},{8,9},{9,8},{10,11... | collective-permute-start | bytes 405512 | tf_op jit(solution)/shard_map/ppermute | solution.py:56
